TPU v7x, 32 devices: a whole 2x2x4 slice. The times are simulated.
32 devices in a mesh: groups: 2 (over y), shot: 4 (over z), dom: 2 (over x), pair: 2 (over core).
Axes of the slice: x: 2, y: 2, z: 4, core: 2. Of those that a mesh axis runs over, the one named last changes fastest.
Arguments:
- velocity: float32 [128, 8, 8, 128], P(('groups', 'shot', 'dom')), parts along dimension 0, may hold values from 0.12 to 0.36
- density: float32 [128, 8, 8, 128], P(('groups', 'shot', 'dom')), parts along dimension 0, may hold values from 1 to 2
- owner_map: int32 [128], P('groups'), parts along dimension 0, may hold values from 0 to 63, as said below
- footprint: int32 [8, 32], P(('groups', 'shot'), 'dom'), parts along dimension 0, may hold values from 0 to 63, as said below
- aperture: int32 [8], P(('groups', 'shot')), parts along dimension 0, may hold values from 4 to 8, as said below
- source_cell: int32 [8], P(('groups', 'shot')), parts along dimension 0, may hold values from 0 to 131071
- receiver_cells: int32 [8, 512], P(('groups', 'shot')), parts along dimension 0, may hold values from 0 to 131071
- wavelet: float32 [8, 16], P(('groups', 'shot')), parts along dimension 0, may hold values from -6 to 6
- traces: float32 [8, 16, 512], P(('groups', 'shot')), parts along dimension 0, may hold values from -6 to 6
- states: float32 [8, 2, 2, 64, 32, 128], P(('groups', 'shot'), 'pair', None, 'dom'), parts along dimension 0, may hold values from -6 to 6
- stored_rims: float32 [8, 16, 2, 64, 128], P(('groups', 'shot'), None, None, 'dom'), parts along dimension 0, may hold values from -6 to 6
Outputs:
- migrated: float32 [128, 8, 8, 128], P(('groups', 'shot', 'dom'), 'pair'), parts along dimension 0
There are 2 independent parts, one for each index of `groups`. A program takes and returns all parts, laid end to end along the dimension named above; each array names one. Nothing has to cross between parts.
Inputs may be any that keep to these rules, and one draw needn't show every extreme that they name: owner_map[g] is the row of the brick tables that holds brick g; every row holds exactly one brick. The 16 entries footprint[s, d * 16 + k] name bricks whose rows lie on the owners of dom index d, exactly 4 on each shot index; within a shot all bricks differ. Shot s uses its first aperture[s] brick columns; both ends of the range are reached in every draw.
All inputs are finite; a program needn't handle non-finite values.
Results may differ from a plain program's by a relative error of at most 0.0003.
Values sent between devices are 32-bit elements; how exact they have to be, the bound alone decides.
No kernel may reach another device: no remote copies, remote signals or barrier semaphores. Data moves between devices by JAX's collectives and lax.ppermute only.
A program may use at most 64 MiB of HBM per device.

v0:
```python
import jax
import jax.numpy as jnp
from jax import lax
from jax.sharding import PartitionSpec as P

KY = 4
STEPS = 16


first_weights = (0.8, -0.2, 4.0 / 105.0, -1.0 / 280.0)
second_weights = (-205.0 / 72.0, 1.6, -0.2, 8.0 / 315.0, -1.0 / 560.0)


def padded_2(shard, sides, width):
    for axis, dim in sides:
        size, length = (lax.axis_size(axis), shard.shape[dim])
        up = [(i, (i + 1) % size) for i in range(size - 1)]
        down = [(j, i) for i, j in up]
        last = lax.slice_in_dim(shard, length - width, length, axis=dim)
        leading = lax.slice_in_dim(shard, 0, width, axis=dim)
        before = lax.ppermute(last, axis, up)
        after = lax.ppermute(leading, axis, down)
        shard = jnp.concatenate([before, shard, after], axis=dim)
    return shard


def from_partner(shard, axis, apart):
    return lax.ppermute(shard, axis, [(i, i ^ 1 << apart) for i in range(lax.axis_size(axis))])


def derivatives(padded):
    size_x = padded.shape[0] - 8
    size_y = padded.shape[1] - 8
    size_z = padded.shape[2] - 8

    def window(direction, reach):
        start = [4, 4, 4]
        start[direction] = start[direction] + reach
        return padded[
            start[0] : start[0] + size_x, start[1] : start[1] + size_y, start[2] : start[2] + size_z
        ]

    centre = window(0, 0)
    laplace = 3.0 * second_weights[0] * centre
    slopes = []
    for direction in range(3):
        slope = jnp.zeros_like(centre)
        for reach in range(1, 5):
            ahead = window(direction, reach)
            behind = window(direction, -reach)
            laplace = laplace + second_weights[reach] * (ahead + behind)
            slope = slope + first_weights[reach - 1] * (ahead - behind)
        slopes.append(slope)
    return (laplace, slopes)


def advance(padded, earlier, courant_sq, bends):
    laplace, slopes = derivatives(padded)
    drift = bends[0] * slopes[0] + bends[1] * slopes[1] + bends[2] * slopes[2]
    return 2.0 * padded[4:-4, 4:-4, 4:-4] - earlier + courant_sq * (laplace - drift)


def pad_inner(extended):
    return jnp.pad(extended, ((0, 0), (4, 4), (4, 4)))


def per_device(
    velocity,
    density,
    owner_map,
    footprint,
    aperture,
    source_cell,
    receiver_cells,
    wavelet,
    traces,
    states,
    stored_rims,
):
    owners = lax.axis_size("shot")
    columns = lax.axis_size("dom")
    column = lax.axis_index("dom")
    core_index = lax.axis_index("pair")
    stored = velocity.shape[0]
    brick_x = velocity.shape[1]
    brick_y = velocity.shape[2]
    brick_z = velocity.shape[3]
    half_x = brick_x // 2
    prints = footprint[0]
    slot_count = prints.shape[0]
    per_owner = slot_count // owners
    across = KY
    bricks_x = slot_count // across
    table_rows = owner_map[prints]
    owner_of = table_rows // (stored * columns)
    local_row = table_rows % stored
    x_brick = column * bricks_x + jnp.arange(bricks_x, dtype=jnp.int32)
    active_x = x_brick < aperture[0]
    active = jnp.repeat(active_x, across)
    sorted_slots = jnp.argsort(owner_of, stable=True)
    unsorted = jnp.argsort(sorted_slots, stable=True)
    request = jnp.where(active[sorted_slots], local_row[sorted_slots], stored).reshape(
        owners, per_owner
    )
    asked_rows = lax.all_to_all(request, "shot", split_axis=0, concat_axis=0, tiled=True)
    live_rows = (asked_rows < stored).astype(jnp.float32)[:, :, None, None, None]
    picked = jnp.minimum(asked_rows, stored - 1)
    got_vel, got_dens = (
        lax.all_to_all(
            velocity[picked] * live_rows, "shot", split_axis=0, concat_axis=0, tiled=True
        ),
        lax.all_to_all(
            density[picked] * live_rows, "shot", split_axis=0, concat_axis=0, tiled=True
        ),
    )

    def to_block(received):
        bricks = received.reshape(slot_count, brick_x, brick_y, brick_z)[unsorted]
        blocks = bricks.reshape(bricks_x, across, brick_x, brick_y, brick_z).transpose(
            0, 2, 1, 3, 4
        )
        return blocks.reshape(bricks_x * brick_x, across * brick_y, brick_z)

    courant = to_block(got_vel)
    dens_grid = to_block(got_dens)
    in_aperture = jnp.repeat(active_x, brick_x)[:, None, None]
    courant_sq = jnp.where(in_aperture, courant * courant, 0.0)
    log_dens = jnp.where(in_aperture, jnp.log(jnp.where(in_aperture, dens_grid, 1.0)), 0.0)
    dens_extended = padded_2(log_dens, (("dom", 0),), 4)
    unused, bends = derivatives(pad_inner(dens_extended))
    width_x = bricks_x * brick_x
    height = across * brick_y
    cell_count = width_x * height * brick_z
    is_source = core_index == 0
    points = jnp.concatenate([source_cell, receiver_cells[0]]) - column * cell_count
    inside = (points >= 0) & (points < cell_count)
    spot_index = jnp.where(inside, points, 0)
    pulses = wavelet[0]
    recorded = traces[0]
    rim_table = stored_rims[0]

    def advance_one(moment, carry):
        earlier, current, imaged = carry
        extended = padded_2(current, (("dom", 0),), 4)
        updated = advance(pad_inner(extended), earlier, courant_sq, bends)
        src_val = -lax.dynamic_slice_in_dim(pulses, moment, 1)
        rec_val = lax.dynamic_index_in_dim(recorded, moment, 0, keepdims=False)
        values = jnp.where(
            is_source,
            jnp.concatenate([src_val, jnp.zeros_like(rec_val)]),
            jnp.concatenate([jnp.zeros_like(src_val), rec_val]),
        )
        values = jnp.where(inside, values, 0.0)
        updated = updated.reshape(-1).at[spot_index].add(values).reshape(updated.shape)
        rim_now = lax.dynamic_index_in_dim(rim_table, moment, 0, keepdims=False)
        rimmed = updated.at[:, 0, :].set(rim_now[0]).at[:, height - 1, :].set(rim_now[1])
        updated = jnp.where(is_source, rimmed, updated)
        updated = jnp.where(in_aperture, updated, 0.0)
        halves = updated.reshape(bricks_x, 2, half_x, height, brick_z)
        own_cells = lax.dynamic_index_in_dim(halves, core_index, 1, keepdims=False)
        theirs = lax.dynamic_index_in_dim(halves, 1 - core_index, 1, keepdims=False)
        partner = from_partner(theirs, "pair", 0)
        imaged = imaged + own_cells * partner
        return (current, updated, imaged)

    start = (
        states[0, 0, 0],
        states[0, 0, 1],
        jnp.zeros((bricks_x, half_x, height, brick_z), jnp.float32),
    )
    finish = lax.fori_loop(0, STEPS, advance_one, start)
    partial_image = (
        finish[2].reshape(bricks_x, half_x, across, brick_y, brick_z).transpose(0, 2, 1, 3, 4)
    )
    partial_image = partial_image.reshape(slot_count, half_x, brick_y, brick_z)[sorted_slots]
    returned = lax.all_to_all(
        partial_image.reshape(owners, per_owner, half_x, brick_y, brick_z),
        "shot",
        split_axis=0,
        concat_axis=0,
        tiled=True,
    )
    selector = (asked_rows.reshape(1, -1) == jnp.arange(stored, dtype=jnp.int32)[:, None]).astype(
        jnp.float32
    )
    summed = jnp.dot(
        selector,
        returned.reshape(owners * per_owner, -1),
        precision=lax.Precision.HIGHEST,
        preferred_element_type=jnp.float32,
    )
    return summed.reshape(stored, half_x, brick_y, brick_z)


def solution(mesh):
    placed = (
        P(("groups", "shot", "dom"), None, None, None),
        P(("groups", "shot", "dom"), None, None, None),
        P("groups"),
        P(("groups", "shot"), "dom"),
        P(("groups", "shot")),
        P(("groups", "shot")),
        P(("groups", "shot"), None),
        P(("groups", "shot"), None),
        P(("groups", "shot"), None, None),
        P(("groups", "shot"), "pair", None, "dom", None, None),
        P(("groups", "shot"), None, None, "dom", None),
    )
    return jax.shard_map(
        per_device,
        mesh=mesh,
        in_specs=placed,
        out_specs=P(("groups", "shot", "dom"), "pair", None, None),
        check_vma=False,
    )
```

profile of v0, /device:TPU:0, one launch (start us, length us, event | category | flops | bytes accessed | tf_op | source)
XLA Modules:
  0.0 452.1 jit_solution(8120606231775977425)
XLA Ops:
  5.6 11.7 %all_to_all.21 = s32[4,1,4]{2,1,0:T(1,128)S(1)} all-to-all(s32[4,1,4]{2,1,0:T(1,128)S(1)} %bitcast.99), channel_id=1, replica_groups=mesh['groups'=2,'shot'=4,'dom'=2,'pair'=2] {'shot'}, dimensions={0} | all-to-all | bytes 128 | tf_op jit(solution)/shard_map/all_to_all | solution.py:105
  20.7 15.7 %all_to_all.22 = f32[4,4,8,8,128]{4,3,2,1,0:T(8,128)S(1)} all-to-all(f32[4,4,8,8,128]{4,3,2,1,0:T(8,128)S(1)} %get-tuple-element.570), channel_id=1, replica_groups=mesh['groups'=2,'shot'=4,'dom'=2,'pair'=2] {'shot'}, dimensions={0} | all-to-all | bytes 1048576 | tf_op jit(solution)/shard_map/all_to_all | solution.py:109
  36.4 3.5 all-to-all-start.1
  43.7 9.6 %all-to-all-done.1 = f32[4,4,8,8,128]{4,3,2,1,0:T(8,128)S(1)} async-done(((f32[4,4,8,8,128]{4,3,2,1,0:T(8,128)}), f32[4,4,8,8,128]{4,3,2,1,0:T(8,128)S(1)}, u32[]{:S(2)}, u32[]{:S(2)}) %all-to-all-start.1) | async-done | bytes 524320 | tf_op jit(solution)/shard_map/all_to_all | solution.py:112
  55.5 4.5 %collective-permute-start.4 = (f32[4,32,128]{2,1,0:T(8,128)S(1)}, f32[4,32,128]{2,1,0:T(8,128)S(1)}, u32[]{:S(2)}, u32[]{:S(2)}) collective-permute-start(f32[4,32,128]{2,1,0:T(8,128)S(1)} %get-tuple-element.563), channel_id=1, source_target_pairs={{0,2},{1,3},{4,6},{5,7},{8,10},{9,11},{12,14},{13,15},{16,18},{17,... | collective-permute-start | bytes 196616 | tf_op jit(solution)/shard_map/ppermute | solution.py:21
  62.4 2.1 fusion.27
  65.5 370.4 %while.22 = (s32[]{:T(128)}, f32[32,32,128]{2,1,0:T(8,128)}, f32[32,32,128]{2,1,0:T(8,128)S(1)}, f32[4,4,32,128]{3,2,1,0:T(8,128)}, pred[]{:T(512)}, /*index=5*/...) while((s32[]{:T(128)}, f32[32,32,128]{2,1,0:T(8,128)}, ...), condition=%wide.region_4.5_spmd.clone, body=%wide.region_2.4_spmd.clone.sunk | while | flops 14212108 | bytes 26844204 | solution.py:171
  65.5 4.3 collective-permute-start.1
  76.5 3.4 multiply_add_fusion.2
  80.7 4.8 %scatter_fusion = f32[131072]{0:T(1024)S(1)} fusion(f32[131072]{0:T(1024)S(1)} %bitcast.76, s32[513]{0:T(1024)S(1)} %fusion.58, f32[513]{0:T(1024)S(1)} %fusion.59), kind=kCustom, calls=%fused_computation.8.clone.clone.1 | custom fusion | flops 513 | bytes 8208 | tf_op jit(solution)/shard_map/while/body/eval_jaxpr/scatter-add | solution.py:154
  88.3 3.7 collective-permute-start.1
  98.7 3.4 multiply_add_fusion.2
  102.9 4.8 %scatter_fusion = f32[131072]{0:T(1024)S(1)} fusion(f32[131072]{0:T(1024)S(1)} %bitcast.76, s32[513]{0:T(1024)S(1)} %fusion.58, f32[513]{0:T(1024)S(1)} %fusion.59), kind=kCustom, calls=%fused_computation.8.clone.clone.1 | custom fusion | flops 513 | bytes 8208 | tf_op jit(solution)/shard_map/while/body/eval_jaxpr/scatter-add | solution.py:154
  109.7 1.7 fusion.60
  111.4 3.7 collective-permute-start.1
  121.9 3.4 multiply_add_fusion.2
  126.1 4.8 %scatter_fusion = f32[131072]{0:T(1024)S(1)} fusion(f32[131072]{0:T(1024)S(1)} %bitcast.76, s32[513]{0:T(1024)S(1)} %fusion.58, f32[513]{0:T(1024)S(1)} %fusion.59), kind=kCustom, calls=%fused_computation.8.clone.clone.1 | custom fusion | flops 513 | bytes 8208 | tf_op jit(solution)/shard_map/while/body/eval_jaxpr/scatter-add | solution.py:154
  134.6 3.7 collective-permute-start.1
  145.0 3.4 multiply_add_fusion.2
  149.2 4.8 %scatter_fusion = f32[131072]{0:T(1024)S(1)} fusion(f32[131072]{0:T(1024)S(1)} %bitcast.76, s32[513]{0:T(1024)S(1)} %fusion.58, f32[513]{0:T(1024)S(1)} %fusion.59), kind=kCustom, calls=%fused_computation.8.clone.clone.1 | custom fusion | flops 513 | bytes 8208 | tf_op jit(solution)/shard_map/while/body/eval_jaxpr/scatter-add | solution.py:154
  156.1 1.7 fusion.60
  157.8 3.7 collective-permute-start.1
  168.2 3.4 multiply_add_fusion.2
  172.4 4.8 %scatter_fusion = f32[131072]{0:T(1024)S(1)} fusion(f32[131072]{0:T(1024)S(1)} %bitcast.76, s32[513]{0:T(1024)S(1)} %fusion.58, f32[513]{0:T(1024)S(1)} %fusion.59), kind=kCustom, calls=%fused_computation.8.clone.clone.1 | custom fusion | flops 513 | bytes 8208 | tf_op jit(solution)/shard_map/while/body/eval_jaxpr/scatter-add | solution.py:154
  181.0 3.7 collective-permute-start.1
  191.4 3.4 multiply_add_fusion.2
  195.6 4.8 %scatter_fusion = f32[131072]{0:T(1024)S(1)} fusion(f32[131072]{0:T(1024)S(1)} %bitcast.76, s32[513]{0:T(1024)S(1)} %fusion.58, f32[513]{0:T(1024)S(1)} %fusion.59), kind=kCustom, calls=%fused_computation.8.clone.clone.1 | custom fusion | flops 513 | bytes 8208 | tf_op jit(solution)/shard_map/while/body/eval_jaxpr/scatter-add | solution.py:154
  202.4 1.7 fusion.60
  204.1 3.7 collective-permute-start.1
  214.6 3.4 multiply_add_fusion.2
  218.7 4.8 %scatter_fusion = f32[131072]{0:T(1024)S(1)} fusion(f32[131072]{0:T(1024)S(1)} %bitcast.76, s32[513]{0:T(1024)S(1)} %fusion.58, f32[513]{0:T(1024)S(1)} %fusion.59), kind=kCustom, calls=%fused_computation.8.clone.clone.1 | custom fusion | flops 513 | bytes 8208 | tf_op jit(solution)/shard_map/while/body/eval_jaxpr/scatter-add | solution.py:154
  227.3 3.7 collective-permute-start.1
  237.7 3.4 multiply_add_fusion.2
  241.9 4.8 %scatter_fusion = f32[131072]{0:T(1024)S(1)} fusion(f32[131072]{0:T(1024)S(1)} %bitcast.76, s32[513]{0:T(1024)S(1)} %fusion.58, f32[513]{0:T(1024)S(1)} %fusion.59), kind=kCustom, calls=%fused_computation.8.clone.clone.1 | custom fusion | flops 513 | bytes 8208 | tf_op jit(solution)/shard_map/while/body/eval_jaxpr/scatter-add | solution.py:154
  248.7 1.7 fusion.60
  250.5 3.7 collective-permute-start.1
  260.9 3.4 multiply_add_fusion.2
  265.1 4.8 %scatter_fusion = f32[131072]{0:T(1024)S(1)} fusion(f32[131072]{0:T(1024)S(1)} %bitcast.76, s32[513]{0:T(1024)S(1)} %fusion.58, f32[513]{0:T(1024)S(1)} %fusion.59), kind=kCustom, calls=%fused_computation.8.clone.clone.1 | custom fusion | flops 513 | bytes 8208 | tf_op jit(solution)/shard_map/while/body/eval_jaxpr/scatter-add | solution.py:154
  273.7 3.7 collective-permute-start.1
  284.1 3.4 multiply_add_fusion.2
  288.3 4.8 %scatter_fusion = f32[131072]{0:T(1024)S(1)} fusion(f32[131072]{0:T(1024)S(1)} %bitcast.76, s32[513]{0:T(1024)S(1)} %fusion.58, f32[513]{0:T(1024)S(1)} %fusion.59), kind=kCustom, calls=%fused_computation.8.clone.clone.1 | custom fusion | flops 513 | bytes 8208 | tf_op jit(solution)/shard_map/while/body/eval_jaxpr/scatter-add | solution.py:154
  296.8 3.7 collective-permute-start.1
  307.2 3.4 multiply_add_fusion.2
  311.4 4.8 %scatter_fusion = f32[131072]{0:T(1024)S(1)} fusion(f32[131072]{0:T(1024)S(1)} %bitcast.76, s32[513]{0:T(1024)S(1)} %fusion.58, f32[513]{0:T(1024)S(1)} %fusion.59), kind=kCustom, calls=%fused_computation.8.clone.clone.1 | custom fusion | flops 513 | bytes 8208 | tf_op jit(solution)/shard_map/while/body/eval_jaxpr/scatter-add | solution.py:154
  318.3 1.7 fusion.60
  320.0 3.7 collective-permute-start.1
  330.4 3.4 multiply_add_fusion.2
  334.6 4.8 %scatter_fusion = f32[131072]{0:T(1024)S(1)} fusion(f32[131072]{0:T(1024)S(1)} %bitcast.76, s32[513]{0:T(1024)S(1)} %fusion.58, f32[513]{0:T(1024)S(1)} %fusion.59), kind=kCustom, calls=%fused_computation.8.clone.clone.1 | custom fusion | flops 513 | bytes 8208 | tf_op jit(solution)/shard_map/while/body/eval_jaxpr/scatter-add | solution.py:154
  343.2 3.7 collective-permute-start.1
  353.6 3.4 multiply_add_fusion.2
  357.8 4.8 %scatter_fusion = f32[131072]{0:T(1024)S(1)} fusion(f32[131072]{0:T(1024)S(1)} %bitcast.76, s32[513]{0:T(1024)S(1)} %fusion.58, f32[513]{0:T(1024)S(1)} %fusion.59), kind=kCustom, calls=%fused_computation.8.clone.clone.1 | custom fusion | flops 513 | bytes 8208 | tf_op jit(solution)/shard_map/while/body/eval_jaxpr/scatter-add | solution.py:154
  364.6 1.7 fusion.60
  366.3 3.7 collective-permute-start.1
  376.8 3.4 multiply_add_fusion.2
  381.0 4.8 %scatter_fusion = f32[131072]{0:T(1024)S(1)} fusion(f32[131072]{0:T(1024)S(1)} %bitcast.76, s32[513]{0:T(1024)S(1)} %fusion.58, f32[513]{0:T(1024)S(1)} %fusion.59), kind=kCustom, calls=%fused_computation.8.clone.clone.1 | custom fusion | flops 513 | bytes 8208 | tf_op jit(solution)/shard_map/while/body/eval_jaxpr/scatter-add | solution.py:154
  389.5 3.7 collective-permute-start.1
  399.9 3.4 multiply_add_fusion.2
  404.1 4.8 %scatter_fusion = f32[131072]{0:T(1024)S(1)} fusion(f32[131072]{0:T(1024)S(1)} %bitcast.76, s32[513]{0:T(1024)S(1)} %fusion.58, f32[513]{0:T(1024)S(1)} %fusion.59), kind=kCustom, calls=%fused_computation.8.clone.clone.1 | custom fusion | flops 513 | bytes 8208 | tf_op jit(solution)/shard_map/while/body/eval_jaxpr/scatter-add | solution.py:154
  411.0 1.7 fusion.60
  412.7 3.7 collective-permute-start.1
  423.1 3.4 multiply_add_fusion.2
  427.3 4.8 %scatter_fusion = f32[131072]{0:T(1024)S(1)} fusion(f32[131072]{0:T(1024)S(1)} %bitcast.76, s32[513]{0:T(1024)S(1)} %fusion.58, f32[513]{0:T(1024)S(1)} %fusion.59), kind=kCustom, calls=%fused_computation.8.clone.clone.1 | custom fusion | flops 513 | bytes 8208 | tf_op jit(solution)/shard_map/while/body/eval_jaxpr/scatter-add | solution.py:154
  438.1 3.4 all-to-all-start.3
  441.6 9.3 %all-to-all-done.3 = f32[4,4,4,8,128]{4,3,2,1,0:T(8,128)S(1)} async-done(((f32[4,4,4,8,128]{4,3,2,1,0:T(8,128)}), f32[4,4,4,8,128]{4,3,2,1,0:T(8,128)S(1)}, u32[]{:S(2)}, u32[]{:S(2)}) %all-to-all-start.3) | async-done | bytes 262176 | tf_op jit(solution)/shard_map/all_to_all | solution.py:176
  (441 shorter events, 174.7 us)
Async XLA Ops:
  0.0 18.5 %copy-start = (f32[8,8,8,128]{3,2,1,0:T(8,128)S(1)}, f32[8,8,8,128]{3,2,1,0:T(8,128)}, u32[]{:S(2)}) copy-start(f32[8,8,8,128]{3,2,1,0:T(8,128)} %param.17) | copy-start | bytes 786436
  0.0 19.1 %copy-start.2 = (f32[8,8,8,128]{3,2,1,0:T(8,128)S(1)}, f32[8,8,8,128]{3,2,1,0:T(8,128)}, u32[]{:S(2)}) copy-start(f32[8,8,8,128]{3,2,1,0:T(8,128)} %param.18) | copy-start | bytes 786436
  19.7 22.3 %copy-start.3 = (s32[1,512]{1,0:T(1,128)S(1)}, s32[1,512]{1,0:T(1,128)}, u32[]{:S(2)}) copy-start(s32[1,512]{1,0:T(1,128)} %param.23) | copy-start | bytes 6148
  19.7 22.4 %copy-start.1 = (f32[1,1,2,32,32,128]{5,4,3,2,1,0:T(8,128)S(1)}, f32[1,1,2,32,32,128]{5,4,3,2,1,0:T(8,128)}, u32[]{:S(2)}) copy-start(f32[1,1,2,32,32,128]{5,4,3,2,1,0:T(8,128)} %param.26) | copy-start | bytes 3145732
  36.4 16.9 %all-to-all-start.1 = ((f32[4,4,8,8,128]{4,3,2,1,0:T(8,128)}), f32[4,4,8,8,128]{4,3,2,1,0:T(8,128)S(1)}, u32[]{:S(2)}, u32[]{:S(2)}) async-start(f32[4,4,8,8,128]{4,3,2,1,0:T(8,128)} %get-tuple-element.571), calls=%async_computation.1 | async-start | bytes 1048576 | tf_op jit(solution)/shard_map/all_to_all | solution.py:112
  54.2 6.2 %collective-permute-start.3 = (f32[4,32,128]{2,1,0:T(8,128)S(1)}, f32[4,32,128]{2,1,0:T(8,128)S(1)}, u32[]{:S(2)}, u32[]{:S(2)}) collective-permute-start(f32[4,32,128]{2,1,0:T(8,128)S(1)} %get-tuple-element.562), channel_id=1, source_target_pairs={{2,0},{3,1},{6,4},{7,5},{10,8},{11,9},{14,12},{15,13},{18,16},{19,... | collective-permute-start | bytes 196616 | tf_op jit(solution)/shard_map/ppermute | solution.py:22
  55.5 6.4 %collective-permute-start.4 = (f32[4,32,128]{2,1,0:T(8,128)S(1)}, f32[4,32,128]{2,1,0:T(8,128)S(1)}, u32[]{:S(2)}, u32[]{:S(2)}) collective-permute-start(f32[4,32,128]{2,1,0:T(8,128)S(1)} %get-tuple-element.563), channel_id=1, source_target_pairs={{0,2},{1,3},{4,6},{5,7},{8,10},{9,11},{12,14},{13,15},{16,18},{17,... | collective-permute-start | bytes 196616 | tf_op jit(solution)/shard_map/ppermute | solution.py:21
  62.4 3.1 copy-start.4
  65.5 8.6 %collective-permute-start.1 = (f32[4,32,128]{2,1,0:T(8,128)S(1)}, f32[4,32,128]{2,1,0:T(8,128)S(1)}, u32[]{:S(2)}, u32[]{:S(2)}) collective-permute-start(f32[4,32,128]{2,1,0:T(8,128)S(1)} %get-tuple-element.686), channel_id=1, source_target_pairs={{0,2},{1,3},{4,6},{5,7},{8,10},{9,11},{12,14},{13,15},{16,18},{17,... | collective-permute-start | bytes 196616 | tf_op jit(solution)/shard_map/while/body/eval_jaxpr/ppermute | solution.py:21
  69.8 6.2 %collective-permute-start = (f32[4,32,128]{2,1,0:T(8,128)S(1)}, f32[4,32,128]{2,1,0:T(8,128)S(1)}, u32[]{:S(2)}, u32[]{:S(2)}) collective-permute-start(f32[4,32,128]{2,1,0:T(8,128)S(1)} %get-tuple-element.685), channel_id=1, source_target_pairs={{2,0},{3,1},{6,4},{7,5},{10,8},{11,9},{14,12},{15,13},{18,16},{19,... | collective-permute-start | bytes 196616 | tf_op jit(solution)/shard_map/while/body/eval_jaxpr/ppermute | solution.py:22
  85.9 1.6 collective-permute-start.2
  88.3 8.1 %collective-permute-start.1 = (f32[4,32,128]{2,1,0:T(8,128)S(1)}, f32[4,32,128]{2,1,0:T(8,128)S(1)}, u32[]{:S(2)}, u32[]{:S(2)}) collective-permute-start(f32[4,32,128]{2,1,0:T(8,128)S(1)} %get-tuple-element.686), channel_id=1, source_target_pairs={{0,2},{1,3},{4,6},{5,7},{8,10},{9,11},{12,14},{13,15},{16,18},{17,... | collective-permute-start | bytes 196616 | tf_op jit(solution)/shard_map/while/body/eval_jaxpr/ppermute | solution.py:21
  92.0 6.2 %collective-permute-start = (f32[4,32,128]{2,1,0:T(8,128)S(1)}, f32[4,32,128]{2,1,0:T(8,128)S(1)}, u32[]{:S(2)}, u32[]{:S(2)}) collective-permute-start(f32[4,32,128]{2,1,0:T(8,128)S(1)} %get-tuple-element.685), channel_id=1, source_target_pairs={{2,0},{3,1},{6,4},{7,5},{10,8},{11,9},{14,12},{15,13},{18,16},{19,... | collective-permute-start | bytes 196616 | tf_op jit(solution)/shard_map/while/body/eval_jaxpr/ppermute | solution.py:22
  108.1 1.6 collective-permute-start.2
  111.4 8.1 %collective-permute-start.1 = (f32[4,32,128]{2,1,0:T(8,128)S(1)}, f32[4,32,128]{2,1,0:T(8,128)S(1)}, u32[]{:S(2)}, u32[]{:S(2)}) collective-permute-start(f32[4,32,128]{2,1,0:T(8,128)S(1)} %get-tuple-element.686), channel_id=1, source_target_pairs={{0,2},{1,3},{4,6},{5,7},{8,10},{9,11},{12,14},{13,15},{16,18},{17,... | collective-permute-start | bytes 196616 | tf_op jit(solution)/shard_map/while/body/eval_jaxpr/ppermute | solution.py:21
  115.2 6.2 %collective-permute-start = (f32[4,32,128]{2,1,0:T(8,128)S(1)}, f32[4,32,128]{2,1,0:T(8,128)S(1)}, u32[]{:S(2)}, u32[]{:S(2)}) collective-permute-start(f32[4,32,128]{2,1,0:T(8,128)S(1)} %get-tuple-element.685), channel_id=1, source_target_pairs={{2,0},{3,1},{6,4},{7,5},{10,8},{11,9},{14,12},{15,13},{18,16},{19,... | collective-permute-start | bytes 196616 | tf_op jit(solution)/shard_map/while/body/eval_jaxpr/ppermute | solution.py:22
  131.3 1.6 collective-permute-start.2
  134.6 8.1 %collective-permute-start.1 = (f32[4,32,128]{2,1,0:T(8,128)S(1)}, f32[4,32,128]{2,1,0:T(8,128)S(1)}, u32[]{:S(2)}, u32[]{:S(2)}) collective-permute-start(f32[4,32,128]{2,1,0:T(8,128)S(1)} %get-tuple-element.686), channel_id=1, source_target_pairs={{0,2},{1,3},{4,6},{5,7},{8,10},{9,11},{12,14},{13,15},{16,18},{17,... | collective-permute-start | bytes 196616 | tf_op jit(solution)/shard_map/while/body/eval_jaxpr/ppermute | solution.py:21
  138.4 6.2 %collective-permute-start = (f32[4,32,128]{2,1,0:T(8,128)S(1)}, f32[4,32,128]{2,1,0:T(8,128)S(1)}, u32[]{:S(2)}, u32[]{:S(2)}) collective-permute-start(f32[4,32,128]{2,1,0:T(8,128)S(1)} %get-tuple-element.685), channel_id=1, source_target_pairs={{2,0},{3,1},{6,4},{7,5},{10,8},{11,9},{14,12},{15,13},{18,16},{19,... | collective-permute-start | bytes 196616 | tf_op jit(solution)/shard_map/while/body/eval_jaxpr/ppermute | solution.py:22
  154.4 1.6 collective-permute-start.2
  157.8 8.1 %collective-permute-start.1 = (f32[4,32,128]{2,1,0:T(8,128)S(1)}, f32[4,32,128]{2,1,0:T(8,128)S(1)}, u32[]{:S(2)}, u32[]{:S(2)}) collective-permute-start(f32[4,32,128]{2,1,0:T(8,128)S(1)} %get-tuple-element.686), channel_id=1, source_target_pairs={{0,2},{1,3},{4,6},{5,7},{8,10},{9,11},{12,14},{13,15},{16,18},{17,... | collective-permute-start | bytes 196616 | tf_op jit(solution)/shard_map/while/body/eval_jaxpr/ppermute | solution.py:21
  161.5 6.2 %collective-permute-start = (f32[4,32,128]{2,1,0:T(8,128)S(1)}, f32[4,32,128]{2,1,0:T(8,128)S(1)}, u32[]{:S(2)}, u32[]{:S(2)}) collective-permute-start(f32[4,32,128]{2,1,0:T(8,128)S(1)} %get-tuple-element.685), channel_id=1, source_target_pairs={{2,0},{3,1},{6,4},{7,5},{10,8},{11,9},{14,12},{15,13},{18,16},{19,... | collective-permute-start | bytes 196616 | tf_op jit(solution)/shard_map/while/body/eval_jaxpr/ppermute | solution.py:22
  177.6 1.6 collective-permute-start.2
  181.0 8.1 %collective-permute-start.1 = (f32[4,32,128]{2,1,0:T(8,128)S(1)}, f32[4,32,128]{2,1,0:T(8,128)S(1)}, u32[]{:S(2)}, u32[]{:S(2)}) collective-permute-start(f32[4,32,128]{2,1,0:T(8,128)S(1)} %get-tuple-element.686), channel_id=1, source_target_pairs={{0,2},{1,3},{4,6},{5,7},{8,10},{9,11},{12,14},{13,15},{16,18},{17,... | collective-permute-start | bytes 196616 | tf_op jit(solution)/shard_map/while/body/eval_jaxpr/ppermute | solution.py:21
  184.7 6.2 %collective-permute-start = (f32[4,32,128]{2,1,0:T(8,128)S(1)}, f32[4,32,128]{2,1,0:T(8,128)S(1)}, u32[]{:S(2)}, u32[]{:S(2)}) collective-permute-start(f32[4,32,128]{2,1,0:T(8,128)S(1)} %get-tuple-element.685), channel_id=1, source_target_pairs={{2,0},{3,1},{6,4},{7,5},{10,8},{11,9},{14,12},{15,13},{18,16},{19,... | collective-permute-start | bytes 196616 | tf_op jit(solution)/shard_map/while/body/eval_jaxpr/ppermute | solution.py:22
  200.8 1.6 collective-permute-start.2
  204.1 8.1 %collective-permute-start.1 = (f32[4,32,128]{2,1,0:T(8,128)S(1)}, f32[4,32,128]{2,1,0:T(8,128)S(1)}, u32[]{:S(2)}, u32[]{:S(2)}) collective-permute-start(f32[4,32,128]{2,1,0:T(8,128)S(1)} %get-tuple-element.686), channel_id=1, source_target_pairs={{0,2},{1,3},{4,6},{5,7},{8,10},{9,11},{12,14},{13,15},{16,18},{17,... | collective-permute-start | bytes 196616 | tf_op jit(solution)/shard_map/while/body/eval_jaxpr/ppermute | solution.py:21
  207.9 6.2 %collective-permute-start = (f32[4,32,128]{2,1,0:T(8,128)S(1)}, f32[4,32,128]{2,1,0:T(8,128)S(1)}, u32[]{:S(2)}, u32[]{:S(2)}) collective-permute-start(f32[4,32,128]{2,1,0:T(8,128)S(1)} %get-tuple-element.685), channel_id=1, source_target_pairs={{2,0},{3,1},{6,4},{7,5},{10,8},{11,9},{14,12},{15,13},{18,16},{19,... | collective-permute-start | bytes 196616 | tf_op jit(solution)/shard_map/while/body/eval_jaxpr/ppermute | solution.py:22
  224.0 1.6 collective-permute-start.2
  227.3 8.1 %collective-permute-start.1 = (f32[4,32,128]{2,1,0:T(8,128)S(1)}, f32[4,32,128]{2,1,0:T(8,128)S(1)}, u32[]{:S(2)}, u32[]{:S(2)}) collective-permute-start(f32[4,32,128]{2,1,0:T(8,128)S(1)} %get-tuple-element.686), channel_id=1, source_target_pairs={{0,2},{1,3},{4,6},{5,7},{8,10},{9,11},{12,14},{13,15},{16,18},{17,... | collective-permute-start | bytes 196616 | tf_op jit(solution)/shard_map/while/body/eval_jaxpr/ppermute | solution.py:21
  231.0 6.2 %collective-permute-start = (f32[4,32,128]{2,1,0:T(8,128)S(1)}, f32[4,32,128]{2,1,0:T(8,128)S(1)}, u32[]{:S(2)}, u32[]{:S(2)}) collective-permute-start(f32[4,32,128]{2,1,0:T(8,128)S(1)} %get-tuple-element.685), channel_id=1, source_target_pairs={{2,0},{3,1},{6,4},{7,5},{10,8},{11,9},{14,12},{15,13},{18,16},{19,... | collective-permute-start | bytes 196616 | tf_op jit(solution)/shard_map/while/body/eval_jaxpr/ppermute | solution.py:22
  247.1 1.6 collective-permute-start.2
  250.5 8.1 %collective-permute-start.1 = (f32[4,32,128]{2,1,0:T(8,128)S(1)}, f32[4,32,128]{2,1,0:T(8,128)S(1)}, u32[]{:S(2)}, u32[]{:S(2)}) collective-permute-start(f32[4,32,128]{2,1,0:T(8,128)S(1)} %get-tuple-element.686), channel_id=1, source_target_pairs={{0,2},{1,3},{4,6},{5,7},{8,10},{9,11},{12,14},{13,15},{16,18},{17,... | collective-permute-start | bytes 196616 | tf_op jit(solution)/shard_map/while/body/eval_jaxpr/ppermute | solution.py:21
  254.2 6.2 %collective-permute-start = (f32[4,32,128]{2,1,0:T(8,128)S(1)}, f32[4,32,128]{2,1,0:T(8,128)S(1)}, u32[]{:S(2)}, u32[]{:S(2)}) collective-permute-start(f32[4,32,128]{2,1,0:T(8,128)S(1)} %get-tuple-element.685), channel_id=1, source_target_pairs={{2,0},{3,1},{6,4},{7,5},{10,8},{11,9},{14,12},{15,13},{18,16},{19,... | collective-permute-start | bytes 196616 | tf_op jit(solution)/shard_map/while/body/eval_jaxpr/ppermute | solution.py:22
  270.3 1.6 collective-permute-start.2
  273.7 8.1 %collective-permute-start.1 = (f32[4,32,128]{2,1,0:T(8,128)S(1)}, f32[4,32,128]{2,1,0:T(8,128)S(1)}, u32[]{:S(2)}, u32[]{:S(2)}) collective-permute-start(f32[4,32,128]{2,1,0:T(8,128)S(1)} %get-tuple-element.686), channel_id=1, source_target_pairs={{0,2},{1,3},{4,6},{5,7},{8,10},{9,11},{12,14},{13,15},{16,18},{17,... | collective-permute-start | bytes 196616 | tf_op jit(solution)/shard_map/while/body/eval_jaxpr/ppermute | solution.py:21
  277.4 6.2 %collective-permute-start = (f32[4,32,128]{2,1,0:T(8,128)S(1)}, f32[4,32,128]{2,1,0:T(8,128)S(1)}, u32[]{:S(2)}, u32[]{:S(2)}) collective-permute-start(f32[4,32,128]{2,1,0:T(8,128)S(1)} %get-tuple-element.685), channel_id=1, source_target_pairs={{2,0},{3,1},{6,4},{7,5},{10,8},{11,9},{14,12},{15,13},{18,16},{19,... | collective-permute-start | bytes 196616 | tf_op jit(solution)/shard_map/while/body/eval_jaxpr/ppermute | solution.py:22
  293.5 1.6 collective-permute-start.2
  296.8 8.1 %collective-permute-start.1 = (f32[4,32,128]{2,1,0:T(8,128)S(1)}, f32[4,32,128]{2,1,0:T(8,128)S(1)}, u32[]{:S(2)}, u32[]{:S(2)}) collective-permute-start(f32[4,32,128]{2,1,0:T(8,128)S(1)} %get-tuple-element.686), channel_id=1, source_target_pairs={{0,2},{1,3},{4,6},{5,7},{8,10},{9,11},{12,14},{13,15},{16,18},{17,... | collective-permute-start | bytes 196616 | tf_op jit(solution)/shard_map/while/body/eval_jaxpr/ppermute | solution.py:21
  300.6 6.2 %collective-permute-start = (f32[4,32,128]{2,1,0:T(8,128)S(1)}, f32[4,32,128]{2,1,0:T(8,128)S(1)}, u32[]{:S(2)}, u32[]{:S(2)}) collective-permute-start(f32[4,32,128]{2,1,0:T(8,128)S(1)} %get-tuple-element.685), channel_id=1, source_target_pairs={{2,0},{3,1},{6,4},{7,5},{10,8},{11,9},{14,12},{15,13},{18,16},{19,... | collective-permute-start | bytes 196616 | tf_op jit(solution)/shard_map/while/body/eval_jaxpr/ppermute | solution.py:22
  316.7 1.6 collective-permute-start.2
  320.0 8.1 %collective-permute-start.1 = (f32[4,32,128]{2,1,0:T(8,128)S(1)}, f32[4,32,128]{2,1,0:T(8,128)S(1)}, u32[]{:S(2)}, u32[]{:S(2)}) collective-permute-start(f32[4,32,128]{2,1,0:T(8,128)S(1)} %get-tuple-element.686), channel_id=1, source_target_pairs={{0,2},{1,3},{4,6},{5,7},{8,10},{9,11},{12,14},{13,15},{16,18},{17,... | collective-permute-start | bytes 196616 | tf_op jit(solution)/shard_map/while/body/eval_jaxpr/ppermute | solution.py:21
  323.7 6.2 %collective-permute-start = (f32[4,32,128]{2,1,0:T(8,128)S(1)}, f32[4,32,128]{2,1,0:T(8,128)S(1)}, u32[]{:S(2)}, u32[]{:S(2)}) collective-permute-start(f32[4,32,128]{2,1,0:T(8,128)S(1)} %get-tuple-element.685), channel_id=1, source_target_pairs={{2,0},{3,1},{6,4},{7,5},{10,8},{11,9},{14,12},{15,13},{18,16},{19,... | collective-permute-start | bytes 196616 | tf_op jit(solution)/shard_map/while/body/eval_jaxpr/ppermute | solution.py:22
  339.8 1.6 collective-permute-start.2
  343.2 8.1 %collective-permute-start.1 = (f32[4,32,128]{2,1,0:T(8,128)S(1)}, f32[4,32,128]{2,1,0:T(8,128)S(1)}, u32[]{:S(2)}, u32[]{:S(2)}) collective-permute-start(f32[4,32,128]{2,1,0:T(8,128)S(1)} %get-tuple-element.686), channel_id=1, source_target_pairs={{0,2},{1,3},{4,6},{5,7},{8,10},{9,11},{12,14},{13,15},{16,18},{17,... | collective-permute-start | bytes 196616 | tf_op jit(solution)/shard_map/while/body/eval_jaxpr/ppermute | solution.py:21
  346.9 6.2 %collective-permute-start = (f32[4,32,128]{2,1,0:T(8,128)S(1)}, f32[4,32,128]{2,1,0:T(8,128)S(1)}, u32[]{:S(2)}, u32[]{:S(2)}) collective-permute-start(f32[4,32,128]{2,1,0:T(8,128)S(1)} %get-tuple-element.685), channel_id=1, source_target_pairs={{2,0},{3,1},{6,4},{7,5},{10,8},{11,9},{14,12},{15,13},{18,16},{19,... | collective-permute-start | bytes 196616 | tf_op jit(solution)/shard_map/while/body/eval_jaxpr/ppermute | solution.py:22
  363.0 1.6 collective-permute-start.2
  366.3 8.1 %collective-permute-start.1 = (f32[4,32,128]{2,1,0:T(8,128)S(1)}, f32[4,32,128]{2,1,0:T(8,128)S(1)}, u32[]{:S(2)}, u32[]{:S(2)}) collective-permute-start(f32[4,32,128]{2,1,0:T(8,128)S(1)} %get-tuple-element.686), channel_id=1, source_target_pairs={{0,2},{1,3},{4,6},{5,7},{8,10},{9,11},{12,14},{13,15},{16,18},{17,... | collective-permute-start | bytes 196616 | tf_op jit(solution)/shard_map/while/body/eval_jaxpr/ppermute | solution.py:21
  370.1 6.2 %collective-permute-start = (f32[4,32,128]{2,1,0:T(8,128)S(1)}, f32[4,32,128]{2,1,0:T(8,128)S(1)}, u32[]{:S(2)}, u32[]{:S(2)}) collective-permute-start(f32[4,32,128]{2,1,0:T(8,128)S(1)} %get-tuple-element.685), channel_id=1, source_target_pairs={{2,0},{3,1},{6,4},{7,5},{10,8},{11,9},{14,12},{15,13},{18,16},{19,... | collective-permute-start | bytes 196616 | tf_op jit(solution)/shard_map/while/body/eval_jaxpr/ppermute | solution.py:22
  386.2 1.6 collective-permute-start.2
  389.5 8.1 %collective-permute-start.1 = (f32[4,32,128]{2,1,0:T(8,128)S(1)}, f32[4,32,128]{2,1,0:T(8,128)S(1)}, u32[]{:S(2)}, u32[]{:S(2)}) collective-permute-start(f32[4,32,128]{2,1,0:T(8,128)S(1)} %get-tuple-element.686), channel_id=1, source_target_pairs={{0,2},{1,3},{4,6},{5,7},{8,10},{9,11},{12,14},{13,15},{16,18},{17,... | collective-permute-start | bytes 196616 | tf_op jit(solution)/shard_map/while/body/eval_jaxpr/ppermute | solution.py:21
  393.3 6.2 %collective-permute-start = (f32[4,32,128]{2,1,0:T(8,128)S(1)}, f32[4,32,128]{2,1,0:T(8,128)S(1)}, u32[]{:S(2)}, u32[]{:S(2)}) collective-permute-start(f32[4,32,128]{2,1,0:T(8,128)S(1)} %get-tuple-element.685), channel_id=1, source_target_pairs={{2,0},{3,1},{6,4},{7,5},{10,8},{11,9},{14,12},{15,13},{18,16},{19,... | collective-permute-start | bytes 196616 | tf_op jit(solution)/shard_map/while/body/eval_jaxpr/ppermute | solution.py:22
  409.3 1.6 collective-permute-start.2
  412.7 8.1 %collective-permute-start.1 = (f32[4,32,128]{2,1,0:T(8,128)S(1)}, f32[4,32,128]{2,1,0:T(8,128)S(1)}, u32[]{:S(2)}, u32[]{:S(2)}) collective-permute-start(f32[4,32,128]{2,1,0:T(8,128)S(1)} %get-tuple-element.686), channel_id=1, source_target_pairs={{0,2},{1,3},{4,6},{5,7},{8,10},{9,11},{12,14},{13,15},{16,18},{17,... | collective-permute-start | bytes 196616 | tf_op jit(solution)/shard_map/while/body/eval_jaxpr/ppermute | solution.py:21
  416.4 6.2 %collective-permute-start = (f32[4,32,128]{2,1,0:T(8,128)S(1)}, f32[4,32,128]{2,1,0:T(8,128)S(1)}, u32[]{:S(2)}, u32[]{:S(2)}) collective-permute-start(f32[4,32,128]{2,1,0:T(8,128)S(1)} %get-tuple-element.685), channel_id=1, source_target_pairs={{2,0},{3,1},{6,4},{7,5},{10,8},{11,9},{14,12},{15,13},{18,16},{19,... | collective-permute-start | bytes 196616 | tf_op jit(solution)/shard_map/while/body/eval_jaxpr/ppermute | solution.py:22
  432.5 1.6 collective-permute-start.2
  438.1 12.8 %all-to-all-start.3 = ((f32[4,4,4,8,128]{4,3,2,1,0:T(8,128)}), f32[4,4,4,8,128]{4,3,2,1,0:T(8,128)S(1)}, u32[]{:S(2)}, u32[]{:S(2)}) async-start(f32[4,4,4,8,128]{4,3,2,1,0:T(8,128)} %bitcast.25), calls=%async_computation.3 | async-start | bytes 524288 | tf_op jit(solution)/shard_map/all_to_all | solution.py:176
where the time goes:
time: 457 us; the launch traced here: 452 us
  other arithmetic  178 us (39%)
  starting transfers between devices  94.7 us (21%)
  waiting for transfers between devices  72.1 us (16%)
  local copies, waits for them, and re-layouts  65.5 us (14%)
  blocking collectives  27.4 us (6%)
  loops' own time  12.2 us (3%)
    scatter-add x16, other arithmetic, advance_one(): updated.reshape(-1).at[spot_index].add(values).reshape(updated.shape)  77.2 us
    ppermute x17, starting transfers between devices, padded_2(): before = lax.ppermute(last, axis, up)  64.7 us
    add x16, other arithmetic, advance(): 2.0 * padded[4:-4, 4:-4, 4:-4] - earlier + courant_sq * (laplace - drift)  54.3 us
    ppermute x17, waiting for transfers between devices, padded_2(): after = lax.ppermute(leading, axis, down)  27.2 us
    add x16, other arithmetic, advance_one(): imaged = imaged + own_cells * partner  26.7 us
    ppermute x16, waiting for transfers between devices, from_partner(): lax.ppermute(shard, axis, [(i, i ^ 1 << apart) for i in range(lax.axis_si...  24.3 us
    ppermute x17, starting transfers between devices, padded_2(): after = lax.ppermute(leading, axis, down)  22 us
    all_to_all x1, blocking collectives, per_device(): lax.all_to_all(velocity[picked] * live_rows, 'shot', split_axis=0, concat...  15.7 us
  transfers between devices with their start and end apart: 52, of which 36 were waited for; matrix products, arithmetic and copies ran while one was open for 10% of the time, Pallas kernels for 0%

commit v1 on v0

v1 whole, which is shorter than its diff:
```python
import functools

import jax
import jax.numpy as jnp
import numpy as np
from jax import lax
from jax.experimental import pallas as pl
from jax.experimental.pallas import tpu as pltpu
from jax.sharding import PartitionSpec as P

KY = 4
REACH = 4

first_weights = (0.8, -0.2, 4.0 / 105.0, -1.0 / 280.0)
second_weights = (-205.0 / 72.0, 1.6, -0.2, 8.0 / 315.0, -1.0 / 560.0)

FIRST = first_weights[0]
SECOND = second_weights[1]
first_ratio = tuple(w / FIRST for w in first_weights)
second_ratio = tuple(w / SECOND for w in second_weights[1:])

VMEM_LIMIT = 60 * 1024 * 1024

smem = pl.BlockSpec(memory_space=pltpu.SMEM)
vmem = pl.BlockSpec(memory_space=pltpu.VMEM)
anywhere = pl.BlockSpec(memory_space=pl.ANY)


def z_matrix(size):
    second = np.zeros((size, size))
    first = np.zeros((size, size))
    for r in range(1, REACH + 1):
        for z in range(size):
            if z + r < size:
                second[z + r, z] = second_ratio[r - 1]
                first[z + r, z] = first_ratio[r - 1]
            if z - r >= 0:
                second[z - r, z] = second_ratio[r - 1]
                first[z - r, z] = -first_ratio[r - 1]
    whole = np.concatenate([second, first], axis=1).astype(np.float32)
    high = whole.astype(jnp.bfloat16)
    low = (whole - high.astype(np.float32)).astype(jnp.bfloat16)
    return np.concatenate([high, high, low, low], axis=0)


def xor_swap(block, axis, bits):
    size = lax.axis_size(axis)
    return lax.ppermute(block, axis, [(i, i ^ bits) for i in range(size)])


def slabs_of(block):
    size = lax.axis_size("dom")
    if size == 1:
        return [block]
    if size == 2:
        return [block, xor_swap(block, "dom", 1)]
    hops = 2
    up = [(i, i + 1) for i in range(size - 1)]
    down = [(i + 1, i) for i in range(size - 1)]
    found = [block]
    left = right = block
    for _ in range(hops):
        left = lax.ppermute(left, "dom", up)
        right = lax.ppermute(right, "dom", down)
        found = [left] + found + [right]
    return found


def pack_kernel(owners, columns, slots, meta, prints, owner_map, velocity, density, *outs):
    stored = velocity.shape[0]
    me = meta[0]
    first = meta[2] == 0
    for b in range(owners):

        def place(m, count, b=b):
            row = owner_map[prints[b, m]]
            mine = row // (stored * columns) == me
            local = row % stored

            @pl.when(mine)
            def _():
                outs[b][count] = jnp.where(first, velocity[local], density[local])

            return count + mine.astype(jnp.int32)

        lax.fori_loop(0, slots, place, jnp.int32(0))


def unpack_kernel(owners, columns, slots, stored, meta, prints, owner_map, *refs):
    blocks, out = refs[:-1], refs[-1]
    me = meta[0]
    brick_x, brick_y = blocks[0].shape[1:3]
    for b in range(owners):

        def place(m, count, b=b):
            row = owner_map[prints[0, m]]
            mine = row // (stored * columns) == me ^ b

            @pl.when(mine)
            def _():
                x = pl.multiple_of(m // KY * brick_x, brick_x)
                y = pl.multiple_of(m % KY * brick_y, brick_y)
                out[pl.ds(x, brick_x), pl.ds(y, brick_y), :] = blocks[b][count]

            return count + mine.astype(jnp.int32)

        lax.fori_loop(0, slots, place, jnp.int32(0))


def along_x(load, t, i):
    sums, slopes = [], []
    for r in range(1, REACH + 1):
        ahead, behind = load(i + r, t), load(i - r, t)
        sums.append(ahead + behind)
        slopes.append(ahead - behind)
    return sums, slopes


def along_y(rows, ups, downs, t):
    sums, slopes = [], []
    for r in range(1, REACH + 1):
        ahead = rows[t + r] if t + r < 4 else ups[t + r - 4]
        behind = rows[t - r] if t - r >= 0 else downs[t - r + 4]
        sums.append(ahead + behind)
        slopes.append(ahead - behind)
    return sums, slopes


def weigh(parts, ratios):
    total = parts[0]
    for part, ratio in zip(parts[1:], ratios[1:]):
        total = total + ratio * part
    return total


def shifted_rows(rows, sublane):
    ups = [jnp.where(sublane == 7, 0.0, pltpu.roll(row, 7, 0)) for row in rows]
    downs = [jnp.where(sublane == 0, 0.0, pltpu.roll(row, 1, 0)) for row in rows]
    return ups, downs


def split_rows(value):
    high = value.astype(jnp.bfloat16)
    low = (value - high.astype(jnp.float32)).astype(jnp.bfloat16)
    both = jnp.concatenate([high, low], axis=1)
    return jnp.concatenate([both, both], axis=1)


def steps_kernel(count_slabs, own_lo, flipped, inject_lo, meta, zmat, inject_a, inject_b, *refs):
    states = refs[:count_slabs]
    mine = refs[count_slabs : 2 * count_slabs]
    theirs = refs[2 * count_slabs : 3 * count_slabs]
    rims = refs[3 * count_slabs : 4 * count_slabs]
    keep, send = refs[4 * count_slabs : 4 * count_slabs + 2]
    field, logs, square, centre, gx, gy, gz, pulses, sems = refs[4 * count_slabs + 2 :]
    thick = states[0].shape[1]
    steps = rims[0].shape[0]
    lanes = states[0].shape[3]
    window = thick * count_slabs
    own_hi = own_lo + thick
    column = meta[1]
    is_source = meta[2] == 0
    limit = meta[3]
    sublane = lax.broadcasted_iota(jnp.int32, (8, lanes), 0)
    half_of = meta[2]
    reversed_x = flipped & (column == 1)

    def global_x(w):
        if flipped:
            return jnp.where(column == 1, window - 1 - w, w)
        return w + column * thick - own_lo

    def active(w):
        x = global_x(w)
        return (x >= 0) & (x < limit)

    def local_x(v):
        return jnp.where(reversed_x, thick - 1 - v, v)

    def z_parts(load, width):
        rows = jnp.concatenate([load(i, t) for i in range(width) for t in range(4)], axis=0)
        return jnp.dot(split_rows(rows), zmat[...], preferred_element_type=jnp.float32)

    def lo_of(k):
        return jnp.maximum(0, own_lo - REACH * (steps - 1 - k))

    def hi_of(k):
        return jnp.minimum(window, own_hi + REACH * (steps - 1 - k))

    early = inject_a.shape[0]
    rows_b = inject_b.shape[1]

    def copy_a(k, slot):
        return pltpu.make_async_copy(inject_a.at[k], pulses.at[slot], sems.at[slot])

    def copy_b(k, slot):
        return pltpu.make_async_copy(
            inject_b.at[k - early],
            pulses.at[slot, pl.ds(inject_lo, rows_b)],
            sems.at[slot],
        )

    def start_copy(k, slot):
        @pl.when(k < early)
        def _():
            copy_a(k, slot).start()

        @pl.when((k >= early) & (k < steps))
        def _():
            copy_b(k, slot).start()

    def wait_copy(k, slot):
        @pl.when(k < early)
        def _():
            copy_a(k, slot).wait()

        @pl.when(k >= early)
        def _():
            copy_b(k, slot).wait()

    copy_a(0, 0).start()

    zero = jnp.zeros((REACH, 4, 8, lanes), jnp.float32)
    for level in range(2):
        field[level, 0:REACH] = zero
        field[level, REACH + window : 2 * REACH + window] = zero
    logs[0:REACH] = zero
    logs[REACH + window : 2 * REACH + window] = zero

    for s in range(count_slabs):

        def fill(v, carry, s=s):
            w = s * thick + v
            x = local_x(v)
            on = active(w)
            for t in range(4):
                rows = pl.ds(t, 8, stride=4)
                field[0, REACH + w, t] = states[s][0, x, rows, :]
                field[1, REACH + w, t] = states[s][1, x, rows, :]
                a = mine[s][x, rows, :]
                b = theirs[s][x, rows, :]
                courant = jnp.where(is_source, a, b)
                density = jnp.where(is_source, b, a)
                squared = jnp.where(on, courant * courant, 0.0)
                square[w, t] = SECOND * squared
                centre[w, t] = 2.0 + (3.0 * second_weights[0]) * squared
                logs[REACH + w, t] = jnp.where(on, jnp.log(jnp.where(on, density, 1.0)), 0.0)
            return carry

        lax.fori_loop(0, thick, fill, 0)

    def bend(b, carry):
        w = b * 4

        def load(i, t):
            return logs[REACH + w + i, t]

        zs = z_parts(load, 4)
        for i in range(4):
            rows = [load(i, t) for t in range(4)]
            ups, downs = shifted_rows(rows, sublane)
            for t in range(4):
                scale = (FIRST * FIRST / SECOND) * square[w + i, t]
                at = (i * 4 + t) * 8
                gx[w + i, t] = scale * weigh(along_x(load, t, i)[1], first_ratio)
                gy[w + i, t] = scale * weigh(along_y(rows, ups, downs, t)[1], first_ratio)
                gz[w + i, t] = scale * zs[at : at + 8, lanes : 2 * lanes]
        return carry

    lax.fori_loop(0, window // 4, bend, 0)

    rim_low = (sublane == 0) & is_source
    rim_high = (sublane == 7) & is_source

    def one_step(k, carry):
        old = lax.rem(k, 2)
        new = 1 - old
        slot = lax.rem(k, 2)
        wait_copy(k, slot)
        start_copy(k + 1, 1 - slot)

        def block(b, carry):
            w = b * 4
            on = active(w)

            @pl.when(on)
            def _():
                def load(i, t):
                    return field[new, REACH + w + i, t]

                zs = z_parts(load, 4)
                for i in range(4):
                    rows = [load(i, t) for t in range(4)]
                    ups, downs = shifted_rows(rows, sublane)
                    for t in range(4):
                        sx, dx = along_x(load, t, i)
                        sy, dy = along_y(rows, ups, downs, t)
                        at = (i * 4 + t) * 8
                        laplace = weigh([p + q for p, q in zip(sx, sy)], second_ratio)
                        laplace = laplace + zs[at : at + 8, 0:lanes]
                        value = centre[w + i, t] * rows[t] - field[old, REACH + w + i, t]
                        value = value + square[w + i, t] * laplace
                        value = value - gx[w + i, t] * weigh(dx, first_ratio)
                        value = value - gy[w + i, t] * weigh(dy, first_ratio)
                        value = value - gz[w + i, t] * zs[at : at + 8, lanes : 2 * lanes]
                        row = pl.multiple_of(w * 32 + at, 8)
                        value = value + pulses[slot, pl.ds(row, 8), :]
                        field[old, REACH + w + i, t] = value

            @pl.when(jnp.logical_not(on))
            def _():
                field[old, pl.ds(REACH + w, 4)] = jnp.zeros((4, 4, 8, lanes), jnp.float32)

            return carry

        lax.fori_loop(lo_of(k) // 4, hi_of(k) // 4, block, 0)

        @pl.when(is_source)
        def _():
            for s in range(count_slabs):
                first = jnp.maximum(lo_of(k) - s * thick, 0)
                last = jnp.minimum(hi_of(k) - s * thick, thick)

                def rim(v, carry, s=s):
                    w = s * thick + v
                    x = local_x(v)
                    on = active(w)
                    low = jnp.broadcast_to(rims[s][k, 0, pl.ds(x, 1), :], (8, lanes))
                    high = jnp.broadcast_to(rims[s][k, 1, pl.ds(x, 1), :], (8, lanes))
                    field[old, REACH + w, 0] = jnp.where(
                        rim_low & on, low, field[old, REACH + w, 0]
                    )
                    field[old, REACH + w, 3] = jnp.where(
                        rim_high & on, high, field[old, REACH + w, 3]
                    )
                    return carry

                lax.fori_loop(first, last, rim, 0)

        def record(b, carry):
            w = REACH + own_lo + b * 4
            block_half = lax.rem(jnp.where(reversed_x, b + 1, b), 2)
            values = field[old, pl.ds(w, 4)]

            @pl.when(block_half == half_of)
            def _():
                keep[k, b // 2] = values

            @pl.when(block_half != half_of)
            def _():
                send[k, b // 2] = values

            return carry

        lax.fori_loop(0, thick // 4, record, 0)
        return carry

    lax.fori_loop(0, steps, one_step, 0)


def image_kernel(owners, columns, slots, stored, flipped, meta, prints, owner_map, keep, got, *refs):
    outs, total, grid = refs[:owners], refs[owners], refs[owners + 1]
    steps, cols = keep.shape[:2]
    me = meta[0]
    reversed_x = flipped & (meta[1] == 1)
    brick_y = outs[0].shape[2]

    def clear(c, carry):
        def add(k, value):
            return value + keep[k, c] * got[k, c]

        total[c] = lax.fori_loop(0, steps, add, jnp.zeros(keep.shape[2:], jnp.float32))
        return carry

    lax.fori_loop(0, cols, clear, 0)
    for c in range(cols):
        to = jnp.where(reversed_x, cols - 1 - c, c)
        for i in range(4):
            layer = to * 4 + jnp.where(reversed_x, 3 - i, i)
            for t in range(4):
                grid[layer, pl.ds(t, 8, stride=4), :] = total[c, i, t]
    for b in range(owners):

        def place(m, count, b=b):
            row = owner_map[prints[0, m]]
            mine = row // (stored * columns) == me ^ b

            @pl.when(mine)
            def _():
                x = pl.multiple_of(m // KY * 4, 4)
                y = pl.multiple_of(m % KY * brick_y, brick_y)
                outs[b][count] = grid[pl.ds(x, 4), pl.ds(y, brick_y), :]

            return count + mine.astype(jnp.int32)

        lax.fori_loop(0, slots, place, jnp.int32(0))


def sum_kernel(owners, columns, slots, stored, meta, prints, owner_map, *refs):
    blocks, out = refs[:-1], refs[-1]
    me = meta[0]
    out[...] = jnp.zeros_like(out)
    for b in range(owners):

        def place(m, count, b=b):
            row = owner_map[prints[b, m]]
            mine = row // (stored * columns) == me
            local = row % stored

            @pl.when(mine)
            def _():
                out[local] += blocks[b][count]

            return count + mine.astype(jnp.int32)

        lax.fori_loop(0, slots, place, jnp.int32(0))


def call(kernel, out_shape, in_specs, out_specs, scratch=(), cost=None):
    return pl.pallas_call(
        kernel,
        out_shape=out_shape,
        in_specs=in_specs,
        out_specs=out_specs,
        scratch_shapes=list(scratch),
        compiler_params=pltpu.CompilerParams(vmem_limit_bytes=VMEM_LIMIT),
        cost_estimate=cost,
    )


def injection(window, column, own_lo, flipped, thick, height, lanes, is_source,
              source_cell, receivers, pulses, recorded):
    steps, spots = recorded.shape
    cells = jnp.where(is_source, jnp.concatenate([source_cell, jnp.full((spots - 1,), -1, jnp.int32)]), receivers)
    source_values = jnp.concatenate([-pulses[:, None], jnp.zeros((steps, spots - 1), jnp.float32)], axis=1)
    values = jnp.where(is_source, source_values, recorded)
    x = cells // (height * lanes)
    y = cells // lanes % height
    z = cells % lanes
    if flipped:
        w = jnp.where(column == 1, window - 1 - x, x)
    else:
        w = x - column * thick + own_lo
    rows = w * height + y % 4 * 8 + y // 4
    rows = jnp.where((cells >= 0) & (w >= 0) & (w < window), rows, -1)
    which_row = (lax.broadcasted_iota(jnp.int32, (window * height, spots), 0) == rows[None, :]).astype(jnp.bfloat16)
    early = steps // 2
    deep = REACH * (steps - 1 - early)
    lo = max(0, own_lo - deep)
    hi = min(window, own_lo + thick + deep)
    which_lane = (z[:, None] == lax.broadcasted_iota(jnp.int32, (spots, lanes), 1)).astype(jnp.float32)
    high = lax.reduce_precision(values, 8, 7)
    low = lax.reduce_precision(values - high, 8, 7)
    both = jnp.concatenate([high, low], axis=1)
    spread = both[:, :, None] * jnp.concatenate([which_lane, which_lane], axis=0)[None]
    spread = spread.astype(jnp.bfloat16)
    twice = jnp.concatenate([which_row, which_row], axis=1)

    def product(rows, spread):
        return jnp.einsum("rp,kpz->krz", rows, spread, preferred_element_type=jnp.float32)

    return (
        product(twice, spread[:early]),
        product(twice[lo * height : hi * height], spread[early:]),
        lo * height,
    )


def per_device(
    velocity,
    density,
    owner_map,
    footprint,
    aperture,
    source_cell,
    receiver_cells,
    wavelet,
    traces,
    states,
    stored_rims,
):
    f32 = jnp.float32
    owners = lax.axis_size("shot")
    columns = lax.axis_size("dom")
    column = lax.axis_index("dom")
    pair = lax.axis_index("pair")
    shot = lax.axis_index("shot")
    stored, brick_x, brick_y, brick_z = velocity.shape
    half_x = brick_x // 2
    slots = footprint.shape[1]
    per_owner = slots // owners
    across = KY
    bricks_x = slots // across
    thick = bricks_x * brick_x
    height = across * brick_y
    lanes = brick_z
    steps = wavelet.shape[1]
    flipped = columns == 2
    meta = jnp.stack(
        [shot.astype(jnp.int32), column.astype(jnp.int32), pair.astype(jnp.int32), aperture[0] * brick_x]
    )

    prints = jnp.concatenate(
        [footprint] + [xor_swap(footprint, "shot", b) for b in range(1, owners)], axis=0
    )
    brick = jax.ShapeDtypeStruct((per_owner, brick_x, brick_y, brick_z), f32)
    packed = call(
        functools.partial(pack_kernel, owners, columns, slots),
        [brick] * owners,
        [smem, smem, smem, vmem, vmem],
        [vmem] * owners,
    )(meta, prints, owner_map, velocity, density)
    bricks = [packed[0]] + [xor_swap(packed[b], "shot", b) for b in range(1, owners)]
    table = call(
        functools.partial(unpack_kernel, owners, columns, slots, stored),
        jax.ShapeDtypeStruct((thick, height, lanes), f32),
        [smem, smem, smem] + [vmem] * owners,
        vmem,
    )(meta, prints, owner_map, *bricks)

    state_slabs = slabs_of(states[0, 0])
    rim_slabs = slabs_of(stored_rims[0])
    mine = slabs_of(table)
    theirs = [xor_swap(slab, "pair", 1) for slab in mine]

    count = len(mine)
    own_lo = 0 if flipped else (count // 2) * thick
    window = count * thick
    inject_a, inject_b, inject_lo = injection(
        window, column, own_lo, flipped, thick, height, lanes, pair == 0,
        source_cell, receiver_cells[0], wavelet[0], traces[0],
    )

    kept = jax.ShapeDtypeStruct((steps, bricks_x, half_x, 4, height // 4, lanes), f32)
    grid = (window, 4, height // 4, lanes)
    padded = (window + 2 * REACH, 4, height // 4, lanes)
    keep, send = call(
        functools.partial(steps_kernel, count, own_lo, flipped, inject_lo),
        [kept, kept],
        [smem, vmem, anywhere, anywhere] + [vmem] * (4 * count),
        [vmem, vmem],
        [
            pltpu.VMEM((2,) + padded, f32),
            pltpu.VMEM(padded, f32),
            pltpu.VMEM(grid, f32),
            pltpu.VMEM(grid, f32),
            pltpu.VMEM(grid, f32),
            pltpu.VMEM(grid, f32),
            pltpu.VMEM(grid, f32),
            pltpu.VMEM((2, window * height, lanes), f32),
            pltpu.SemaphoreType.DMA((2,)),
        ],
    )(meta, z_matrix(lanes), inject_a, inject_b, *state_slabs, *mine, *theirs, *rim_slabs)
    got = xor_swap(send, "pair", 1)

    part = jax.ShapeDtypeStruct((per_owner, half_x, brick_y, brick_z), f32)
    images = call(
        functools.partial(image_kernel, owners, columns, slots, stored, flipped),
        [part] * owners,
        [smem, smem, smem, vmem, vmem],
        [vmem] * owners,
        [
            pltpu.VMEM(kept.shape[1:], f32),
            pltpu.VMEM((bricks_x * half_x, height, lanes), f32),
        ],
    )(meta, prints, owner_map, keep, got)
    returned = [images[0]] + [xor_swap(images[b], "shot", b) for b in range(1, owners)]
    return call(
        functools.partial(sum_kernel, owners, columns, slots, stored),
        jax.ShapeDtypeStruct((stored, half_x, brick_y, brick_z), f32),
        [smem, smem, smem] + [vmem] * owners,
        vmem,
    )(meta, prints, owner_map, *returned)


def solution(mesh):
    placed = (
        P(("groups", "shot", "dom"), None, None, None),
        P(("groups", "shot", "dom"), None, None, None),
        P("groups"),
        P(("groups", "shot"), "dom"),
        P(("groups", "shot")),
        P(("groups", "shot")),
        P(("groups", "shot"), None),
        P(("groups", "shot"), None),
        P(("groups", "shot"), None, None),
        P(("groups", "shot"), "pair", None, "dom", None, None),
        P(("groups", "shot"), None, None, "dom", None),
    )
    return jax.shard_map(
        per_device,
        mesh=mesh,
        in_specs=placed,
        out_specs=P(("groups", "shot", "dom"), "pair", None, None),
        check_vma=False,
    )
```

time: 457 us -> 205 us (0.45); the launches traced: 452 us -> 205 us
  other arithmetic: 178 us -> 4.3 us
  Pallas kernels: 0 us -> 134 us
  starting transfers between devices: 94.7 us -> 18 us
  local copies, waits for them, and re-layouts: 65.5 us -> 3.34 us
  waiting for transfers between devices: 72.1 us -> 31.2 us
  blocking collectives: 27.4 us -> 0 us
  matrix products: 0.36 us -> 13.2 us
  loops' own time: 12.2 us -> 0 us
    pallas_call x0 -> x5, Pallas kernels: none -> 134 us  [the longest x1 117 us: per_device(): call(functools.partial(steps_kernel, count, own_lo, flipped, inject_lo),...]
    add x34 -> x0, other arithmetic: 84.1 us -> none  [the longest x16 54.3 us: advance(): 2.0 * padded[4:-4, 4:-4, 4:-4] - earlier + courant_sq * (laplace - drift)]
    scatter-add x16 -> x0, other arithmetic: 77.2 us -> none  [advance_one(): updated.reshape(-1).at[spot_index].add(values).reshape(updated.shape)]
    ppermute x50 -> x15, starting transfers between devices: 87.8 us -> 18 us  [xor_swap(): return lax.ppermute(block, axis, [(i, i ^ bits) for i in range(size)])]
    all_to_all x2 -> x0, blocking collectives: 27.4 us -> none  [the longest x1 15.7 us: per_device(): lax.all_to_all(velocity[picked] * live_rows, 'shot', split_axis=0, concat...]
    dynamic_slice x32 -> x0, local copies, waits for them, and re-layouts: 22 us -> none  [the longest x16 11.7 us: advance_one(): rec_val = lax.dynamic_index_in_dim(recorded, moment, 0, keepdims=False)]
    ppermute x50 -> x15, waiting for transfers between devices: 53.1 us -> 31.2 us  [xor_swap(): return lax.ppermute(block, axis, [(i, i ^ bits) for i in range(size)])]
    all_to_all x2 -> x0, waiting for transfers between devices: 18.9 us -> none  [the longest x1 9.58 us: per_device(): lax.all_to_all(density[picked] * live_rows, 'shot', split_axis=0, concat_...]
  transfers between devices with their start and end apart: 52 -> 15, of which waited for: 36 -> 6; matrix products, arithmetic and copies ran while one was open for 10% -> 9% of each run, Pallas kernels for 0% -> 3%
where the time goes in v1:
time: 205 us
  Pallas kernels  134 us (65%)
  waiting for transfers between devices  31.2 us (15%)
  starting transfers between devices  18 us (9%)
  matrix products  13.2 us (6%)
  other arithmetic  4.3 us (2%)
  local copies, waits for them, and re-layouts  3.34 us (2%)
    pallas_call x1, Pallas kernels, per_device(): call(functools.partial(steps_kernel, count, own_lo, flipped, inject_lo),...  117 us
    ppermute x15, waiting for transfers between devices, xor_swap(): return lax.ppermute(block, axis, [(i, i ^ bits) for i in range(size)])  31.2 us
    ppermute x15, starting transfers between devices, xor_swap(): return lax.ppermute(block, axis, [(i, i ^ bits) for i in range(size)])  18 us
    dot_general x2, matrix products, product(): jnp.einsum('rp,kpz->krz', rows, spread, preferred_element_type=jnp.float32)  13.2 us
    pallas_call x1, Pallas kernels, per_device(): call(functools.partial(image_kernel, owners, columns, slots, stored, flip...  6.6 us
  transfers between devices with their start and end apart: 15, of which 6 were waited for; matrix products, arithmetic and copies ran while one was open for 9% of the time, Pallas kernels for 3%

profile of v1, /device:TPU:0, one launch (start us, length us, event | category | flops | bytes accessed | tf_op | source)
XLA Modules:
  0.0 205.1 jit_solution(15885848862593457694)
XLA Ops:
  0.0 4.0 %collective-permute-start.1 = (s32[1,16]{1,0:T(1,128)}, s32[1,16]{1,0:T(1,128)S(1)}, u32[]{:S(2)}, u32[]{:S(2)}) collective-permute-start(s32[1,16]{1,0:T(1,128)} %param.15), channel_id=1, source_target_pairs={{0,8},{4,12},{8,0},{12,4},{1,9},{5,13},{9,1},{13,5},{2,10},{6,14},... | collective-permute-start | bytes 200 | tf_op jit(solution)/shard_map/ppermute | solution.py:48
  4.0 1.6 collective-permute-start
  5.6 0.0 collective-permute-start.2
  5.6 1.7 collective-permute-start.10
  7.3 0.3 collective-permute-start.3
  8.9 0.7 negate_bitcast_fusion
  9.6 0.1 copy.22
  9.8 0.8 iota_compare_fusion
  10.6 0.8 fusion.17
  11.4 0.7 pad_add_fusion.2.meta
  12.0 0.0 collective-permute-done.1
  12.0 0.0 collective-permute-done
  12.0 0.0 collective-permute-done.2
  12.0 1.3 pad_add_fusion.1.prints
  13.3 3.5 %shard_map.118 = (f32[4,8,8,128]{3,2,1,0:T(8,128)}, f32[4,8,8,128]{3,2,1,0:T(8,128)}, f32[4,8,8,128]{3,2,1,0:T(8,128)}, f32[4,8,8,128]{3,2,1,0:T(8,128)}) custom-call(s32[4]{0:T(128)} %pad_add_fusion.2.meta, s32[4,16]{1,0:T(4,128)} %pad_add_fusion.1.prints, s32[64]{0:T(128)} %owner_map.7, f32[8,8,8,128]{3,2,1,0:T(8,128)} %velocity.1, f32[8,8,8,128]{3,2,1,0:T(8,128)} %density.1), custom_call_target="tpu_custom_call" | custom-call | tf_op jit(solution)/shard_map/pallas_call | solution.py:507
  16.8 0.9 collective-permute-start.4
  17.7 3.5 %collective-permute-start.5 = (f32[4,8,8,128]{3,2,1,0:T(8,128)}, f32[4,8,8,128]{3,2,1,0:T(8,128)S(1)}, u32[]{:S(2)}, u32[]{:S(2)}) collective-permute-start(f32[4,8,8,128]{3,2,1,0:T(8,128)} %get-tuple-element.17), channel_id=1, source_target_pairs={{0,8},{4,12},{8,0},{12,4},{1,9},{5,13},{9,1},{13,5},{2,10},{6,14},... | collective-permute-start | bytes 393224 | tf_op jit(solution)/shard_map/ppermute | solution.py:48
  21.2 0.0 collective-permute-start.6
  21.2 0.1 add_convert_fusion
  21.3 2.2 %collective-permute-done.4.refs_1_ = f32[4,8,8,128]{3,2,1,0:T(8,128)S(1)} collective-permute-done((f32[4,8,8,128]{3,2,1,0:T(8,128)}, f32[4,8,8,128]{3,2,1,0:T(8,128)S(1)}, u32[]{:S(2)}, u32[]{:S(2)}) %collective-permute-start.4) | collective-permute-done | bytes 131104 | tf_op jit(solution)/shard_map/ppermute | solution.py:48
  23.5 0.0 copy-start.5
  23.5 7.4 %collective-permute-done.5.refs_2_ = f32[4,8,8,128]{3,2,1,0:T(8,128)S(1)} collective-permute-done((f32[4,8,8,128]{3,2,1,0:T(8,128)}, f32[4,8,8,128]{3,2,1,0:T(8,128)S(1)}, u32[]{:S(2)}, u32[]{:S(2)}) %collective-permute-start.5) | collective-permute-done | bytes 131104 | tf_op jit(solution)/shard_map/ppermute | solution.py:48
  31.0 0.0 copy-start.6
  31.0 0.0 collective-permute-done.6.refs_3_
  31.0 0.0 copy-start.7
  31.0 0.0 copy-done.5
  31.0 0.6 copy-done.6
  31.6 0.1 copy-done.7
  31.7 3.5 %shard_map.119.refs_2_ = f32[32,32,128]{2,1,0:T(8,128)} custom-call(s32[4]{0:T(128)} %pad_add_fusion.2.meta, s32[4,16]{1,0:T(4,128)} %pad_add_fusion.1.prints, s32[64]{0:T(128)} %owner_map.7, f32[4,8,8,128]{3,2,1,0:T(8,128)} %get-tuple-element.15.refs_0_, f32[4,8,8,128]{3,2,1,0:T(8,128)} %copy-done.5, f32[4,8,8,128]{3,2,1,0:T(8,128)} %copy-done.6, ...), custom_call_target="tpu_custom_call" | custom-call | tf_op jit(solution)/shard_map/pallas_call | solution.py:514
  35.2 0.0 copy-start
  35.2 1.5 collective-permute-start.7
  36.7 6.8 %fusion.10.inject_a = f32[8,2048,128]{2,1,0:T(8,128)} fusion(pred[2048,512]{1,0:T(32,128)(4,1)S(1)} %iota_compare_fusion, f32[1024,128]{0,1:T(8,128)S(1)} %add_convert_fusion, f32[16,1024]{1,0:T(8,128)S(1)} %pad_maximum_fusion), kind=kOutput, calls=%fused_computation.10 | convolution fusion | flops 4301258752 | bytes 10027008 | tf_op jit(solution)/shard_map/rp,kpz->krz/dot_general | solution.py:460
  43.5 0.0 copy-done
  43.5 0.0 collective-permute-start.8
  43.5 9.2 %collective-permute-done.7.refs_3_ = f32[32,32,128]{2,1,0:T(8,128)S(1)} collective-permute-done((f32[32,32,128]{2,1,0:T(8,128)}, f32[32,32,128]{2,1,0:T(8,128)S(1)}, u32[]{:S(2)}, u32[]{:S(2)}) %collective-permute-start.7) | collective-permute-done | bytes 524320 | tf_op jit(solution)/shard_map/ppermute | solution.py:48
  52.6 0.0 copy-start.3
  52.6 0.0 collective-permute-start.9
  52.6 6.4 %fusion.7.inject_b = f32[8,1920,128]{2,1,0:T(8,128)} fusion(pred[2048,512]{1,0:T(32,128)(4,1)S(1)} %iota_compare_fusion, f32[1024,128]{0,1:T(8,128)S(1)} %add_convert_fusion, f32[16,1024]{1,0:T(8,128)S(1)} %pad_maximum_fusion), kind=kOutput, calls=%fused_computation.9 | convolution fusion | flops 4032692224 | bytes 9502720 | tf_op jit(solution)/shard_map/rp,kpz->krz/dot_general | solution.py:460
  59.0 0.0 copy-done.3
  59.0 0.0 collective-permute-done.10.refs_7_
  59.0 0.0 copy-start.2
  59.0 0.0 collective-permute-done.8.refs_4_
  59.0 0.0 copy-start.4
  59.0 0.0 collective-permute-done.3.refs_1_
  59.1 0.8 copy-done.4
  59.9 0.0 copy-start.1
  59.9 0.0 collective-permute-done.9.refs_5_
  59.9 0.1 copy-done.2
  60.0 1.0 copy-done.1
  61.0 116.8 %shard_map.120 = (f32[16,4,4,4,8,128]{5,4,3,2,1,0:T(8,128)}, f32[16,4,4,4,8,128]{5,4,3,2,1,0:T(8,128)}) custom-call(s32[4]{0:T(128)} %pad_add_fusion.2.meta, bf16[512,256]{1,0:T(8,128)(2,1)} %constant.100.clone.zmat, f32[8,2048,128]{2,1,0:T(8,128)} %fusion.10.inject_a, f32[8,1920,128]{2,1,0:T(8,128)} %fusion.7.inject_b, f32[2,32,32,128]{3,2,1,0:T(8,128)} %bitcast.31, ...), custom_call_target="tpu_custom_call" | custom-call | tf_op jit(solution)/shard_map/pallas_call | solution.py:537
  177.8 0.1 collective-permute-start.11
  177.8 7.5 %collective-permute-done.11.got = f32[16,4,4,4,8,128]{5,4,3,2,1,0:T(8,128)} collective-permute-done((f32[16,4,4,4,8,128]{5,4,3,2,1,0:T(8,128)}, f32[16,4,4,4,8,128]{5,4,3,2,1,0:T(8,128)}, u32[]{:S(2)}, u32[]{:S(2)}) %collective-permute-start.11) | collective-permute-done | bytes 4194336 | tf_op jit(solution)/shard_map/ppermute | solution.py:48
  185.3 6.6 %shard_map.121 = (f32[4,4,8,128]{3,2,1,0:T(8,128)}, f32[4,4,8,128]{3,2,1,0:T(8,128)}, f32[4,4,8,128]{3,2,1,0:T(8,128)}, f32[4,4,8,128]{3,2,1,0:T(8,128)}) custom-call(s32[4]{0:T(128)} %pad_add_fusion.2.meta, s32[4,16]{1,0:T(4,128)} %pad_add_fusion.1.prints, s32[64]{0:T(128)} %owner_map.7, f32[16,4,4,4,8,128]{5,4,3,2,1,0:T(8,128)} %get-tuple-element.19.keep, ...), custom_call_target="tpu_custom_call" | custom-call | tf_op jit(solution)/shard_map/pallas_call | solution.py:557
  191.9 0.6 collective-permute-start.12
  192.5 1.1 collective-permute-start.13
  193.6 2.7 %collective-permute-start.14 = (f32[4,4,8,128]{3,2,1,0:T(8,128)}, f32[4,4,8,128]{3,2,1,0:T(8,128)S(1)}, u32[]{:S(2)}, u32[]{:S(2)}) collective-permute-start(f32[4,4,8,128]{3,2,1,0:T(8,128)} %get-tuple-element.24), channel_id=1, source_target_pairs={{0,12},{4,8},{8,4},{12,0},{1,13},{5,9},{9,5},{13,1},{2,14},{6,10},... | collective-permute-start | bytes 196616 | tf_op jit(solution)/shard_map/ppermute | solution.py:48
  196.3 0.8 collective-permute-done.12.refs_1_
  197.1 0.0 copy-start.8
  197.1 4.1 %collective-permute-done.13.refs_2_ = f32[4,4,8,128]{3,2,1,0:T(8,128)S(1)} collective-permute-done((f32[4,4,8,128]{3,2,1,0:T(8,128)}, f32[4,4,8,128]{3,2,1,0:T(8,128)S(1)}, u32[]{:S(2)}, u32[]{:S(2)}) %collective-permute-start.13) | collective-permute-done | bytes 65568 | tf_op jit(solution)/shard_map/ppermute | solution.py:48
  201.2 0.0 collective-permute-done.14.refs_3_
  201.2 0.0 copy-done.8
  201.2 0.6 copy-done.9
  201.8 0.0 copy-done.10
  201.9 3.3 %shard_map.122 = f32[8,4,8,128]{3,2,1,0:T(8,128)} custom-call(s32[4]{0:T(128)} %pad_add_fusion.2.meta, s32[4,16]{1,0:T(4,128)} %pad_add_fusion.1.prints, s32[64]{0:T(128)} %owner_map.7, f32[4,4,8,128]{3,2,1,0:T(8,128)} %get-tuple-element.21.refs_0_, f32[4,4,8,128]{3,2,1,0:T(8,128)} %copy-done.8, f32[4,4,8,128]{3,2,1,0:T(8,128)} %copy-done.9, ...), custom_call_target="tpu_custom_call" | custom-call | tf_op jit(solution)/shard_map/pallas_call | solution.py:568
  (5 shorter events, 0.1 us)
Async XLA Ops:
  0.0 12.0 %collective-permute-start.1 = (s32[1,16]{1,0:T(1,128)}, s32[1,16]{1,0:T(1,128)S(1)}, u32[]{:S(2)}, u32[]{:S(2)}) collective-permute-start(s32[1,16]{1,0:T(1,128)} %param.15), channel_id=1, source_target_pairs={{0,8},{4,12},{8,0},{12,4},{1,9},{5,13},{9,1},{13,5},{2,10},{6,14},... | collective-permute-start | bytes 200 | tf_op jit(solution)/shard_map/ppermute | solution.py:48
  4.0 8.0 %collective-permute-start = (s32[1,16]{1,0:T(1,128)}, s32[1,16]{1,0:T(1,128)S(1)}, u32[]{:S(2)}, u32[]{:S(2)}) collective-permute-start(s32[1,16]{1,0:T(1,128)} %param.15), channel_id=1, source_target_pairs={{0,4},{4,0},{8,12},{12,8},{1,5},{5,1},{9,13},{13,9},{2,6},{6,2},{1... | collective-permute-start | bytes 200 | tf_op jit(solution)/shard_map/ppermute | solution.py:48
  5.6 6.4 %collective-permute-start.2 = (s32[1,16]{1,0:T(1,128)}, s32[1,16]{1,0:T(1,128)S(1)}, u32[]{:S(2)}, u32[]{:S(2)}) collective-permute-start(s32[1,16]{1,0:T(1,128)} %param.15), channel_id=1, source_target_pairs={{0,12},{4,8},{8,4},{12,0},{1,13},{5,9},{9,5},{13,1},{2,14},{6,10},... | collective-permute-start | bytes 200 | tf_op jit(solution)/shard_map/ppermute | solution.py:48
  5.6 53.4 %collective-permute-start.10 = (f32[16,2,32,128]{3,2,1,0:T(8,128)}, f32[16,2,32,128]{3,2,1,0:T(8,128)S(1)}, u32[]{:S(2)}, u32[]{:S(2)}) collective-permute-start(f32[16,2,32,128]{3,2,1,0:T(8,128)} %bitcast.32), channel_id=1, source_target_pairs={{0,2},{2,0},{1,3},{3,1},{4,6},{6,4},{5,7},{7,5},{8,10},{10,8},{9,1... | collective-permute-start | bytes 1572872 | tf_op jit(solution)/shard_map/ppermute | solution.py:48
  7.3 51.7 %collective-permute-start.3 = (f32[2,32,32,128]{3,2,1,0:T(8,128)}, f32[2,32,32,128]{3,2,1,0:T(8,128)S(1)}, u32[]{:S(2)}, u32[]{:S(2)}) collective-permute-start(f32[2,32,32,128]{3,2,1,0:T(8,128)} %bitcast.30), channel_id=1, source_target_pairs={{0,2},{2,0},{1,3},{3,1},{4,6},{6,4},{5,7},{7,5},{8,10},{10,8},{9,1... | collective-permute-start | bytes 3145736 | tf_op jit(solution)/shard_map/ppermute | solution.py:48
  16.8 6.7 %collective-permute-start.4 = (f32[4,8,8,128]{3,2,1,0:T(8,128)}, f32[4,8,8,128]{3,2,1,0:T(8,128)S(1)}, u32[]{:S(2)}, u32[]{:S(2)}) collective-permute-start(f32[4,8,8,128]{3,2,1,0:T(8,128)} %get-tuple-element.16), channel_id=1, source_target_pairs={{0,4},{4,0},{8,12},{12,8},{1,5},{5,1},{9,13},{13,9},{2,6},{6,2},{1... | collective-permute-start | bytes 393224 | tf_op jit(solution)/shard_map/ppermute | solution.py:48
  17.7 13.2 %collective-permute-start.5 = (f32[4,8,8,128]{3,2,1,0:T(8,128)}, f32[4,8,8,128]{3,2,1,0:T(8,128)S(1)}, u32[]{:S(2)}, u32[]{:S(2)}) collective-permute-start(f32[4,8,8,128]{3,2,1,0:T(8,128)} %get-tuple-element.17), channel_id=1, source_target_pairs={{0,8},{4,12},{8,0},{12,4},{1,9},{5,13},{9,1},{13,5},{2,10},{6,14},... | collective-permute-start | bytes 393224 | tf_op jit(solution)/shard_map/ppermute | solution.py:48
  21.2 9.8 %collective-permute-start.6 = (f32[4,8,8,128]{3,2,1,0:T(8,128)}, f32[4,8,8,128]{3,2,1,0:T(8,128)S(1)}, u32[]{:S(2)}, u32[]{:S(2)}) collective-permute-start(f32[4,8,8,128]{3,2,1,0:T(8,128)} %get-tuple-element.18), channel_id=1, source_target_pairs={{0,12},{4,8},{8,4},{12,0},{1,13},{5,9},{9,5},{13,1},{2,14},{6,10},... | collective-permute-start | bytes 393224 | tf_op jit(solution)/shard_map/ppermute | solution.py:48
  23.5 7.5 %copy-start.5 = (f32[4,8,8,128]{3,2,1,0:T(8,128)}, f32[4,8,8,128]{3,2,1,0:T(8,128)S(1)}, u32[]{:S(2)}) copy-start(f32[4,8,8,128]{3,2,1,0:T(8,128)S(1)} %collective-permute-done.4.refs_1_) | copy-start | bytes 393220
  31.0 0.6 copy-start.6
  31.0 0.7 copy-start.7
  35.2 8.3 %copy-start = (f32[32,32,128]{2,1,0:T(8,128)S(1)}, f32[32,32,128]{2,1,0:T(8,128)}, u32[]{:S(2)}) copy-start(f32[32,32,128]{2,1,0:T(8,128)} %shard_map.119.refs_2_) | copy-start | bytes 1572868
  35.2 17.5 %collective-permute-start.7 = (f32[32,32,128]{2,1,0:T(8,128)}, f32[32,32,128]{2,1,0:T(8,128)S(1)}, u32[]{:S(2)}, u32[]{:S(2)}) collective-permute-start(f32[32,32,128]{2,1,0:T(8,128)} %shard_map.119.refs_2_), channel_id=1, source_target_pairs={{0,2},{2,0},{1,3},{3,1},{4,6},{6,4},{5,7},{7,5},{8,10},{10,8},{9,1... | collective-permute-start | bytes 1572872 | tf_op jit(solution)/shard_map/ppermute | solution.py:48
  43.5 15.6 %collective-permute-start.8 = (f32[32,32,128]{2,1,0:T(8,128)S(1)}, f32[32,32,128]{2,1,0:T(8,128)S(1)}, u32[]{:S(2)}, u32[]{:S(2)}) collective-permute-start(f32[32,32,128]{2,1,0:T(8,128)S(1)} %copy-done), channel_id=1, source_target_pairs={{0,1},{1,0},{2,3},{3,2},{4,5},{5,4},{6,7},{7,6},{8,9},{9,8},{10,11... | collective-permute-start | bytes 1572872 | tf_op jit(solution)/shard_map/ppermute | solution.py:48
  52.6 6.4 %copy-start.3 = (f32[32,32,128]{2,1,0:T(8,128)}, f32[32,32,128]{2,1,0:T(8,128)S(1)}, u32[]{:S(2)}) copy-start(f32[32,32,128]{2,1,0:T(8,128)S(1)} %collective-permute-done.7.refs_3_) | copy-start | bytes 1572868
  52.6 7.2 %collective-permute-start.9 = (f32[32,32,128]{2,1,0:T(8,128)S(1)}, f32[32,32,128]{2,1,0:T(8,128)}, u32[]{:S(2)}, u32[]{:S(2)}) collective-permute-start(f32[32,32,128]{2,1,0:T(8,128)S(1)} %collective-permute-done.7.refs_3_), channel_id=1, source_target_pairs={{0,1},{1,0},{2,3},{3,2},{4,5},{5,4},{6,7},{7,6},{8,9},{9,8},{10,11... | collective-permute-start | bytes 1572872 | tf_op jit(solution)/shard_map/ppermute | solution.py:48
  59.0 1.0 copy-start.2
  59.0 0.9 copy-start.4
  59.9 1.1 copy-start.1
  177.8 7.6 %collective-permute-start.11 = (f32[16,4,4,4,8,128]{5,4,3,2,1,0:T(8,128)}, f32[16,4,4,4,8,128]{5,4,3,2,1,0:T(8,128)}, u32[]{:S(2)}, u32[]{:S(2)}) collective-permute-start(f32[16,4,4,4,8,128]{5,4,3,2,1,0:T(8,128)} %get-tuple-element.20), channel_id=1, source_target_pairs={{0,1},{1,0},{2,3},{3,2},{4,5},{5,4},{6,7},{7,6},{8,9},{9,8},{10,11... | collective-permute-start | bytes 12582920 | tf_op jit(solution)/shard_map/ppermute | solution.py:48
  191.9 5.2 %collective-permute-start.12 = (f32[4,4,8,128]{3,2,1,0:T(8,128)}, f32[4,4,8,128]{3,2,1,0:T(8,128)S(1)}, u32[]{:S(2)}, u32[]{:S(2)}) collective-permute-start(f32[4,4,8,128]{3,2,1,0:T(8,128)} %get-tuple-element.22), channel_id=1, source_target_pairs={{0,4},{4,0},{8,12},{12,8},{1,5},{5,1},{9,13},{13,9},{2,6},{6,2},{1... | collective-permute-start | bytes 196616 | tf_op jit(solution)/shard_map/ppermute | solution.py:48
  192.5 8.7 %collective-permute-start.13 = (f32[4,4,8,128]{3,2,1,0:T(8,128)}, f32[4,4,8,128]{3,2,1,0:T(8,128)S(1)}, u32[]{:S(2)}, u32[]{:S(2)}) collective-permute-start(f32[4,4,8,128]{3,2,1,0:T(8,128)} %get-tuple-element.23), channel_id=1, source_target_pairs={{0,8},{4,12},{8,0},{12,4},{1,9},{5,13},{9,1},{13,5},{2,10},{6,14},... | collective-permute-start | bytes 196616 | tf_op jit(solution)/shard_map/ppermute | solution.py:48
  193.6 7.6 %collective-permute-start.14 = (f32[4,4,8,128]{3,2,1,0:T(8,128)}, f32[4,4,8,128]{3,2,1,0:T(8,128)S(1)}, u32[]{:S(2)}, u32[]{:S(2)}) collective-permute-start(f32[4,4,8,128]{3,2,1,0:T(8,128)} %get-tuple-element.24), channel_id=1, source_target_pairs={{0,12},{4,8},{8,4},{12,0},{1,13},{5,9},{9,5},{13,1},{2,14},{6,10},... | collective-permute-start | bytes 196616 | tf_op jit(solution)/shard_map/ppermute | solution.py:48
  197.1 4.1 %copy-start.8 = (f32[4,4,8,128]{3,2,1,0:T(8,128)}, f32[4,4,8,128]{3,2,1,0:T(8,128)S(1)}, u32[]{:S(2)}) copy-start(f32[4,4,8,128]{3,2,1,0:T(8,128)S(1)} %collective-permute-done.12.refs_1_) | copy-start | bytes 196612
  201.2 0.6 copy-start.9
  201.2 0.6 copy-start.10

commit v2 on v1

--- a/solution.py
+++ b/solution.py
@@ -19,6 +19,11 @@
 first_ratio = tuple(w / FIRST for w in first_weights)
 second_ratio = tuple(w / SECOND for w in second_weights[1:])
 
+SECOND_UNIT = 8064.0
+FIRST_UNIT = 672.0
+second_whole = (8064.0, -1008.0, 128.0, -9.0)
+first_whole = (672.0, -168.0, 32.0, -3.0)
+
 VMEM_LIMIT = 60 * 1024 * 1024
 
 smem = pl.BlockSpec(memory_space=pltpu.SMEM)
@@ -32,15 +37,13 @@
     for r in range(1, REACH + 1):
         for z in range(size):
             if z + r < size:
-                second[z + r, z] = second_ratio[r - 1]
-                first[z + r, z] = first_ratio[r - 1]
+                second[z + r, z] = second_whole[r - 1]
+                first[z + r, z] = first_whole[r - 1]
             if z - r >= 0:
-                second[z - r, z] = second_ratio[r - 1]
-                first[z - r, z] = -first_ratio[r - 1]
-    whole = np.concatenate([second, first], axis=1).astype(np.float32)
-    high = whole.astype(jnp.bfloat16)
-    low = (whole - high.astype(np.float32)).astype(jnp.bfloat16)
-    return np.concatenate([high, high, low, low], axis=0)
+                second[z - r, z] = second_whole[r - 1]
+                first[z - r, z] = -first_whole[r - 1]
+    whole = np.concatenate([second, first], axis=1)
+    return np.concatenate([whole, whole], axis=0).astype(jnp.bfloat16)
 
 
 def xor_swap(block, axis, bits):
@@ -107,69 +110,71 @@
         lax.fori_loop(0, slots, place, jnp.int32(0))
 
 
-def along_x(load, t, i):
-    sums, slopes = [], []
-    for r in range(1, REACH + 1):
-        ahead, behind = load(i + r, t), load(i - r, t)
-        sums.append(ahead + behind)
-        slopes.append(ahead - behind)
-    return sums, slopes
-
-
-def along_y(rows, ups, downs, t):
-    sums, slopes = [], []
-    for r in range(1, REACH + 1):
-        ahead = rows[t + r] if t + r < 4 else ups[t + r - 4]
-        behind = rows[t - r] if t - r >= 0 else downs[t - r + 4]
-        sums.append(ahead + behind)
-        slopes.append(ahead - behind)
-    return sums, slopes
-
-
-def weigh(parts, ratios):
-    total = parts[0]
-    for part, ratio in zip(parts[1:], ratios[1:]):
-        total = total + ratio * part
-    return total
+def each(f, *lists):
+    return [f(*items) for items in zip(*lists)]
+
+
+def add(a, b):
+    return each(lambda p, q: p + q, a, b)
+
+
+def sub(a, b):
+    return each(lambda p, q: p - q, a, b)
+
+
+def mul(a, b):
+    return each(lambda p, q: p * q, a, b)
+
+
+def scaled(factor, a):
+    return [factor * p for p in a]
 
 
 def shifted_rows(rows, sublane):
     ups = [jnp.where(sublane == 7, 0.0, pltpu.roll(row, 7, 0)) for row in rows]
     downs = [jnp.where(sublane == 0, 0.0, pltpu.roll(row, 1, 0)) for row in rows]
-    return ups, downs
+    return downs + rows + ups
 
 
 def split_rows(value):
     high = value.astype(jnp.bfloat16)
     low = (value - high.astype(jnp.float32)).astype(jnp.bfloat16)
-    both = jnp.concatenate([high, low], axis=1)
-    return jnp.concatenate([both, both], axis=1)
+    return jnp.concatenate([high, low], axis=1)
 
 
 def steps_kernel(count_slabs, own_lo, flipped, inject_lo, meta, zmat, inject_a, inject_b, *refs):
     states = refs[:count_slabs]
     mine = refs[count_slabs : 2 * count_slabs]
     theirs = refs[2 * count_slabs : 3 * count_slabs]
-    rims = refs[3 * count_slabs : 4 * count_slabs]
-    keep, send = refs[4 * count_slabs : 4 * count_slabs + 2]
-    field, logs, square, centre, gx, gy, gz, pulses, sems = refs[4 * count_slabs + 2 :]
+    rims = refs[3 * count_slabs]
+    keep, send = refs[3 * count_slabs + 1 : 3 * count_slabs + 3]
+    field, logs, square, centre, gx, gy, gz, pulses, zbuf, record, sems, out_sems = refs[
+        3 * count_slabs + 3 :
+    ]
     thick = states[0].shape[1]
-    steps = rims[0].shape[0]
+    steps = rims.shape[0]
     lanes = states[0].shape[3]
     window = thick * count_slabs
     own_hi = own_lo + thick
+    cols = thick // 8
     column = meta[1]
     is_source = meta[2] == 0
     limit = meta[3]
+    half_of = meta[2]
     sublane = lax.broadcasted_iota(jnp.int32, (8, lanes), 0)
-    half_of = meta[2]
     reversed_x = flipped & (column == 1)
+    turn = reversed_x.astype(jnp.int32)
 
     def global_x(w):
         if flipped:
             return jnp.where(column == 1, window - 1 - w, w)
         return w + column * thick - own_lo
 
+    def rim_x(w):
+        if flipped:
+            return jnp.where(column == 1, window - 1 - w, w)
+        return w
+
     def active(w):
         x = global_x(w)
         return (x >= 0) & (x < limit)
@@ -177,8 +182,8 @@
     def local_x(v):
         return jnp.where(reversed_x, thick - 1 - v, v)
 
-    def z_parts(load, width):
-        rows = jnp.concatenate([load(i, t) for i in range(width) for t in range(4)], axis=0)
+    def z_parts(load):
+        rows = jnp.concatenate([load(i, t) for i in range(4) for t in range(4)], axis=0)
         return jnp.dot(split_rows(rows), zmat[...], preferred_element_type=jnp.float32)
 
     def lo_of(k):
@@ -217,6 +222,16 @@
         @pl.when(k >= early)
         def _():
             copy_b(k, slot).wait()
+
+    def out_copies(k, slot):
+        return [
+            pltpu.make_async_copy(
+                record.at[slot, pl.ds(0, cols)], keep.at[k], out_sems.at[slot, 0]
+            ),
+            pltpu.make_async_copy(
+                record.at[slot, pl.ds(cols, cols)], send.at[k], out_sems.at[slot, 1]
+            ),
+        ]
 
     copy_a(0, 0).start()
 
@@ -249,22 +264,34 @@
 
         lax.fori_loop(0, thick, fill, 0)
 
+    def slopes(load, i, rows):
+        dx = dy = None
+        for r in range(1, REACH + 1):
+            px = sub([load(i + r, t) for t in range(4)], [load(i - r, t) for t in range(4)])
+            py = sub(rows[4 + r : 8 + r], rows[4 - r : 8 - r])
+            if r == 1:
+                dx, dy = px, py
+            else:
+                dx = add(dx, scaled(first_ratio[r - 1], px))
+                dy = add(dy, scaled(first_ratio[r - 1], py))
+        return dx, dy
+
     def bend(b, carry):
         w = b * 4
 
         def load(i, t):
             return logs[REACH + w + i, t]
 
-        zs = z_parts(load, 4)
+        zs = z_parts(load)
         for i in range(4):
-            rows = [load(i, t) for t in range(4)]
-            ups, downs = shifted_rows(rows, sublane)
+            rows = shifted_rows([load(i, t) for t in range(4)], sublane)
+            dx, dy = slopes(load, i, rows)
             for t in range(4):
                 scale = (FIRST * FIRST / SECOND) * square[w + i, t]
                 at = (i * 4 + t) * 8
-                gx[w + i, t] = scale * weigh(along_x(load, t, i)[1], first_ratio)
-                gy[w + i, t] = scale * weigh(along_y(rows, ups, downs, t)[1], first_ratio)
-                gz[w + i, t] = scale * zs[at : at + 8, lanes : 2 * lanes]
+                gx[w + i, t] = scale * dx[t]
+                gy[w + i, t] = scale * dy[t]
+                gz[w + i, t] = (scale * (1.0 / (FIRST_UNIT * FIRST_UNIT))) * zs[at : at + 8, lanes:]
         return carry
 
     lax.fori_loop(0, window // 4, bend, 0)
@@ -279,83 +306,92 @@
         wait_copy(k, slot)
         start_copy(k + 1, 1 - slot)
 
+        @pl.when(k >= 2)
+        def _():
+            for copy in out_copies(k - 2, slot):
+                copy.wait()
+
+        first = lo_of(k) // 4
+        last = hi_of(k) // 4
+        zbuf[lax.rem(first, 2)] = z_parts(lambda i, t: field[new, REACH + first * 4 + i, t])
+
         def block(b, carry):
             w = b * 4
             on = active(w)
+            after = jnp.minimum(b + 1, window // 4 - 1) * 4
+            own = b - own_lo // 4
+            half = lax.rem(own + turn, 2)
+            is_own = (own >= 0) & (own < thick // 4)
+            to = jnp.where(is_own, jnp.where(half == half_of, 0, cols) + own // 2, 2 * cols)
+            zslot = lax.rem(b, 2)
 
             @pl.when(on)
             def _():
                 def load(i, t):
                     return field[new, REACH + w + i, t]
 
-                zs = z_parts(load, 4)
+                zs = z_parts(lambda i, t: field[new, REACH + after + i, t])
                 for i in range(4):
-                    rows = [load(i, t) for t in range(4)]
-                    ups, downs = shifted_rows(rows, sublane)
+                    mid = [load(i, t) for t in range(4)]
+                    rows = shifted_rows(mid, sublane)
+                    lap = dx = dy = None
+                    for r in range(1, REACH + 1):
+                        ax = [load(i + r, t) for t in range(4)]
+                        bx = [load(i - r, t) for t in range(4)]
+                        ay = rows[4 + r : 8 + r]
+                        by = rows[4 - r : 8 - r]
+                        px = sub(ax, bx)
+                        py = sub(ay, by)
+                        total = add(add(ax, bx), add(ay, by))
+                        if r == 1:
+                            lap, dx, dy = total, px, py
+                        else:
+                            lap = add(lap, scaled(second_ratio[r - 1], total))
+                            dx = add(dx, scaled(first_ratio[r - 1], px))
+                            dy = add(dy, scaled(first_ratio[r - 1], py))
+                    at = [(i * 4 + t) * 8 for t in range(4)]
+                    z2 = [zbuf[zslot, a : a + 8, 0:lanes] for a in at]
+                    z1 = [zbuf[zslot, a : a + 8, lanes:] for a in at]
+                    lap = add(lap, scaled(1.0 / SECOND_UNIT, z2))
+                    value = sub(
+                        mul([centre[w + i, t] for t in range(4)], mid),
+                        [field[old, REACH + w + i, t] for t in range(4)],
+                    )
+                    row = pl.multiple_of(w * 32 + i * 32, 32)
+                    value = add(value, [pulses[slot, pl.ds(row + t * 8, 8), :] for t in range(4)])
+                    value = add(value, mul([square[w + i, t] for t in range(4)], lap))
+                    drift = mul([gx[w + i, t] for t in range(4)], dx)
+                    drift = add(drift, mul([gy[w + i, t] for t in range(4)], dy))
+                    drift = add(drift, mul([gz[w + i, t] for t in range(4)], z1))
+                    value = sub(value, drift)
+                    x = rim_x(w + i)
+                    low = jnp.broadcast_to(rims[k, 0, pl.ds(x, 1), :], (8, lanes))
+                    high = jnp.broadcast_to(rims[k, 1, pl.ds(x, 1), :], (8, lanes))
+                    value[0] = jnp.where(rim_low, low, value[0])
+                    value[3] = jnp.where(rim_high, high, value[3])
                     for t in range(4):
-                        sx, dx = along_x(load, t, i)
-                        sy, dy = along_y(rows, ups, downs, t)
-                        at = (i * 4 + t) * 8
-                        laplace = weigh([p + q for p, q in zip(sx, sy)], second_ratio)
-                        laplace = laplace + zs[at : at + 8, 0:lanes]
-                        value = centre[w + i, t] * rows[t] - field[old, REACH + w + i, t]
-                        value = value + square[w + i, t] * laplace
-                        value = value - gx[w + i, t] * weigh(dx, first_ratio)
-                        value = value - gy[w + i, t] * weigh(dy, first_ratio)
-                        value = value - gz[w + i, t] * zs[at : at + 8, lanes : 2 * lanes]
-                        row = pl.multiple_of(w * 32 + at, 8)
-                        value = value + pulses[slot, pl.ds(row, 8), :]
-                        field[old, REACH + w + i, t] = value
+                        field[old, REACH + w + i, t] = value[t]
+                        record[slot, to, i, t] = value[t]
+                zbuf[1 - zslot] = zs
 
             @pl.when(jnp.logical_not(on))
             def _():
-                field[old, pl.ds(REACH + w, 4)] = jnp.zeros((4, 4, 8, lanes), jnp.float32)
+                nothing = jnp.zeros((4, 4, 8, lanes), jnp.float32)
+                field[old, pl.ds(REACH + w, 4)] = nothing
+                record[slot, to] = nothing
+                zbuf[1 - zslot] = z_parts(lambda i, t: field[new, REACH + after + i, t])
 
             return carry
 
-        lax.fori_loop(lo_of(k) // 4, hi_of(k) // 4, block, 0)
-
-        @pl.when(is_source)
-        def _():
-            for s in range(count_slabs):
-                first = jnp.maximum(lo_of(k) - s * thick, 0)
-                last = jnp.minimum(hi_of(k) - s * thick, thick)
-
-                def rim(v, carry, s=s):
-                    w = s * thick + v
-                    x = local_x(v)
-                    on = active(w)
-                    low = jnp.broadcast_to(rims[s][k, 0, pl.ds(x, 1), :], (8, lanes))
-                    high = jnp.broadcast_to(rims[s][k, 1, pl.ds(x, 1), :], (8, lanes))
-                    field[old, REACH + w, 0] = jnp.where(
-                        rim_low & on, low, field[old, REACH + w, 0]
-                    )
-                    field[old, REACH + w, 3] = jnp.where(
-                        rim_high & on, high, field[old, REACH + w, 3]
-                    )
-                    return carry
-
-                lax.fori_loop(first, last, rim, 0)
-
-        def record(b, carry):
-            w = REACH + own_lo + b * 4
-            block_half = lax.rem(jnp.where(reversed_x, b + 1, b), 2)
-            values = field[old, pl.ds(w, 4)]
-
-            @pl.when(block_half == half_of)
-            def _():
-                keep[k, b // 2] = values
-
-            @pl.when(block_half != half_of)
-            def _():
-                send[k, b // 2] = values
-
-            return carry
-
-        lax.fori_loop(0, thick // 4, record, 0)
+        lax.fori_loop(first, last, block, 0)
+        for copy in out_copies(k, slot):
+            copy.start()
         return carry
 
     lax.fori_loop(0, steps, one_step, 0)
+    for k in (steps - 2, steps - 1):
+        for copy in out_copies(k, k % 2):
+            copy.wait()
 
 
 def image_kernel(owners, columns, slots, stored, flipped, meta, prints, owner_map, keep, got, *refs):
@@ -426,6 +462,38 @@
         compiler_params=pltpu.CompilerParams(vmem_limit_bytes=VMEM_LIMIT),
         cost_estimate=cost,
     )
+
+
+def run_steps(
+    count, own_lo, flipped, inject_lo, steps, meta, inject_a, inject_b, state_slabs, mine, theirs, rims
+):
+    f32 = jnp.float32
+    thick, height, lanes = mine[0].shape
+    cols = thick // 8
+    window = count * thick
+    kept = jax.ShapeDtypeStruct((steps, cols, 4, 4, height // 4, lanes), f32)
+    grid = (window, 4, height // 4, lanes)
+    padded = (window + 2 * REACH, 4, height // 4, lanes)
+    return call(
+        functools.partial(steps_kernel, count, own_lo, flipped, inject_lo),
+        [kept, kept],
+        [smem, vmem, anywhere, anywhere] + [vmem] * (3 * count + 1),
+        [anywhere, anywhere],
+        [
+            pltpu.VMEM((2,) + padded, f32),
+            pltpu.VMEM(padded, f32),
+            pltpu.VMEM(grid, f32),
+            pltpu.VMEM(grid, f32),
+            pltpu.VMEM(grid, f32),
+            pltpu.VMEM(grid, f32),
+            pltpu.VMEM(grid, f32),
+            pltpu.VMEM((2, window * height, lanes), f32),
+            pltpu.VMEM((2, 128, 2 * lanes), f32),
+            pltpu.VMEM((2, 2 * cols + 1, 4, 4, height // 4, lanes), f32),
+            pltpu.SemaphoreType.DMA((2,)),
+            pltpu.SemaphoreType.DMA((2, 2)),
+        ],
+    )(meta, z_matrix(lanes), inject_a, inject_b, *state_slabs, *mine, *theirs, rims)
 
 
 def injection(window, column, own_lo, flipped, thick, height, lanes, is_source,
@@ -520,6 +588,14 @@
 
     state_slabs = slabs_of(states[0, 0])
     rim_slabs = slabs_of(stored_rims[0])
+    if flipped:
+        rims = jnp.where(
+            column == 1,
+            jnp.concatenate(rim_slabs[::-1], axis=2),
+            jnp.concatenate(rim_slabs, axis=2),
+        )
+    else:
+        rims = jnp.concatenate(rim_slabs, axis=2)
     mine = slabs_of(table)
     theirs = [xor_swap(slab, "pair", 1) for slab in mine]
 
@@ -531,26 +607,9 @@
         source_cell, receiver_cells[0], wavelet[0], traces[0],
     )
 
-    kept = jax.ShapeDtypeStruct((steps, bricks_x, half_x, 4, height // 4, lanes), f32)
-    grid = (window, 4, height // 4, lanes)
-    padded = (window + 2 * REACH, 4, height // 4, lanes)
-    keep, send = call(
-        functools.partial(steps_kernel, count, own_lo, flipped, inject_lo),
-        [kept, kept],
-        [smem, vmem, anywhere, anywhere] + [vmem] * (4 * count),
-        [vmem, vmem],
-        [
-            pltpu.VMEM((2,) + padded, f32),
-            pltpu.VMEM(padded, f32),
-            pltpu.VMEM(grid, f32),
-            pltpu.VMEM(grid, f32),
-            pltpu.VMEM(grid, f32),
-            pltpu.VMEM(grid, f32),
-            pltpu.VMEM(grid, f32),
-            pltpu.VMEM((2, window * height, lanes), f32),
-            pltpu.SemaphoreType.DMA((2,)),
-        ],
-    )(meta, z_matrix(lanes), inject_a, inject_b, *state_slabs, *mine, *theirs, *rim_slabs)
+    keep, send = run_steps(
+        count, own_lo, flipped, inject_lo, steps, meta, inject_a, inject_b, state_slabs, mine, theirs, rims
+    )
     got = xor_swap(send, "pair", 1)
 
     part = jax.ShapeDtypeStruct((per_owner, half_x, brick_y, brick_z), f32)
@@ -560,7 +619,7 @@
         [smem, smem, smem, vmem, vmem],
         [vmem] * owners,
         [
-            pltpu.VMEM(kept.shape[1:], f32),
+            pltpu.VMEM(keep.shape[1:], f32),
             pltpu.VMEM((bricks_x * half_x, height, lanes), f32),
         ],
     )(meta, prints, owner_map, keep, got)

time: 205 us -> 143 us (0.70)
  Pallas kernels: 134 us -> 69 us
    pallas_call x1, Pallas kernels: 117 us -> 52.1 us  [run_steps(): call(functools.partial(steps_kernel, count, own_lo, flipped, inject_lo),...]
  transfers between devices with their start and end apart: 15 -> 15, of which waited for: 6 -> 6; matrix products, arithmetic and copies ran while one was open for 9% -> 13% of each run, Pallas kernels for 3% -> 5%
where the time goes in v2:
time: 143 us
  Pallas kernels  69 us (48%)
  waiting for transfers between devices  31.6 us (22%)
  starting transfers between devices  18.9 us (13%)
  matrix products  13.1 us (9%)
  other arithmetic  5.45 us (4%)
  local copies, waits for them, and re-layouts  3.28 us (2%)
    pallas_call x1, Pallas kernels, run_steps(): call(functools.partial(steps_kernel, count, own_lo, flipped, inject_lo),...  52.1 us
    ppermute x15, waiting for transfers between devices, xor_swap(): return lax.ppermute(block, axis, [(i, i ^ bits) for i in range(size)])  31.6 us
    ppermute x15, starting transfers between devices, xor_swap(): return lax.ppermute(block, axis, [(i, i ^ bits) for i in range(size)])  18.9 us
    dot_general x2, matrix products, product(): jnp.einsum('rp,kpz->krz', rows, spread, preferred_element_type=jnp.float32)  13.1 us
    pallas_call x1, Pallas kernels, per_device(): call(functools.partial(image_kernel, owners, columns, slots, stored, flip...  6.6 us
    pallas_call x1, Pallas kernels, per_device(): call(functools.partial(unpack_kernel, owners, columns, slots, stored), ja...  3.55 us
    pallas_call x1, Pallas kernels, per_device(): call(functools.partial(pack_kernel, owners, columns, slots), [brick] * ow...  3.52 us
    pallas_call x1, Pallas kernels, per_device(): call(functools.partial(sum_kernel, owners, columns, slots, stored), jax.S...  3.26 us
  transfers between devices with their start and end apart: 15, of which 6 were waited for; matrix products, arithmetic and copies ran while one was open for 13% of the time, Pallas kernels for 5%

profile of v2, /device:TPU:0, one launch (start us, length us, event | category | flops | bytes accessed | tf_op | source)
XLA Modules:
  0.0 142.8 jit_solution(7387048230883284497)
XLA Ops:
  0.0 4.0 %collective-permute-start.1 = (s32[1,16]{1,0:T(1,128)}, s32[1,16]{1,0:T(1,128)S(1)}, u32[]{:S(2)}, u32[]{:S(2)}) collective-permute-start(s32[1,16]{1,0:T(1,128)} %param.15), channel_id=1, source_target_pairs={{0,8},{4,12},{8,0},{12,4},{1,9},{5,13},{9,1},{13,5},{2,10},{6,14},... | collective-permute-start | bytes 200 | tf_op jit(solution)/shard_map/ppermute | solution.py:51
  4.0 1.6 %collective-permute-start = (s32[1,16]{1,0:T(1,128)}, s32[1,16]{1,0:T(1,128)S(1)}, u32[]{:S(2)}, u32[]{:S(2)}) collective-permute-start(s32[1,16]{1,0:T(1,128)} %param.15), channel_id=1, source_target_pairs={{0,4},{4,0},{8,12},{12,8},{1,5},{5,1},{9,13},{13,9},{2,6},{6,2},{1... | collective-permute-start | bytes 200 | tf_op jit(solution)/shard_map/ppermute | solution.py:51
  5.6 0.0 collective-permute-start.2
  5.6 1.7 %collective-permute-start.10 = (f32[16,2,32,128]{3,2,1,0:T(8,128)}, f32[16,2,32,128]{3,2,1,0:T(8,128)S(1)}, u32[]{:S(2)}, u32[]{:S(2)}) collective-permute-start(f32[16,2,32,128]{3,2,1,0:T(8,128)} %bitcast.32), channel_id=1, source_target_pairs={{0,2},{2,0},{1,3},{3,1},{4,6},{6,4},{5,7},{7,5},{8,10},{10,8},{9,1... | collective-permute-start | bytes 1572872 | tf_op jit(solution)/shard_map/ppermute | solution.py:51
  7.3 0.3 collective-permute-start.3
  8.9 0.7 negate_bitcast_fusion
  9.6 0.1 copy.22
  9.8 0.8 iota_compare_fusion
  10.6 0.8 fusion.17
  11.4 0.7 pad_add_fusion.2.meta
  12.0 0.0 collective-permute-done.1
  12.0 0.0 collective-permute-done
  12.0 0.0 collective-permute-done.2
  12.0 1.3 pad_add_fusion.1.prints
  13.3 3.5 %shard_map.118 = (f32[4,8,8,128]{3,2,1,0:T(8,128)}, f32[4,8,8,128]{3,2,1,0:T(8,128)}, f32[4,8,8,128]{3,2,1,0:T(8,128)}, f32[4,8,8,128]{3,2,1,0:T(8,128)}) custom-call(s32[4]{0:T(128)} %pad_add_fusion.2.meta, s32[4,16]{1,0:T(4,128)} %pad_add_fusion.1.prints, s32[64]{0:T(128)} %owner_map.7, f32[8,8,8,128]{3,2,1,0:T(8,128)} %velocity.1, f32[8,8,8,128]{3,2,1,0:T(8,128)} %density.1), custom_call_target="tpu_custom_call" | custom-call | tf_op jit(solution)/shard_map/pallas_call | solution.py:575
  16.8 0.9 collective-permute-start.4
  17.7 3.5 %collective-permute-start.5 = (f32[4,8,8,128]{3,2,1,0:T(8,128)}, f32[4,8,8,128]{3,2,1,0:T(8,128)S(1)}, u32[]{:S(2)}, u32[]{:S(2)}) collective-permute-start(f32[4,8,8,128]{3,2,1,0:T(8,128)} %get-tuple-element.17), channel_id=1, source_target_pairs={{0,8},{4,12},{8,0},{12,4},{1,9},{5,13},{9,1},{13,5},{2,10},{6,14},... | collective-permute-start | bytes 393224 | tf_op jit(solution)/shard_map/ppermute | solution.py:51
  21.2 0.0 collective-permute-start.6
  21.2 0.1 add_convert_fusion
  21.3 2.2 %collective-permute-done.4.refs_1_ = f32[4,8,8,128]{3,2,1,0:T(8,128)S(1)} collective-permute-done((f32[4,8,8,128]{3,2,1,0:T(8,128)}, f32[4,8,8,128]{3,2,1,0:T(8,128)S(1)}, u32[]{:S(2)}, u32[]{:S(2)}) %collective-permute-start.4) | collective-permute-done | bytes 131104 | tf_op jit(solution)/shard_map/ppermute | solution.py:51
  23.5 0.0 copy-start.5
  23.5 7.4 %collective-permute-done.5.refs_2_ = f32[4,8,8,128]{3,2,1,0:T(8,128)S(1)} collective-permute-done((f32[4,8,8,128]{3,2,1,0:T(8,128)}, f32[4,8,8,128]{3,2,1,0:T(8,128)S(1)}, u32[]{:S(2)}, u32[]{:S(2)}) %collective-permute-start.5) | collective-permute-done | bytes 131104 | tf_op jit(solution)/shard_map/ppermute | solution.py:51
  31.0 0.0 copy-start.6
  31.0 0.0 collective-permute-done.6.refs_3_
  31.0 0.0 copy-start.7
  31.0 0.0 copy-done.5
  31.0 0.6 copy-done.6
  31.6 0.1 copy-done.7
  31.7 3.5 %shard_map.119.refs_2_ = f32[32,32,128]{2,1,0:T(8,128)} custom-call(s32[4]{0:T(128)} %pad_add_fusion.2.meta, s32[4,16]{1,0:T(4,128)} %pad_add_fusion.1.prints, s32[64]{0:T(128)} %owner_map.7, f32[4,8,8,128]{3,2,1,0:T(8,128)} %get-tuple-element.15.refs_0_, f32[4,8,8,128]{3,2,1,0:T(8,128)} %copy-done.5, f32[4,8,8,128]{3,2,1,0:T(8,128)} %copy-done.6, ...), custom_call_target="tpu_custom_call" | custom-call | tf_op jit(solution)/shard_map/pallas_call | solution.py:582
  35.2 0.0 copy-start
  35.2 1.5 %collective-permute-start.7 = (f32[32,32,128]{2,1,0:T(8,128)}, f32[32,32,128]{2,1,0:T(8,128)S(1)}, u32[]{:S(2)}, u32[]{:S(2)}) collective-permute-start(f32[32,32,128]{2,1,0:T(8,128)} %shard_map.119.refs_2_), channel_id=1, source_target_pairs={{0,2},{2,0},{1,3},{3,1},{4,6},{6,4},{5,7},{7,5},{8,10},{10,8},{9,1... | collective-permute-start | bytes 1572872 | tf_op jit(solution)/shard_map/ppermute | solution.py:51
  36.7 6.8 %fusion.10.inject_a = f32[8,2048,128]{2,1,0:T(8,128)} fusion(pred[2048,512]{1,0:T(32,128)(4,1)S(1)} %iota_compare_fusion, f32[1024,128]{0,1:T(8,128)S(1)} %add_convert_fusion, f32[16,1024]{1,0:T(8,128)S(1)} %pad_maximum_fusion), kind=kOutput, calls=%fused_computation.10 | convolution fusion | flops 4301258752 | bytes 10027008 | tf_op jit(solution)/shard_map/rp,kpz->krz/dot_general | solution.py:528
  43.5 0.0 copy-done
  43.5 0.0 copy-start.2
  43.5 0.0 collective-permute-start.8
  43.5 9.1 %collective-permute-done.7.refs_3_ = f32[32,32,128]{2,1,0:T(8,128)S(1)} collective-permute-done((f32[32,32,128]{2,1,0:T(8,128)}, f32[32,32,128]{2,1,0:T(8,128)S(1)}, u32[]{:S(2)}, u32[]{:S(2)}) %collective-permute-start.7) | collective-permute-done | bytes 524320 | tf_op jit(solution)/shard_map/ppermute | solution.py:51
  52.6 0.0 copy-start.3
  52.6 0.0 collective-permute-start.9
  52.6 6.4 %fusion.7.inject_b = f32[8,1920,128]{2,1,0:T(8,128)} fusion(pred[2048,512]{1,0:T(32,128)(4,1)S(1)} %iota_compare_fusion, f32[1024,128]{0,1:T(8,128)S(1)} %add_convert_fusion, f32[16,1024]{1,0:T(8,128)S(1)} %pad_maximum_fusion), kind=kOutput, calls=%fused_computation.9 | convolution fusion | flops 4032692224 | bytes 9502720 | tf_op jit(solution)/shard_map/rp,kpz->krz/dot_general | solution.py:528
  59.0 0.0 copy-done.3
  59.0 0.0 collective-permute-done.10
  59.0 0.0 copy-done.2
  59.0 1.2 maximum_select_fusion.refs_6_
  60.2 0.0 collective-permute-done.8.refs_4_
  60.2 0.0 copy-start.4
  60.2 0.0 collective-permute-done.3.refs_1_
  60.2 0.8 copy-done.4
  61.0 0.0 copy-start.1
  61.0 0.0 collective-permute-done.9.refs_5_
  61.0 1.1 copy-done.1
  62.0 52.1 %shard_map.120 = (f32[16,4,4,4,8,128]{5,4,3,2,1,0:T(8,128)}, f32[16,4,4,4,8,128]{5,4,3,2,1,0:T(8,128)}) custom-call(s32[4]{0:T(128)} %pad_add_fusion.2.meta, bf16[256,256]{1,0:T(8,128)(2,1)} %constant.100.clone.zmat, f32[8,2048,128]{2,1,0:T(8,128)} %fusion.10.inject_a, f32[8,1920,128]{2,1,0:T(8,128)} %fusion.7.inject_b, f32[2,32,32,128]{3,2,1,0:T(8,128)} %bitcast.31, ...), custom_call_target="tpu_custom_call" | custom-call | tf_op jit(solution)/shard_map/pallas_call | solution.py:477
  114.2 0.6 collective-permute-start.11
  114.7 7.1 %collective-permute-done.11.got = f32[16,4,4,4,8,128]{5,4,3,2,1,0:T(8,128)} collective-permute-done((f32[16,4,4,4,8,128]{5,4,3,2,1,0:T(8,128)}, f32[16,4,4,4,8,128]{5,4,3,2,1,0:T(8,128)}, u32[]{:S(2)}, u32[]{:S(2)}) %collective-permute-start.11) | collective-permute-done | bytes 4194336 | tf_op jit(solution)/shard_map/ppermute | solution.py:51
  121.9 6.6 %shard_map.121 = (f32[4,4,8,128]{3,2,1,0:T(8,128)}, f32[4,4,8,128]{3,2,1,0:T(8,128)}, f32[4,4,8,128]{3,2,1,0:T(8,128)}, f32[4,4,8,128]{3,2,1,0:T(8,128)}) custom-call(s32[4]{0:T(128)} %pad_add_fusion.2.meta, s32[4,16]{1,0:T(4,128)} %pad_add_fusion.1.prints, s32[64]{0:T(128)} %owner_map.7, f32[16,4,4,4,8,128]{5,4,3,2,1,0:T(8,128)} %get-tuple-element.19.keep, ...), custom_call_target="tpu_custom_call" | custom-call | tf_op jit(solution)/shard_map/pallas_call | solution.py:616
  128.5 0.0 collective-permute-start.12
  128.5 4.1 %collective-permute-start.13 = (f32[4,4,8,128]{3,2,1,0:T(8,128)}, f32[4,4,8,128]{3,2,1,0:T(8,128)S(1)}, u32[]{:S(2)}, u32[]{:S(2)}) collective-permute-start(f32[4,4,8,128]{3,2,1,0:T(8,128)} %get-tuple-element.23), channel_id=1, source_target_pairs={{0,8},{4,12},{8,0},{12,4},{1,9},{5,13},{9,1},{13,5},{2,10},{6,14},... | collective-permute-start | bytes 196616 | tf_op jit(solution)/shard_map/ppermute | solution.py:51
  132.6 0.7 collective-permute-start.14
  133.3 0.0 collective-permute-done.12.refs_1_
  133.3 2.0 %collective-permute-done.13.refs_2_ = f32[4,4,8,128]{3,2,1,0:T(8,128)S(1)} collective-permute-done((f32[4,4,8,128]{3,2,1,0:T(8,128)}, f32[4,4,8,128]{3,2,1,0:T(8,128)S(1)}, u32[]{:S(2)}, u32[]{:S(2)}) %collective-permute-start.13) | collective-permute-done | bytes 65568 | tf_op jit(solution)/shard_map/ppermute | solution.py:51
  135.2 3.7 %collective-permute-done.14.refs_3_ = f32[4,4,8,128]{3,2,1,0:T(8,128)S(1)} collective-permute-done((f32[4,4,8,128]{3,2,1,0:T(8,128)}, f32[4,4,8,128]{3,2,1,0:T(8,128)S(1)}, u32[]{:S(2)}, u32[]{:S(2)}) %collective-permute-start.14) | collective-permute-done | bytes 65568 | tf_op jit(solution)/shard_map/ppermute | solution.py:51
  138.9 0.0 copy-done.8
  138.9 0.0 copy-done.9
  138.9 0.6 copy-done.10
  139.5 3.3 %shard_map.122 = f32[8,4,8,128]{3,2,1,0:T(8,128)} custom-call(s32[4]{0:T(128)} %pad_add_fusion.2.meta, s32[4,16]{1,0:T(4,128)} %pad_add_fusion.1.prints, s32[64]{0:T(128)} %owner_map.7, f32[4,4,8,128]{3,2,1,0:T(8,128)} %get-tuple-element.21.refs_0_, f32[4,4,8,128]{3,2,1,0:T(8,128)} %copy-done.8, f32[4,4,8,128]{3,2,1,0:T(8,128)} %copy-done.9, ...), custom_call_target="tpu_custom_call" | custom-call | tf_op jit(solution)/shard_map/pallas_call | solution.py:627
  (6 shorter events, 0.1 us)
Async XLA Ops:
  0.0 12.0 %collective-permute-start.1 = (s32[1,16]{1,0:T(1,128)}, s32[1,16]{1,0:T(1,128)S(1)}, u32[]{:S(2)}, u32[]{:S(2)}) collective-permute-start(s32[1,16]{1,0:T(1,128)} %param.15), channel_id=1, source_target_pairs={{0,8},{4,12},{8,0},{12,4},{1,9},{5,13},{9,1},{13,5},{2,10},{6,14},... | collective-permute-start | bytes 200 | tf_op jit(solution)/shard_map/ppermute | solution.py:51
  4.0 8.0 %collective-permute-start = (s32[1,16]{1,0:T(1,128)}, s32[1,16]{1,0:T(1,128)S(1)}, u32[]{:S(2)}, u32[]{:S(2)}) collective-permute-start(s32[1,16]{1,0:T(1,128)} %param.15), channel_id=1, source_target_pairs={{0,4},{4,0},{8,12},{12,8},{1,5},{5,1},{9,13},{13,9},{2,6},{6,2},{1... | collective-permute-start | bytes 200 | tf_op jit(solution)/shard_map/ppermute | solution.py:51
  5.6 6.4 %collective-permute-start.2 = (s32[1,16]{1,0:T(1,128)}, s32[1,16]{1,0:T(1,128)S(1)}, u32[]{:S(2)}, u32[]{:S(2)}) collective-permute-start(s32[1,16]{1,0:T(1,128)} %param.15), channel_id=1, source_target_pairs={{0,12},{4,8},{8,4},{12,0},{1,13},{5,9},{9,5},{13,1},{2,14},{6,10},... | collective-permute-start | bytes 200 | tf_op jit(solution)/shard_map/ppermute | solution.py:51
  5.6 53.4 %collective-permute-start.10 = (f32[16,2,32,128]{3,2,1,0:T(8,128)}, f32[16,2,32,128]{3,2,1,0:T(8,128)S(1)}, u32[]{:S(2)}, u32[]{:S(2)}) collective-permute-start(f32[16,2,32,128]{3,2,1,0:T(8,128)} %bitcast.32), channel_id=1, source_target_pairs={{0,2},{2,0},{1,3},{3,1},{4,6},{6,4},{5,7},{7,5},{8,10},{10,8},{9,1... | collective-permute-start | bytes 1572872 | tf_op jit(solution)/shard_map/ppermute | solution.py:51
  7.3 52.9 %collective-permute-start.3 = (f32[2,32,32,128]{3,2,1,0:T(8,128)}, f32[2,32,32,128]{3,2,1,0:T(8,128)S(1)}, u32[]{:S(2)}, u32[]{:S(2)}) collective-permute-start(f32[2,32,32,128]{3,2,1,0:T(8,128)} %bitcast.30), channel_id=1, source_target_pairs={{0,2},{2,0},{1,3},{3,1},{4,6},{6,4},{5,7},{7,5},{8,10},{10,8},{9,1... | collective-permute-start | bytes 3145736 | tf_op jit(solution)/shard_map/ppermute | solution.py:51
  16.8 6.7 %collective-permute-start.4 = (f32[4,8,8,128]{3,2,1,0:T(8,128)}, f32[4,8,8,128]{3,2,1,0:T(8,128)S(1)}, u32[]{:S(2)}, u32[]{:S(2)}) collective-permute-start(f32[4,8,8,128]{3,2,1,0:T(8,128)} %get-tuple-element.16), channel_id=1, source_target_pairs={{0,4},{4,0},{8,12},{12,8},{1,5},{5,1},{9,13},{13,9},{2,6},{6,2},{1... | collective-permute-start | bytes 393224 | tf_op jit(solution)/shard_map/ppermute | solution.py:51
  17.7 13.2 %collective-permute-start.5 = (f32[4,8,8,128]{3,2,1,0:T(8,128)}, f32[4,8,8,128]{3,2,1,0:T(8,128)S(1)}, u32[]{:S(2)}, u32[]{:S(2)}) collective-permute-start(f32[4,8,8,128]{3,2,1,0:T(8,128)} %get-tuple-element.17), channel_id=1, source_target_pairs={{0,8},{4,12},{8,0},{12,4},{1,9},{5,13},{9,1},{13,5},{2,10},{6,14},... | collective-permute-start | bytes 393224 | tf_op jit(solution)/shard_map/ppermute | solution.py:51
  21.2 9.8 %collective-permute-start.6 = (f32[4,8,8,128]{3,2,1,0:T(8,128)}, f32[4,8,8,128]{3,2,1,0:T(8,128)S(1)}, u32[]{:S(2)}, u32[]{:S(2)}) collective-permute-start(f32[4,8,8,128]{3,2,1,0:T(8,128)} %get-tuple-element.18), channel_id=1, source_target_pairs={{0,12},{4,8},{8,4},{12,0},{1,13},{5,9},{9,5},{13,1},{2,14},{6,10},... | collective-permute-start | bytes 393224 | tf_op jit(solution)/shard_map/ppermute | solution.py:51
  23.5 7.5 %copy-start.5 = (f32[4,8,8,128]{3,2,1,0:T(8,128)}, f32[4,8,8,128]{3,2,1,0:T(8,128)S(1)}, u32[]{:S(2)}) copy-start(f32[4,8,8,128]{3,2,1,0:T(8,128)S(1)} %collective-permute-done.4.refs_1_) | copy-start | bytes 393220
  31.0 0.6 copy-start.6
  31.0 0.7 copy-start.7
  35.2 8.3 %copy-start = (f32[32,32,128]{2,1,0:T(8,128)S(1)}, f32[32,32,128]{2,1,0:T(8,128)}, u32[]{:S(2)}) copy-start(f32[32,32,128]{2,1,0:T(8,128)} %shard_map.119.refs_2_) | copy-start | bytes 1572868
  35.2 17.4 %collective-permute-start.7 = (f32[32,32,128]{2,1,0:T(8,128)}, f32[32,32,128]{2,1,0:T(8,128)S(1)}, u32[]{:S(2)}, u32[]{:S(2)}) collective-permute-start(f32[32,32,128]{2,1,0:T(8,128)} %shard_map.119.refs_2_), channel_id=1, source_target_pairs={{0,2},{2,0},{1,3},{3,1},{4,6},{6,4},{5,7},{7,5},{8,10},{10,8},{9,1... | collective-permute-start | bytes 1572872 | tf_op jit(solution)/shard_map/ppermute | solution.py:51
  43.5 15.5 %copy-start.2 = (f32[1,16,2,32,128]{4,3,2,1,0:T(8,128)S(1)}, f32[1,16,2,32,128]{4,3,2,1,0:T(8,128)}, u32[]{:S(2)}) copy-start(f32[1,16,2,32,128]{4,3,2,1,0:T(8,128)} %param.22) | copy-start | bytes 1572868
  43.5 16.7 %collective-permute-start.8 = (f32[32,32,128]{2,1,0:T(8,128)S(1)}, f32[32,32,128]{2,1,0:T(8,128)S(1)}, u32[]{:S(2)}, u32[]{:S(2)}) collective-permute-start(f32[32,32,128]{2,1,0:T(8,128)S(1)} %copy-done), channel_id=1, source_target_pairs={{0,1},{1,0},{2,3},{3,2},{4,5},{5,4},{6,7},{7,6},{8,9},{9,8},{10,11... | collective-permute-start | bytes 1572872 | tf_op jit(solution)/shard_map/ppermute | solution.py:51
  52.6 6.4 %copy-start.3 = (f32[32,32,128]{2,1,0:T(8,128)}, f32[32,32,128]{2,1,0:T(8,128)S(1)}, u32[]{:S(2)}) copy-start(f32[32,32,128]{2,1,0:T(8,128)S(1)} %collective-permute-done.7.refs_3_) | copy-start | bytes 1572868
  52.6 8.3 %collective-permute-start.9 = (f32[32,32,128]{2,1,0:T(8,128)S(1)}, f32[32,32,128]{2,1,0:T(8,128)}, u32[]{:S(2)}, u32[]{:S(2)}) collective-permute-start(f32[32,32,128]{2,1,0:T(8,128)S(1)} %collective-permute-done.7.refs_3_), channel_id=1, source_target_pairs={{0,1},{1,0},{2,3},{3,2},{4,5},{5,4},{6,7},{7,6},{8,9},{9,8},{10,11... | collective-permute-start | bytes 1572872 | tf_op jit(solution)/shard_map/ppermute | solution.py:51
  60.2 0.8 copy-start.4
  61.0 1.1 copy-start.1
  114.2 7.7 %collective-permute-start.11 = (f32[16,4,4,4,8,128]{5,4,3,2,1,0:T(8,128)}, f32[16,4,4,4,8,128]{5,4,3,2,1,0:T(8,128)}, u32[]{:S(2)}, u32[]{:S(2)}) collective-permute-start(f32[16,4,4,4,8,128]{5,4,3,2,1,0:T(8,128)} %get-tuple-element.20), channel_id=1, source_target_pairs={{0,1},{1,0},{2,3},{3,2},{4,5},{5,4},{6,7},{7,6},{8,9},{9,8},{10,11... | collective-permute-start | bytes 12582920 | tf_op jit(solution)/shard_map/ppermute | solution.py:51
  128.5 4.8 %collective-permute-start.12 = (f32[4,4,8,128]{3,2,1,0:T(8,128)}, f32[4,4,8,128]{3,2,1,0:T(8,128)S(1)}, u32[]{:S(2)}, u32[]{:S(2)}) collective-permute-start(f32[4,4,8,128]{3,2,1,0:T(8,128)} %get-tuple-element.22), channel_id=1, source_target_pairs={{0,4},{4,0},{8,12},{12,8},{1,5},{5,1},{9,13},{13,9},{2,6},{6,2},{1... | collective-permute-start | bytes 196616 | tf_op jit(solution)/shard_map/ppermute | solution.py:51
  128.5 6.8 %collective-permute-start.13 = (f32[4,4,8,128]{3,2,1,0:T(8,128)}, f32[4,4,8,128]{3,2,1,0:T(8,128)S(1)}, u32[]{:S(2)}, u32[]{:S(2)}) collective-permute-start(f32[4,4,8,128]{3,2,1,0:T(8,128)} %get-tuple-element.23), channel_id=1, source_target_pairs={{0,8},{4,12},{8,0},{12,4},{1,9},{5,13},{9,1},{13,5},{2,10},{6,14},... | collective-permute-start | bytes 196616 | tf_op jit(solution)/shard_map/ppermute | solution.py:51
  132.6 6.3 %collective-permute-start.14 = (f32[4,4,8,128]{3,2,1,0:T(8,128)}, f32[4,4,8,128]{3,2,1,0:T(8,128)S(1)}, u32[]{:S(2)}, u32[]{:S(2)}) collective-permute-start(f32[4,4,8,128]{3,2,1,0:T(8,128)} %get-tuple-element.24), channel_id=1, source_target_pairs={{0,12},{4,8},{8,4},{12,0},{1,13},{5,9},{9,5},{13,1},{2,14},{6,10},... | collective-permute-start | bytes 196616 | tf_op jit(solution)/shard_map/ppermute | solution.py:51
  133.3 5.7 %copy-start.8 = (f32[4,4,8,128]{3,2,1,0:T(8,128)}, f32[4,4,8,128]{3,2,1,0:T(8,128)S(1)}, u32[]{:S(2)}) copy-start(f32[4,4,8,128]{3,2,1,0:T(8,128)S(1)} %collective-permute-done.12.refs_1_) | copy-start | bytes 196612
  135.2 3.7 %copy-start.9 = (f32[4,4,8,128]{3,2,1,0:T(8,128)}, f32[4,4,8,128]{3,2,1,0:T(8,128)S(1)}, u32[]{:S(2)}) copy-start(f32[4,4,8,128]{3,2,1,0:T(8,128)S(1)} %collective-permute-done.13.refs_2_) | copy-start | bytes 196612
  138.9 0.6 copy-start.10

commit v3 on v2

v3 whole, which is shorter than its diff:
```python
import functools

import jax
import jax.numpy as jnp
import numpy as np
from jax import lax
from jax.experimental import pallas as pl
from jax.experimental.pallas import tpu as pltpu
from jax.sharding import PartitionSpec as P

KY = 4
REACH = 4

first_weights = (0.8, -0.2, 4.0 / 105.0, -1.0 / 280.0)
second_weights = (-205.0 / 72.0, 1.6, -0.2, 8.0 / 315.0, -1.0 / 560.0)

FIRST = first_weights[0]
SECOND = second_weights[1]
first_ratio = tuple(w / FIRST for w in first_weights)
second_ratio = tuple(w / SECOND for w in second_weights[1:])

SECOND_UNIT = 8064.0
FIRST_UNIT = 672.0
second_whole = (8064.0, -1008.0, 128.0, -9.0)
first_whole = (672.0, -168.0, 32.0, -3.0)

HOPS = 2
MIB = 1024 * 1024

smem = pl.BlockSpec(memory_space=pltpu.SMEM)
vmem = pl.BlockSpec(memory_space=pltpu.VMEM)
anywhere = pl.BlockSpec(memory_space=pl.ANY)


def z_matrix(size):
    second = np.zeros((size, size))
    first = np.zeros((size, size))
    for r in range(1, REACH + 1):
        for z in range(size):
            if z + r < size:
                second[z + r, z] = second_whole[r - 1]
                first[z + r, z] = first_whole[r - 1]
            if z - r >= 0:
                second[z - r, z] = second_whole[r - 1]
                first[z - r, z] = -first_whole[r - 1]
    whole = np.concatenate([second, first], axis=1)
    return np.concatenate([whole, whole], axis=0).astype(jnp.bfloat16)


def y_matrix(across, layers):
    second = np.zeros((across, across))
    first = np.zeros((across, across))
    for r in range(1, REACH + 1):
        for y in range(across):
            if y + r < across:
                second[y, y + r] = second_whole[r - 1]
                first[y, y + r] = first_whole[r - 1]
            if y - r >= 0:
                second[y, y - r] = second_whole[r - 1]
                first[y, y - r] = -first_whole[r - 1]
    same = np.eye(layers)
    whole = np.concatenate([np.kron(same, second), np.kron(same, first)], axis=0)
    return np.concatenate([whole, whole], axis=1).astype(jnp.bfloat16)


def xor_swap(block, axis, bits):
    size = lax.axis_size(axis)
    return lax.ppermute(block, axis, [(i, i ^ bits) for i in range(size)])


def slabs_of(block, first_only=False):
    size = lax.axis_size("dom")
    pairs = lax.axis_size("pair")

    def shift(x, moves):
        if first_only:
            return lax.ppermute(x, ("dom", "pair"), [(i * pairs, j * pairs) for i, j in moves])
        return lax.ppermute(x, "dom", moves)

    if size == 1:
        return [block]
    if size == 2:
        return [block, shift(block, [(0, 1), (1, 0)])]
    up = [(i, i + 1) for i in range(size - 1)]
    down = [(i + 1, i) for i in range(size - 1)]
    found = [block]
    left = right = block
    for _ in range(HOPS):
        left = shift(left, up)
        right = shift(right, down)
        found = [left] + found + [right]
    return found


def serve(prints, owner_map, base, stored, take):
    slots = prints.shape[1]

    def one(m, count):
        local = owner_map[prints[0, m]] - base
        mine = (local >= 0) & (local < stored)

        @pl.when(mine)
        def _():
            take(m, local, count)

        return count + mine.astype(jnp.int32)

    lax.fori_loop(0, slots, one, jnp.int32(0))


def pack_kernel(owners, columns, relay, meta, owner_map, *refs):
    prints, refs = refs[:owners], refs[owners:]
    if relay:
        (table,), refs = refs[:1], refs[1:]
        column = 1 - meta[1]
    else:
        (velocity, density), refs = refs[:2], refs[2:]
        table = velocity
        column = meta[1]
    outs, sems = refs[:-1], refs[-1]
    stored = table.shape[0]
    per_owner = outs[0].shape[0]
    first = meta[2] == 0
    base = (meta[0] * columns + column) * stored

    def send(source, local, out, rank, sem):
        pltpu.make_async_copy(source.at[local], out.at[rank], sem).start()

    for b in range(owners):

        def take(m, local, rank, b=b):
            if relay:
                send(table, local, outs[b], rank, sems.at[b, rank])
                return

            @pl.when(first)
            def _():
                send(velocity, local, outs[b], rank, sems.at[b, rank])
                if b == 0:
                    send(density, local, outs[owners], rank, sems.at[owners, rank])

            @pl.when(jnp.logical_not(first))
            def _():
                send(density, local, outs[b], rank, sems.at[b, rank])
                if b == 0:
                    send(velocity, local, outs[owners], rank, sems.at[owners, rank])

        serve(prints[b], owner_map, base, stored, take)
    for b, out in enumerate(outs):
        for rank in range(per_owner):
            pltpu.make_async_copy(table.at[0], out.at[rank], sems.at[b, rank]).wait()


def unpack_kernel(owners, columns, stored, meta, owner_map, prints, *refs):
    blocks, out = refs[:-1], refs[-1]
    for b in range(owners):
        base = ((meta[0] ^ b) * columns + meta[1]) * stored

        def take(m, local, rank, b=b):
            out[m] = blocks[b][rank]

        serve(prints, owner_map, base, stored, take)


def each(f, *lists):
    return [f(*items) for items in zip(*lists)]


def add(a, b):
    return each(lambda p, q: p + q, a, b)


def sub(a, b):
    return each(lambda p, q: p - q, a, b)


def mul(a, b):
    return each(lambda p, q: p * q, a, b)


def scaled(factor, a):
    return [factor * p for p in a]


def along_x(column):
    size = len(column) - 2 * REACH
    lap = slope = None
    for r in range(1, REACH + 1):
        ahead = column[REACH + r : REACH + r + size]
        behind = column[REACH - r : REACH - r + size]
        total, apart = add(ahead, behind), sub(ahead, behind)
        if r == 1:
            lap, slope = total, apart
        else:
            lap = add(lap, scaled(second_ratio[r - 1], total))
            slope = add(slope, scaled(first_ratio[r - 1], apart))
    return lap, slope


def y_and_z(value, zmat, ymat, zout, youts):
    high = value.astype(jnp.bfloat16)
    low = (value - high.astype(jnp.float32)).astype(jnp.bfloat16)
    z = jnp.dot(
        jnp.concatenate([high, low], axis=1), zmat[...], preferred_element_type=jnp.float32
    )
    ys = []
    group = ymat.shape[0] // 2
    for at in range(0, value.shape[0], group):
        both = jnp.concatenate([high[at : at + group], low[at : at + group]], axis=0)
        ys.append(jnp.dot(ymat[...], both, preferred_element_type=jnp.float32))
    return z, ys


BLOCK = 8


def steps_kernel(shape, meta, owner_map, zmat, ymat, inject_a, inject_b, *refs):
    owners, columns, stored, sides, inject_lo = shape
    if sides:
        own_prints, other_prints = refs[:2]
        refs = refs[2:]
    count = 2 if sides else 2 * HOPS + 1
    parts = owners if sides else 1
    mine = [refs[c * parts : (c + 1) * parts] for c in range(count)]
    refs = refs[count * parts :]
    theirs = [refs[c * parts : (c + 1) * parts] for c in range(count)]
    refs = refs[count * parts :]
    states, refs = refs[:count], refs[count:]
    rims, refs = refs[:count], refs[count:]
    keep, send = refs[:2]
    field, logs, square, centre, gx, gy, gz, pulses, zbuf, ybuf, record, rim, sems, out_sems, in_sems = refs[2:]
    thick, height, lanes = states[0].shape[1:]
    steps = rims[0].shape[0]
    window = thick * count
    cols = thick // 8
    rows8 = height // 8
    column = meta[1]
    is_source = meta[2] == 0
    limit = meta[3]
    half_of = meta[2]
    sublane = lax.broadcasted_iota(jnp.int32, (8, lanes), 0)
    if sides:
        own_lo = column * thick
        places = [column * thick, (1 - column) * thick]
    else:
        own_lo = HOPS * thick
        places = [s * thick for s in range(count)]

    def active(w):
        x = w if sides else w + column * thick - own_lo
        return (x >= 0) & (x < limit)

    def lo_of(k):
        return jnp.maximum(0, own_lo - REACH * (steps - 1 - k))

    def hi_of(k):
        return jnp.minimum(window, own_lo + thick + REACH * (steps - 1 - k))

    early = inject_a.shape[0]
    rows_b = inject_b.shape[1]

    def copy_a(k, slot):
        return pltpu.make_async_copy(inject_a.at[k], pulses.at[slot], sems.at[slot])

    def copy_b(k, slot):
        return pltpu.make_async_copy(
            inject_b.at[k - early],
            pulses.at[slot, pl.ds(inject_lo, rows_b)],
            sems.at[slot],
        )

    def start_copy(k, slot):
        @pl.when(k < early)
        def _():
            copy_a(k, slot).start()

        @pl.when((k >= early) & (k < steps))
        def _():
            copy_b(k, slot).start()

    def wait_copy(k, slot):
        @pl.when(k < early)
        def _():
            copy_a(k, slot).wait()

        @pl.when(k >= early)
        def _():
            copy_b(k, slot).wait()

    def out_copies(k, slot):
        return [
            pltpu.make_async_copy(
                record.at[slot, pl.ds(0, cols)], keep.at[k], out_sems.at[slot, 0]
            ),
            pltpu.make_async_copy(
                record.at[slot, pl.ds(cols, cols)], send.at[k], out_sems.at[slot, 1]
            ),
        ]

    def in_copies(s):
        place = places[s] if isinstance(places[s], int) else pl.multiple_of(places[s], 8)
        copies = [
            pltpu.make_async_copy(
                states[s].at[level], field.at[level, pl.ds(REACH + place, thick)], in_sems.at[s, level]
            )
            for level in range(2)
        ]
        return copies + [
            pltpu.make_async_copy(rims[s], rim.at[:, :, pl.ds(place, thick), :], in_sems.at[s, 2])
        ]

    copy_a(0, 0).start()
    for s in range(count):
        for copy in in_copies(s):
            copy.start()

    zero = jnp.zeros((REACH, height, lanes), jnp.float32)
    for level in range(2):
        field[level, 0:REACH] = zero
        field[level, REACH + window : 2 * REACH + window] = zero
    logs[0:REACH] = zero
    logs[REACH + window : 2 * REACH + window] = zero

    for s in range(count):

        def fill(m, a, b, rank, direct, s=s):
            x0 = places[s] + (m // KY) * 8
            y0 = pl.multiple_of((m % KY) * 8, 8)
            on = active(x0)
            for i in range(8):
                courant = jnp.where(is_source, a[rank, i], b[rank, i])
                density = jnp.where(is_source, b[rank, i], a[rank, i])
                squared = jnp.where(on, courant * courant, 0.0)
                square[x0 + i, pl.ds(y0, 8), :] = SECOND * squared
                centre[x0 + i, pl.ds(y0, 8), :] = 2.0 + (3.0 * second_weights[0]) * squared
                logs[REACH + x0 + i, pl.ds(y0, 8), :] = jnp.where(
                    on, jnp.log(jnp.where(on, density, 1.0)), 0.0
                )

        if sides:
            prints = (own_prints, other_prints)[s]
            for b in range(owners):
                base = ((meta[0] ^ b) * columns + (column if s == 0 else 1 - column)) * stored

                def take(m, local, rank, b=b, s=s):
                    fill(m, mine[s][b], theirs[s][b], rank, False)

                serve(prints, owner_map, base, stored, take)
        else:

            def one(m, carry, s=s):
                fill(m, mine[s][0], theirs[s][0], m, False)
                return carry

            lax.fori_loop(0, mine[s][0].shape[0], one, 0)

    def bend(b, carry):
        w = b * 4
        z, ys = y_and_z(
            logs[pl.ds(REACH + w, 4)].reshape(4 * height, lanes), zmat, ymat, None, None
        )
        for q in range(rows8):
            part = slice(q * 8, q * 8 + 8)
            _, slope = along_x([logs[w + j, part, :] for j in range(4 + 2 * REACH)])
            for i in range(4):
                at = i * height + q * 8
                scale = (FIRST * FIRST / SECOND) * square[w + i, part, :]
                whole = scale * (1.0 / (FIRST_UNIT * FIRST_UNIT))
                gx[w + i, part, :] = scale * slope[i]
                gy[w + i, part, :] = whole * ys[0][4 * height + at : 4 * height + at + 8]
                gz[w + i, part, :] = whole * z[at : at + 8, lanes:]
        return carry

    lax.fori_loop(0, window // 4, bend, 0)
    for s in range(count):
        for copy in in_copies(s):
            copy.wait()

    rim_low = (sublane == 0) & is_source
    rim_high = (sublane == 7) & is_source
    groups = BLOCK // 4

    def ahead(level, b, slot):
        w = b * BLOCK
        value = field[level, pl.ds(REACH + w, BLOCK)].reshape(BLOCK * height, lanes)
        return y_and_z(value, zmat, ymat, None, None)

    def one_step(k, carry):
        old = lax.rem(k, 2)
        new = 1 - old
        slot = lax.rem(k, 2)
        wait_copy(k, slot)
        start_copy(k + 1, 1 - slot)

        @pl.when(k >= 2)
        def _():
            for copy in out_copies(k - 2, slot):
                copy.wait()

        first = lo_of(k) // BLOCK
        last = (hi_of(k) + BLOCK - 1) // BLOCK

        def store_ahead(values, slot):
            z, ys = values
            zbuf[slot] = z
            for g in range(groups):
                ybuf[slot, g] = ys[g]

        store_ahead(ahead(new, first, 0), lax.rem(first, 2))

        def block(b, carry):
            w = pl.multiple_of(b * BLOCK, BLOCK)
            on = active(w)
            after = jnp.minimum(b + 1, window // BLOCK - 1)
            is_own = (w >= own_lo) & (w < own_lo + thick)
            bslot = lax.rem(b, 2)

            @pl.when(on)
            def _():
                following = ahead(new, after, 0)
                for g in range(groups):
                    half = jnp.where(half_of == g % 2, 0, cols)
                    to = jnp.where(is_own, half + (w - own_lo) // 8, 2 * cols)
                    xs = [w + g * 4 + i for i in range(4)]
                    for q in range(rows8):
                        part = slice(q * 8, q * 8 + 8)
                        column_x = [
                            field[new, w + g * 4 + j, part, :] for j in range(4 + 2 * REACH)
                        ]
                        lap, dx = along_x(column_x)
                        mid = column_x[REACH : REACH + 4]
                        at = [(g * 4 + i) * height + q * 8 for i in range(4)]
                        aty = [i * height + q * 8 for i in range(4)]
                        z2 = [zbuf[bslot, p : p + 8, 0:lanes] for p in at]
                        z1 = [zbuf[bslot, p : p + 8, lanes:] for p in at]
                        y2 = [ybuf[bslot, g, p : p + 8, :] for p in aty]
                        y1 = [ybuf[bslot, g, 4 * height + p : 4 * height + p + 8, :] for p in aty]
                        lap = add(lap, scaled(1.0 / SECOND_UNIT, add(z2, y2)))
                        value = sub(
                            mul([centre[x, part, :] for x in xs], mid),
                            [field[old, REACH + x, part, :] for x in xs],
                        )
                        value = add(
                            value,
                            [
                                pulses[slot, pl.ds(pl.multiple_of(x * height + q * 8, 8), 8), :]
                                for x in xs
                            ],
                        )
                        value = add(value, mul([square[x, part, :] for x in xs], lap))
                        drift = mul([gx[x, part, :] for x in xs], dx)
                        drift = add(drift, mul([gy[x, part, :] for x in xs], y1))
                        drift = add(drift, mul([gz[x, part, :] for x in xs], z1))
                        value = sub(value, drift)
                        if q == 0:
                            low = [
                                jnp.broadcast_to(rim[k, 0, pl.ds(x, 1), :], (8, lanes)) for x in xs
                            ]
                            value = each(lambda p, v: jnp.where(rim_low, p, v), low, value)
                        if q == rows8 - 1:
                            high = [
                                jnp.broadcast_to(rim[k, 1, pl.ds(x, 1), :], (8, lanes)) for x in xs
                            ]
                            value = each(lambda p, v: jnp.where(rim_high, p, v), high, value)
                        for i in range(4):
                            field[old, REACH + xs[i], part, :] = value[i]
                            record[slot, to, i, part, :] = value[i]
                store_ahead(following, 1 - bslot)

            @pl.when(jnp.logical_not(on))
            def _():
                field[old, pl.ds(REACH + w, BLOCK)] = jnp.zeros((BLOCK, height, lanes), jnp.float32)
                for g in range(groups):
                    half = jnp.where(half_of == g % 2, 0, cols)
                    to = jnp.where(is_own, half + (w - own_lo) // 8, 2 * cols)
                    record[slot, to] = jnp.zeros((4, height, lanes), jnp.float32)
                store_ahead(ahead(new, after, 0), 1 - bslot)

            return carry

        lax.fori_loop(first, last, block, 0)
        for copy in out_copies(k, slot):
            copy.start()
        return carry

    lax.fori_loop(0, steps, one_step, 0)
    for k in (steps - 2, steps - 1):
        for copy in out_copies(k, k % 2):
            copy.wait()


def image_kernel(owners, columns, stored, meta, owner_map, prints, keep, got, *refs):
    outs, total = refs[:owners], refs[owners]
    steps, cols, half, height, lanes = keep.shape
    brick_y = outs[0].shape[2]
    for c in range(cols):
        for i in range(half):

            def one(k, value, c=c, i=i):
                return value + keep[k, c, i] * got[k, c, i]

            total[c, i] = lax.fori_loop(0, steps, one, jnp.zeros((height, lanes), jnp.float32), unroll=4)
    for b in range(owners):
        base = ((meta[0] ^ b) * columns + meta[1]) * stored

        def take(m, local, rank, b=b):
            y = pl.multiple_of((m % KY) * brick_y, brick_y)
            for i in range(half):
                outs[b][rank, i] = total[m // KY, i, pl.ds(y, brick_y), :]

        serve(prints, owner_map, base, stored, take)


def sum_kernel(owners, columns, meta, owner_map, *refs):
    prints, blocks, out = refs[:owners], refs[owners : 2 * owners], refs[2 * owners]
    stored = out.shape[0]
    base = (meta[0] * columns + meta[1]) * stored
    out[...] = jnp.zeros_like(out)
    for b in range(owners):

        def take(m, local, rank, b=b):
            out[local] += blocks[b][rank]

        serve(prints[b], owner_map, base, stored, take)


def call(kernel, out_shape, in_specs, out_specs, scratch=(), mib=8, cost=None):
    return pl.pallas_call(
        kernel,
        out_shape=out_shape,
        in_specs=in_specs,
        out_specs=out_specs,
        scratch_shapes=list(scratch),
        compiler_params=pltpu.CompilerParams(vmem_limit_bytes=mib * MIB),
        cost_estimate=cost,
    )


def run_steps(shape, meta, owner_map, inject, prints, mine, theirs, states, rims):
    f32 = jnp.float32
    owners, columns, stored, sides, _ = shape
    count = len(states)
    steps = rims[0].shape[0]
    thick, height, lanes = states[0].shape[1:]
    cols = thick // 8
    window = count * thick
    kept = jax.ShapeDtypeStruct((steps, cols, 4, height, lanes), f32)
    grid = (window, height, lanes)
    padded = (window + 2 * REACH, height, lanes)
    bricks = [x for slab in mine for x in slab] + [x for slab in theirs for x in slab]
    return call(
        functools.partial(steps_kernel, shape),
        [kept, kept],
        [smem, smem, vmem, vmem, anywhere, anywhere]
        + [smem] * len(prints)
        + [vmem] * len(bricks)
        + [anywhere] * (2 * count),
        [anywhere, anywhere],
        [
            pltpu.VMEM((2,) + padded, f32),
            pltpu.VMEM(padded, f32),
            pltpu.VMEM(grid, f32),
            pltpu.VMEM(grid, f32),
            pltpu.VMEM(grid, f32),
            pltpu.VMEM(grid, f32),
            pltpu.VMEM(grid, f32),
            pltpu.VMEM((2, window * height, lanes), f32),
            pltpu.VMEM((2, BLOCK * height, 2 * lanes), f32),
            pltpu.VMEM((2, BLOCK // 4, 8 * height, lanes), f32),
            pltpu.VMEM((2, 2 * cols + 1, 4, height, lanes), f32),
            pltpu.VMEM((steps, 2, window, lanes), f32),
            pltpu.SemaphoreType.DMA((2,)),
            pltpu.SemaphoreType.DMA((2, 2)),
            pltpu.SemaphoreType.DMA((count, 3)),
        ],
        mib=12 + window // 4,
    )(
        meta, owner_map, z_matrix(lanes), y_matrix(height, 4), *inject, *prints, *bricks, *states, *rims
    )


def injection(window, offset, early, late, height, lanes, is_source, source_cell, receivers, pulses, recorded):
    steps, spots = recorded.shape
    none = jnp.full((spots - 1,), -1, jnp.int32)
    cells = jnp.where(is_source, jnp.concatenate([source_cell, none]), receivers)
    source_values = jnp.concatenate([-pulses[:, None], jnp.zeros((steps, spots - 1), jnp.float32)], axis=1)
    values = jnp.where(is_source, source_values, recorded)
    z = cells % lanes
    rows = cells // lanes - offset * height
    rows = jnp.where(cells >= 0, rows, -1)
    every = lax.broadcasted_iota(jnp.int32, (window * height, spots), 0)
    which_row = (every == rows[None, :]).astype(jnp.bfloat16)
    which_lane = (z[:, None] == lax.broadcasted_iota(jnp.int32, (spots, lanes), 1)).astype(jnp.float32)
    high = lax.reduce_precision(values, 8, 7)
    low = lax.reduce_precision(values - high, 8, 7)
    both = jnp.concatenate([high, low], axis=1)
    spread = both[:, :, None] * jnp.concatenate([which_lane, which_lane], axis=0)[None]
    spread = spread.astype(jnp.bfloat16)
    twice = jnp.concatenate([which_row, which_row], axis=1)

    def product(rows, spread):
        return jnp.einsum("rp,kpz->krz", rows, spread, preferred_element_type=jnp.float32)

    lo, hi = late
    return (
        product(twice, spread[:early]),
        product(twice[lo * height : hi * height], spread[early:]),
    )


def per_device(
    velocity,
    density,
    owner_map,
    footprint,
    aperture,
    source_cell,
    receiver_cells,
    wavelet,
    traces,
    states,
    stored_rims,
):
    f32 = jnp.float32
    owners = lax.axis_size("shot")
    columns = lax.axis_size("dom")
    column = lax.axis_index("dom")
    pair = lax.axis_index("pair")
    shot = lax.axis_index("shot")
    stored, brick_x, brick_y, lanes = velocity.shape
    half_x = brick_x // 2
    slots = footprint.shape[1]
    per_owner = slots // owners
    thick = slots // KY * brick_x
    height = KY * brick_y
    steps = wavelet.shape[1]
    sides = columns == 2
    meta = jnp.stack(
        [shot.astype(jnp.int32), column.astype(jnp.int32), pair.astype(jnp.int32), aperture[0] * brick_x]
    )

    prints = [footprint] + [xor_swap(footprint, "shot", b) for b in range(1, owners)]
    brick = jax.ShapeDtypeStruct((per_owner, brick_x, brick_y, lanes), f32)
    packed = call(
        functools.partial(pack_kernel, owners, columns, False),
        [brick] * (owners + 1),
        [smem] * (2 + owners) + [anywhere] * 2,
        [anywhere] * (owners + 1),
        [pltpu.SemaphoreType.DMA((owners + 1, per_owner))],
    )(meta, owner_map, *prints, velocity, density)
    got = [packed[0]] + [xor_swap(packed[b], "shot", b) for b in range(1, owners)]
    if sides:
        relay = xor_swap(jnp.where(pair == 0, velocity, density), "dom", 1)
        other_prints = xor_swap(jnp.concatenate(prints, axis=0), "dom", 1)
        other_prints = [other_prints[b : b + 1] for b in range(owners)]
        relayed = call(
            functools.partial(pack_kernel, owners, columns, True),
            [brick] * owners,
            [smem] * (2 + owners) + [anywhere],
            [anywhere] * owners,
            [pltpu.SemaphoreType.DMA((owners, per_owner))],
        )(meta, owner_map, *other_prints, relay)
        far = [relayed[0]] + [xor_swap(relayed[b], "shot", b) for b in range(1, owners)]
        mine = [got, far]
        theirs = [
            [packed[owners]] + [xor_swap(x, "pair", 1) for x in got[1:]],
            [xor_swap(x, "pair", 1) for x in far],
        ]
        shown = [prints[0], other_prints[0]]
        own_lo = column * thick
        offset = 0
        window = 2 * thick
        late = (0, window)
    else:
        table = call(
            functools.partial(unpack_kernel, owners, columns, stored),
            jax.ShapeDtypeStruct((slots, brick_x, brick_y, lanes), f32),
            [smem] * 3 + [vmem] * owners,
            vmem,
        )(meta, owner_map, prints[0], *got)
        mine = [[slab] for slab in slabs_of(table)]
        theirs = [[xor_swap(slab[0], "pair", 1)] for slab in mine]
        shown = []
        offset = (column - HOPS) * thick
        window = (2 * HOPS + 1) * thick
        deep = REACH * (steps - 1 - steps // 2)
        late = (HOPS * thick - deep, (HOPS + 1) * thick + deep)

    state_slabs = slabs_of(states[0, 0])
    rim_slabs = slabs_of(stored_rims[0], first_only=True)
    inject = injection(
        window, offset, steps // 2, late, height, lanes, pair == 0,
        source_cell, receiver_cells[0], wavelet[0], traces[0],
    )
    keep, send = run_steps(
        (owners, columns, stored, sides, late[0] * height),
        meta, owner_map, inject, shown, mine, theirs, state_slabs, rim_slabs,
    )
    partner = xor_swap(send, "pair", 1)

    part = jax.ShapeDtypeStruct((per_owner, half_x, brick_y, lanes), f32)
    images = call(
        functools.partial(image_kernel, owners, columns, stored),
        [part] * owners,
        [smem] * 3 + [vmem] * 2,
        [vmem] * owners,
        [pltpu.VMEM(keep.shape[1:], f32)],
        mib=16,
    )(meta, owner_map, prints[0], keep, partner)
    returned = [images[0]] + [xor_swap(images[b], "shot", b) for b in range(1, owners)]
    return call(
        functools.partial(sum_kernel, owners, columns),
        jax.ShapeDtypeStruct((stored, half_x, brick_y, lanes), f32),
        [smem] * (2 + owners) + [vmem] * owners,
        vmem,
    )(meta, owner_map, *prints, *returned)


def solution(mesh):
    placed = (
        P(("groups", "shot", "dom"), None, None, None),
        P(("groups", "shot", "dom"), None, None, None),
        P("groups"),
        P(("groups", "shot"), "dom"),
        P(("groups", "shot")),
        P(("groups", "shot")),
        P(("groups", "shot"), None),
        P(("groups", "shot"), None),
        P(("groups", "shot"), None, None),
        P(("groups", "shot"), "pair", None, "dom", None, None),
        P(("groups", "shot"), None, None, "dom", None),
    )
    return jax.shard_map(
        per_device,
        mesh=mesh,
        in_specs=placed,
        out_specs=P(("groups", "shot", "dom"), "pair", None, None),
        check_vma=False,
    )
```

time: 143 us -> 134 us (0.937)
  starting transfers between devices: 18.9 us -> 26.9 us
  Pallas kernels: 69 us -> 61.1 us
  waiting for transfers between devices: 31.6 us -> 25 us
  matrix products: 13.1 us -> 11.4 us
    ppermute x15 -> x22, waiting for transfers between devices: 31.6 us -> 22.2 us  [xor_swap(): return lax.ppermute(block, axis, [(i, i ^ bits) for i in range(size)])]
    pallas_call x5, Pallas kernels: 69 us -> 61.1 us  [the longest x1 50.6 us: run_steps(): call(functools.partial(steps_kernel, shape), [kept, kept], [smem, smem, v...]
    ppermute x15 -> x22, starting transfers between devices: 18.9 us -> 24 us  [xor_swap(): return lax.ppermute(block, axis, [(i, i ^ bits) for i in range(size)])]
    ppermute x0 -> x2, starting transfers between devices: none -> 2.89 us  [the longest x1 2.57 us: shift(): lax.ppermute(x, ('dom', 'pair'), [(i * pairs, j * pairs) for i, j in moves])]
    ppermute x0 -> x2, waiting for transfers between devices: none -> 2.75 us  [the longest x1 2.75 us: shift(): lax.ppermute(x, ('dom', 'pair'), [(i * pairs, j * pairs) for i, j in moves])]
    dot_general x2, matrix products: 13.1 us -> 11.4 us  [product(): jnp.einsum('rp,kpz->krz', rows, spread, preferred_element_type=jnp.float32)]
  transfers between devices with their start and end apart: 15 -> 24, of which waited for: 6 -> 7; matrix products, arithmetic and copies ran while one was open for 13% -> 12% of each run, Pallas kernels for 5% -> 4%
where the time goes in v3:
time: 134 us
  Pallas kernels  61.1 us (46%)
  starting transfers between devices  26.9 us (20%)
  waiting for transfers between devices  25 us (19%)
  matrix products  11.4 us (9%)
  other arithmetic  4.09 us (3%)
  local copies, waits for them, and re-layouts  3.98 us (3%)
  between operations  1.52 us (1%)
    pallas_call x1, Pallas kernels, run_steps(): call(functools.partial(steps_kernel, shape), [kept, kept], [smem, smem, v...  50.6 us
    ppermute x22, starting transfers between devices, xor_swap(): return lax.ppermute(block, axis, [(i, i ^ bits) for i in range(size)])  24 us
    ppermute x22, waiting for transfers between devices, xor_swap(): return lax.ppermute(block, axis, [(i, i ^ bits) for i in range(size)])  22.2 us
    dot_general x2, matrix products, product(): jnp.einsum('rp,kpz->krz', rows, spread, preferred_element_type=jnp.float32)  11.4 us
    unnamed x22, local copies, waits for them, and re-layouts  3.89 us
    pallas_call x1, Pallas kernels, per_device(): call(functools.partial(pack_kernel, owners, columns, False), [brick] * (o...  2.91 us
    ppermute x1, waiting for transfers between devices, shift(): lax.ppermute(x, ('dom', 'pair'), [(i * pairs, j * pairs) for i, j in moves])  2.75 us
  transfers between devices with their start and end apart: 24, of which 7 were waited for; matrix products, arithmetic and copies ran while one was open for 12% of the time, Pallas kernels for 4%

profile of v3, /device:TPU:0, one launch (start us, length us, event | category | flops | bytes accessed | tf_op | source)
XLA Modules:
  0.0 134.0 jit_solution(9871333051988269725)
XLA Ops:
  0.0 5.0 %collective-permute-start.2 = (s32[1,16]{1,0:T(1,128)}, s32[1,16]{1,0:T(1,128)S(1)}, u32[]{:S(2)}, u32[]{:S(2)}) collective-permute-start(s32[1,16]{1,0:T(1,128)} %refs_0_.5), channel_id=1, source_target_pairs={{0,12},{4,8},{8,4},{12,0},{1,13},{5,9},{9,5},{13,1},{2,14},{6,10},... | collective-permute-start | bytes 200 | tf_op jit(solution)/shard_map/ppermute | solution.py:68
  5.0 0.0 collective-permute-start.1
  5.1 0.6 collective-permute-start
  5.6 1.0 broadcast_select_fusion
  6.6 1.8 %collective-permute-start.7 = (f32[8,8,8,128]{3,2,1,0:T(8,128)S(1)}, f32[8,8,8,128]{3,2,1,0:T(8,128)S(1)}, u32[]{:S(2)}, u32[]{:S(2)}) collective-permute-start(f32[8,8,8,128]{3,2,1,0:T(8,128)S(1)} %broadcast_select_fusion), channel_id=1, source_target_pairs={{0,2},{2,0},{1,3},{3,1},{4,6},{6,4},{5,7},{7,5},{8,10},{10,8},{9,1... | collective-permute-start | bytes 786440 | tf_op jit(solution)/shard_map/ppermute | solution.py:68
  9.7 0.7 negate_bitcast_fusion
  10.3 0.1 copy.23
  10.5 0.1 add_convert_fusion
  10.6 0.8 iota_compare_fusion
  11.4 0.8 fusion.8
  12.2 0.1 pad_add_fusion.1.meta
  12.2 0.0 collective-permute-done.2.refs_3_
  12.2 0.0 collective-permute-done.1.refs_2_
  12.2 0.0 collective-permute-done.refs_1_
  12.2 0.0 copy-start.1
  12.3 0.9 copy-done.1
  13.2 0.9 copy-done.2
  14.2 0.7 copy-done.6
  14.8 0.7 copy-done.9
  15.5 2.9 %shard_map.127 = (f32[4,8,8,128]{3,2,1,0:T(8,128)S(1)}, f32[4,8,8,128]{3,2,1,0:T(8,128)S(1)}, f32[4,8,8,128]{3,2,1,0:T(8,128)S(1)}, f32[4,8,8,128]{3,2,1,0:T(8,128)S(1)}, f32[4,8,8,128]{3,2,1,0:T(8,128)S(1)}) custom-call(s32[4]{0:T(128)S(1)} %pad_add_fusion.1.meta, s32[64]{0:T(128)S(1)} %copy-done.6, s32[1,16]{1,0:T(1,128)S(1)} %copy-done.9, ...), custom_call_target="tpu_custom_call" | custom-call | tf_op jit(solution)/shard_map/pallas_call | solution.py:644
  18.4 1.3 collective-permute-start.4
  19.7 2.9 %collective-permute-start.5 = (f32[4,8,8,128]{3,2,1,0:T(8,128)S(1)}, f32[4,8,8,128]{3,2,1,0:T(8,128)S(1)}, u32[]{:S(2)}, u32[]{:S(2)}) collective-permute-start(f32[4,8,8,128]{3,2,1,0:T(8,128)S(1)} %get-tuple-element.22), channel_id=1, source_target_pairs={{0,8},{4,12},{8,0},{12,4},{1,9},{5,13},{9,1},{13,5},{2,10},{6,14},... | collective-permute-start | bytes 393224 | tf_op jit(solution)/shard_map/ppermute | solution.py:68
  22.6 0.2 collective-permute-start.6
  22.8 0.7 pad_add_fusion
  23.5 0.3 collective-permute-start.3
  23.8 3.3 %collective-permute-done.3 = s32[4,16]{1,0:T(4,128)S(1)} collective-permute-done((s32[4,16]{1,0:T(4,128)S(1)}, s32[4,16]{1,0:T(4,128)S(1)}, u32[]{:S(2)}, u32[]{:S(2)}) %collective-permute-start.3) | collective-permute-done | bytes 288 | tf_op jit(solution)/shard_map/ppermute | solution.py:68
  27.1 0.3 collective-permute-start.18
  27.4 0.0 collective-permute-done.4.refs_3_
  27.4 0.0 collective-permute-start.11
  27.4 5.0 %collective-permute-done.5.refs_4_ = f32[4,8,8,128]{3,2,1,0:T(8,128)S(1)} collective-permute-done((f32[4,8,8,128]{3,2,1,0:T(8,128)S(1)}, f32[4,8,8,128]{3,2,1,0:T(8,128)S(1)}, u32[]{:S(2)}, u32[]{:S(2)}) %collective-permute-start.5) | collective-permute-done | bytes 131104 | tf_op jit(solution)/shard_map/ppermute | solution.py:68
  32.4 0.0 collective-permute-start.12
  32.4 0.0 collective-permute-done.6.refs_5_
  32.4 0.5 collective-permute-start.13
  33.0 0.6 copy-done.7
  33.6 2.6 %shard_map.128 = (f32[4,8,8,128]{3,2,1,0:T(8,128)S(1)}, f32[4,8,8,128]{3,2,1,0:T(8,128)S(1)}, f32[4,8,8,128]{3,2,1,0:T(8,128)S(1)}, f32[4,8,8,128]{3,2,1,0:T(8,128)S(1)}) custom-call(s32[4]{0:T(128)S(1)} %pad_add_fusion.1.meta, s32[64]{0:T(128)S(1)} %copy-done.7, s32[1,16]{1,0:T(1,128)S(1)} %get-tuple-element.40.refs_0_.refs_1_, ...), custom_call_target="tpu_custom_call" | custom-call | tf_op jit(solution)/shard_map/pallas_call | solution.py:656
  36.2 1.5 %collective-permute-start.8 = (f32[4,8,8,128]{3,2,1,0:T(8,128)S(1)}, f32[4,8,8,128]{3,2,1,0:T(8,128)S(1)}, u32[]{:S(2)}, u32[]{:S(2)}) collective-permute-start(f32[4,8,8,128]{3,2,1,0:T(8,128)S(1)} %get-tuple-element.25), channel_id=1, source_target_pairs={{0,4},{4,0},{8,12},{12,8},{1,5},{5,1},{9,13},{13,9},{2,6},{6,2},{1... | collective-permute-start | bytes 393224 | tf_op jit(solution)/shard_map/ppermute | solution.py:68
  37.7 0.0 collective-permute-done.11.refs_11_
  37.8 1.5 %collective-permute-start.9 = (f32[4,8,8,128]{3,2,1,0:T(8,128)S(1)}, f32[4,8,8,128]{3,2,1,0:T(8,128)S(1)}, u32[]{:S(2)}, u32[]{:S(2)}) collective-permute-start(f32[4,8,8,128]{3,2,1,0:T(8,128)S(1)} %get-tuple-element.26), channel_id=1, source_target_pairs={{0,8},{4,12},{8,0},{12,4},{1,9},{5,13},{9,1},{13,5},{2,10},{6,14},... | collective-permute-start | bytes 393224 | tf_op jit(solution)/shard_map/ppermute | solution.py:68
  39.3 1.4 %collective-permute-start.10 = (f32[4,8,8,128]{3,2,1,0:T(8,128)S(1)}, f32[4,8,8,128]{3,2,1,0:T(8,128)S(1)}, u32[]{:S(2)}, u32[]{:S(2)}) collective-permute-start(f32[4,8,8,128]{3,2,1,0:T(8,128)S(1)} %get-tuple-element.27), channel_id=1, source_target_pairs={{0,12},{4,8},{8,4},{12,0},{1,13},{5,9},{9,5},{13,1},{2,14},{6,10},... | collective-permute-start | bytes 393224 | tf_op jit(solution)/shard_map/ppermute | solution.py:68
  40.7 0.0 collective-permute-done.13.refs_13_
  40.7 6.7 %fusion.3.inject_b = f32[8,2048,128]{2,1,0:T(8,128)} fusion(pred[2048,512]{1,0:T(32,128)(4,1)S(1)} %iota_compare_fusion, f32[1024,128]{0,1:T(8,128)S(1)} %add_convert_fusion, f32[16,1024]{1,0:T(8,128)S(1)} %pad_maximum_fusion), kind=kOutput, calls=%fused_computation.5 | convolution fusion | flops 4301258752 | bytes 10027008 | tf_op jit(solution)/shard_map/rp,kpz->krz/dot_general | solution.py:602
  47.4 0.0 copy-start.4
  47.5 0.0 copy-start.5
  47.5 0.0 copy-start.8
  47.5 0.0 copy-start.10
  47.5 2.6 %collective-permute-start.19 = (f32[16,2,32,128]{3,2,1,0:T(8,128)S(1)}, f32[16,2,32,128]{3,2,1,0:T(8,128)S(1)}, u32[]{:S(2)}, u32[]{:S(2)}) collective-permute-start(f32[16,2,32,128]{3,2,1,0:T(8,128)S(1)} %bitcast.30), channel_id=1, source_target_pairs={{0,2},{2,0},{4,6},{6,4},{8,10},{10,8},{12,14},{14,12},{16,18},{18,... | collective-permute-start | bytes 1572872 | tf_op jit(solution)/shard_map/ppermute | solution.py:77
  50.1 0.6 collective-permute-done.9.refs_8_
  50.6 0.0 collective-permute-start.15
  50.6 0.0 collective-permute-done.10.refs_9_
  50.7 0.5 collective-permute-start.16
  51.2 0.0 collective-permute-done.14.refs_14_
  51.2 0.1 collective-permute-start.17
  51.2 4.7 %fusion.2.inject_a = f32[8,2048,128]{2,1,0:T(8,128)S(1)} fusion(pred[2048,512]{1,0:T(32,128)(4,1)S(1)} %iota_compare_fusion, f32[1024,128]{0,1:T(8,128)S(1)} %add_convert_fusion, f32[16,1024]{1,0:T(8,128)S(1)} %pad_maximum_fusion), kind=kOutput, calls=%fused_computation.4 | convolution fusion | flops 4301258752 | bytes 10027008 | tf_op jit(solution)/shard_map/rp,kpz->krz/dot_general | solution.py:602
  55.9 0.0 collective-permute-done.16.refs_16_
  56.0 2.8 %collective-permute-done.19.refs_21_ = f32[16,2,32,128]{3,2,1,0:T(8,128)S(1)} collective-permute-done((f32[16,2,32,128]{3,2,1,0:T(8,128)S(1)}, f32[16,2,32,128]{3,2,1,0:T(8,128)S(1)}, u32[]{:S(2)}, u32[]{:S(2)}) %collective-permute-start.19) | collective-permute-done | bytes 524320 | tf_op jit(solution)/shard_map/ppermute | solution.py:77
  58.7 50.6 %shard_map.129 = (f32[16,4,4,32,128]{4,3,2,1,0:T(8,128)S(1)}, f32[16,4,4,32,128]{4,3,2,1,0:T(8,128)S(1)}) custom-call(s32[4]{0:T(128)S(1)} %pad_add_fusion.1.meta, s32[64]{0:T(128)S(1)} %copy-done.8, bf16[256,256]{1,0:T(8,128)(2,1)S(1)} %copy-done.5, bf16[256,256]{1,0:T(8,128)(2,1)S(1)} %copy-done.4, f32[8,2048,128]{2,1,0:T(8,128)S(1)} %fusion.2.inject_a, ...), custom_call_target="tpu_custom_call" | custom-call | tf_op jit(solution)/shard_map/pallas_call | solution.py:551
  109.4 0.1 collective-permute-start.20
  109.5 7.1 %collective-permute-done.20.got = f32[16,4,4,32,128]{4,3,2,1,0:T(8,128)S(1)} collective-permute-done((f32[16,4,4,32,128]{4,3,2,1,0:T(8,128)S(1)}, f32[16,4,4,32,128]{4,3,2,1,0:T(8,128)S(1)}, u32[]{:S(2)}, u32[]{:S(2)}) %collective-permute-start.20) | collective-permute-done | bytes 4194336 | tf_op jit(solution)/shard_map/ppermute | solution.py:68
  116.6 2.5 %shard_map.130 = (f32[4,4,8,128]{3,2,1,0:T(8,128)S(1)}, f32[4,4,8,128]{3,2,1,0:T(8,128)S(1)}, f32[4,4,8,128]{3,2,1,0:T(8,128)S(1)}, f32[4,4,8,128]{3,2,1,0:T(8,128)S(1)}) custom-call(s32[4]{0:T(128)S(1)} %pad_add_fusion.1.meta, s32[64]{0:T(128)S(1)} %copy-done.8, s32[1,16]{1,0:T(1,128)S(1)} %copy-done.10, f32[16,4,4,32,128]{4,3,2,1,0:T(8,128)S(1)} %get-tuple-element.29.keep, ...), custom_call_target="tpu_custom_call" | custom-call | tf_op jit(solution)/shard_map/pallas_call | solution.py:702
  119.1 2.5 %collective-permute-start.21 = (f32[4,4,8,128]{3,2,1,0:T(8,128)S(1)}, f32[4,4,8,128]{3,2,1,0:T(8,128)S(1)}, u32[]{:S(2)}, u32[]{:S(2)}) collective-permute-start(f32[4,4,8,128]{3,2,1,0:T(8,128)S(1)} %get-tuple-element.32), channel_id=1, source_target_pairs={{0,4},{4,0},{8,12},{12,8},{1,5},{5,1},{9,13},{13,9},{2,6},{6,2},{1... | collective-permute-start | bytes 196616 | tf_op jit(solution)/shard_map/ppermute | solution.py:68
  121.6 3.7 %collective-permute-start.22 = (f32[4,4,8,128]{3,2,1,0:T(8,128)S(1)}, f32[4,4,8,128]{3,2,1,0:T(8,128)S(1)}, u32[]{:S(2)}, u32[]{:S(2)}) collective-permute-start(f32[4,4,8,128]{3,2,1,0:T(8,128)S(1)} %get-tuple-element.33), channel_id=1, source_target_pairs={{0,8},{4,12},{8,0},{12,4},{1,9},{5,13},{9,1},{13,5},{2,10},{6,14},... | collective-permute-start | bytes 196616 | tf_op jit(solution)/shard_map/ppermute | solution.py:68
  125.4 4.0 %collective-permute-done.22.refs_6_ = f32[4,4,8,128]{3,2,1,0:T(8,128)S(1)} collective-permute-done((f32[4,4,8,128]{3,2,1,0:T(8,128)S(1)}, f32[4,4,8,128]{3,2,1,0:T(8,128)S(1)}, u32[]{:S(2)}, u32[]{:S(2)}) %collective-permute-start.22) | collective-permute-done | bytes 65568 | tf_op jit(solution)/shard_map/ppermute | solution.py:68
  129.4 2.1 %collective-permute-done.23.refs_7_ = f32[4,4,8,128]{3,2,1,0:T(8,128)S(1)} collective-permute-done((f32[4,4,8,128]{3,2,1,0:T(8,128)S(1)}, f32[4,4,8,128]{3,2,1,0:T(8,128)S(1)}, u32[]{:S(2)}, u32[]{:S(2)}) %collective-permute-start.23) | collective-permute-done | bytes 65568 | tf_op jit(solution)/shard_map/ppermute | solution.py:68
  131.5 2.5 %shard_map.131 = f32[8,4,8,128]{3,2,1,0:T(8,128)} custom-call(s32[4]{0:T(128)S(1)} %pad_add_fusion.1.meta, s32[64]{0:T(128)S(1)} %copy-done.8, s32[1,16]{1,0:T(1,128)S(1)} %copy-done.10, s32[1,16]{1,0:T(1,128)S(1)} %collective-permute-done.refs_1_, s32[1,16]{1,0:T(1,128)S(1)} %collective-permute-done.1.refs_2_, s32[1,16]{1,0:T(1,128)S(1)} %collective-permute-done.2.refs_3_, ...), custom_call_target="tpu_custom_call" | custom-call | tf_op jit(solution)/shard_map/pallas_call | solution.py:711
  (25 shorter events, 0.1 us)
Async XLA Ops:
  0.0 12.2 %collective-permute-start.2 = (s32[1,16]{1,0:T(1,128)}, s32[1,16]{1,0:T(1,128)S(1)}, u32[]{:S(2)}, u32[]{:S(2)}) collective-permute-start(s32[1,16]{1,0:T(1,128)} %refs_0_.5), channel_id=1, source_target_pairs={{0,12},{4,8},{8,4},{12,0},{1,13},{5,9},{9,5},{13,1},{2,14},{6,10},... | collective-permute-start | bytes 200 | tf_op jit(solution)/shard_map/ppermute | solution.py:68
  5.0 7.2 %collective-permute-start.1 = (s32[1,16]{1,0:T(1,128)}, s32[1,16]{1,0:T(1,128)S(1)}, u32[]{:S(2)}, u32[]{:S(2)}) collective-permute-start(s32[1,16]{1,0:T(1,128)} %refs_0_.5), channel_id=1, source_target_pairs={{0,8},{4,12},{8,0},{12,4},{1,9},{5,13},{9,1},{13,5},{2,10},{6,14},... | collective-permute-start | bytes 200 | tf_op jit(solution)/shard_map/ppermute | solution.py:68
  5.1 7.2 %collective-permute-start = (s32[1,16]{1,0:T(1,128)}, s32[1,16]{1,0:T(1,128)S(1)}, u32[]{:S(2)}, u32[]{:S(2)}) collective-permute-start(s32[1,16]{1,0:T(1,128)} %refs_0_.5), channel_id=1, source_target_pairs={{0,4},{4,0},{8,12},{12,8},{1,5},{5,1},{9,13},{13,9},{2,6},{6,2},{1... | collective-permute-start | bytes 200 | tf_op jit(solution)/shard_map/ppermute | solution.py:68
  6.6 26.4 %collective-permute-start.7 = (f32[8,8,8,128]{3,2,1,0:T(8,128)S(1)}, f32[8,8,8,128]{3,2,1,0:T(8,128)S(1)}, u32[]{:S(2)}, u32[]{:S(2)}) collective-permute-start(f32[8,8,8,128]{3,2,1,0:T(8,128)S(1)} %broadcast_select_fusion), channel_id=1, source_target_pairs={{0,2},{2,0},{1,3},{3,1},{4,6},{6,4},{5,7},{7,5},{8,10},{10,8},{9,1... | collective-permute-start | bytes 786440 | tf_op jit(solution)/shard_map/ppermute | solution.py:68
  12.2 1.0 copy-start.1
  13.2 0.9 copy-start.2
  14.1 0.7 copy-start.6
  14.8 0.7 copy-start.9
  18.4 9.0 %collective-permute-start.4 = (f32[4,8,8,128]{3,2,1,0:T(8,128)S(1)}, f32[4,8,8,128]{3,2,1,0:T(8,128)S(1)}, u32[]{:S(2)}, u32[]{:S(2)}) collective-permute-start(f32[4,8,8,128]{3,2,1,0:T(8,128)S(1)} %get-tuple-element.21), channel_id=1, source_target_pairs={{0,4},{4,0},{8,12},{12,8},{1,5},{5,1},{9,13},{13,9},{2,6},{6,2},{1... | collective-permute-start | bytes 393224 | tf_op jit(solution)/shard_map/ppermute | solution.py:68
  19.7 12.7 %collective-permute-start.5 = (f32[4,8,8,128]{3,2,1,0:T(8,128)S(1)}, f32[4,8,8,128]{3,2,1,0:T(8,128)S(1)}, u32[]{:S(2)}, u32[]{:S(2)}) collective-permute-start(f32[4,8,8,128]{3,2,1,0:T(8,128)S(1)} %get-tuple-element.22), channel_id=1, source_target_pairs={{0,8},{4,12},{8,0},{12,4},{1,9},{5,13},{9,1},{13,5},{2,10},{6,14},... | collective-permute-start | bytes 393224 | tf_op jit(solution)/shard_map/ppermute | solution.py:68
  22.6 9.8 %collective-permute-start.6 = (f32[4,8,8,128]{3,2,1,0:T(8,128)S(1)}, f32[4,8,8,128]{3,2,1,0:T(8,128)S(1)}, u32[]{:S(2)}, u32[]{:S(2)}) collective-permute-start(f32[4,8,8,128]{3,2,1,0:T(8,128)S(1)} %get-tuple-element.23), channel_id=1, source_target_pairs={{0,12},{4,8},{8,4},{12,0},{1,13},{5,9},{9,5},{13,1},{2,14},{6,10},... | collective-permute-start | bytes 393224 | tf_op jit(solution)/shard_map/ppermute | solution.py:68
  23.5 3.6 %collective-permute-start.3 = (s32[4,16]{1,0:T(4,128)S(1)}, s32[4,16]{1,0:T(4,128)S(1)}, u32[]{:S(2)}, u32[]{:S(2)}) collective-permute-start(s32[4,16]{1,0:T(4,128)S(1)} %pad_add_fusion), channel_id=1, source_target_pairs={{0,2},{2,0},{1,3},{3,1},{4,6},{6,4},{5,7},{7,5},{8,10},{10,8},{9,1... | collective-permute-start | bytes 776 | tf_op jit(solution)/shard_map/ppermute | solution.py:68
  27.1 31.6 %collective-permute-start.18 = (f32[2,32,32,128]{3,2,1,0:T(8,128)}, f32[2,32,32,128]{3,2,1,0:T(8,128)S(1)}, u32[]{:S(2)}, u32[]{:S(2)}) collective-permute-start(f32[2,32,32,128]{3,2,1,0:T(8,128)} %bitcast.28), channel_id=1, source_target_pairs={{0,2},{2,0},{1,3},{3,1},{4,6},{6,4},{5,7},{7,5},{8,10},{10,8},{9,1... | collective-permute-start | bytes 3145736 | tf_op jit(solution)/shard_map/ppermute | solution.py:78
  27.4 10.3 %collective-permute-start.11 = (f32[4,8,8,128]{3,2,1,0:T(8,128)S(1)}, f32[4,8,8,128]{3,2,1,0:T(8,128)S(1)}, u32[]{:S(2)}, u32[]{:S(2)}) collective-permute-start(f32[4,8,8,128]{3,2,1,0:T(8,128)S(1)} %collective-permute-done.4.refs_3_), channel_id=1, source_target_pairs={{0,1},{1,0},{2,3},{3,2},{4,5},{5,4},{6,7},{7,6},{8,9},{9,8},{10,11... | collective-permute-start | bytes 393224 | tf_op jit(solution)/shard_map/ppermute | solution.py:68
  32.4 6.8 %collective-permute-start.12 = (f32[4,8,8,128]{3,2,1,0:T(8,128)S(1)}, f32[4,8,8,128]{3,2,1,0:T(8,128)S(1)}, u32[]{:S(2)}, u32[]{:S(2)}) collective-permute-start(f32[4,8,8,128]{3,2,1,0:T(8,128)S(1)} %collective-permute-done.5.refs_4_), channel_id=1, source_target_pairs={{0,1},{1,0},{2,3},{3,2},{4,5},{5,4},{6,7},{7,6},{8,9},{9,8},{10,11... | collective-permute-start | bytes 393224 | tf_op jit(solution)/shard_map/ppermute | solution.py:68
  32.4 8.2 %collective-permute-start.13 = (f32[4,8,8,128]{3,2,1,0:T(8,128)S(1)}, f32[4,8,8,128]{3,2,1,0:T(8,128)S(1)}, u32[]{:S(2)}, u32[]{:S(2)}) collective-permute-start(f32[4,8,8,128]{3,2,1,0:T(8,128)S(1)} %collective-permute-done.6.refs_5_), channel_id=1, source_target_pairs={{0,1},{1,0},{2,3},{3,2},{4,5},{5,4},{6,7},{7,6},{8,9},{9,8},{10,11... | collective-permute-start | bytes 393224 | tf_op jit(solution)/shard_map/ppermute | solution.py:68
  33.0 0.7 copy-start.7
  36.2 11.2 %collective-permute-start.8 = (f32[4,8,8,128]{3,2,1,0:T(8,128)S(1)}, f32[4,8,8,128]{3,2,1,0:T(8,128)S(1)}, u32[]{:S(2)}, u32[]{:S(2)}) collective-permute-start(f32[4,8,8,128]{3,2,1,0:T(8,128)S(1)} %get-tuple-element.25), channel_id=1, source_target_pairs={{0,4},{4,0},{8,12},{12,8},{1,5},{5,1},{9,13},{13,9},{2,6},{6,2},{1... | collective-permute-start | bytes 393224 | tf_op jit(solution)/shard_map/ppermute | solution.py:68
  37.8 12.9 %collective-permute-start.9 = (f32[4,8,8,128]{3,2,1,0:T(8,128)S(1)}, f32[4,8,8,128]{3,2,1,0:T(8,128)S(1)}, u32[]{:S(2)}, u32[]{:S(2)}) collective-permute-start(f32[4,8,8,128]{3,2,1,0:T(8,128)S(1)} %get-tuple-element.26), channel_id=1, source_target_pairs={{0,8},{4,12},{8,0},{12,4},{1,9},{5,13},{9,1},{13,5},{2,10},{6,14},... | collective-permute-start | bytes 393224 | tf_op jit(solution)/shard_map/ppermute | solution.py:68
  39.3 11.4 %collective-permute-start.10 = (f32[4,8,8,128]{3,2,1,0:T(8,128)S(1)}, f32[4,8,8,128]{3,2,1,0:T(8,128)S(1)}, u32[]{:S(2)}, u32[]{:S(2)}) collective-permute-start(f32[4,8,8,128]{3,2,1,0:T(8,128)S(1)} %get-tuple-element.27), channel_id=1, source_target_pairs={{0,12},{4,8},{8,4},{12,0},{1,13},{5,9},{9,5},{13,1},{2,14},{6,10},... | collective-permute-start | bytes 393224 | tf_op jit(solution)/shard_map/ppermute | solution.py:68
  40.7 6.8 %copy-start.3 = (f32[1,16,2,32,128]{4,3,2,1,0:T(8,128)S(1)}, f32[1,16,2,32,128]{4,3,2,1,0:T(8,128)}, u32[]{:S(2)}) copy-start(f32[1,16,2,32,128]{4,3,2,1,0:T(8,128)} %param.23) | copy-start | bytes 1572868
  40.7 10.5 %collective-permute-start.14 = (f32[4,8,8,128]{3,2,1,0:T(8,128)S(1)}, f32[4,8,8,128]{3,2,1,0:T(8,128)S(1)}, u32[]{:S(2)}, u32[]{:S(2)}) collective-permute-start(f32[4,8,8,128]{3,2,1,0:T(8,128)S(1)} %get-tuple-element.24.refs_6_), channel_id=1, source_target_pairs={{0,1},{1,0},{2,3},{3,2},{4,5},{5,4},{6,7},{7,6},{8,9},{9,8},{10,11... | collective-permute-start | bytes 393224 | tf_op jit(solution)/shard_map/ppermute | solution.py:68
  47.4 11.3 %copy-start = (f32[1,1,2,32,32,128]{5,4,3,2,1,0:T(8,128)S(1)}, f32[1,1,2,32,32,128]{5,4,3,2,1,0:T(8,128)}, u32[]{:S(2)}) copy-start(f32[1,1,2,32,32,128]{5,4,3,2,1,0:T(8,128)} %param.22) | copy-start | bytes 3145732
  47.4 11.3 %copy-start.4 = (bf16[256,256]{1,0:T(8,128)(2,1)S(1)}, bf16[256,256]{1,0:T(8,128)(2,1)}, u32[]{:S(2)}) copy-start(bf16[256,256]{1,0:T(8,128)(2,1)} %constant.53.clone.ymat) | copy-start | bytes 393220
  47.5 11.3 %copy-start.5 = (bf16[256,256]{1,0:T(8,128)(2,1)S(1)}, bf16[256,256]{1,0:T(8,128)(2,1)}, u32[]{:S(2)}) copy-start(bf16[256,256]{1,0:T(8,128)(2,1)} %constant.52.clone.zmat) | copy-start | bytes 393220
  47.5 11.3 %copy-start.8 = (s32[64]{0:T(128)S(1)}, s32[64]{0:T(128)}, u32[]{:S(2)}) copy-start(s32[64]{0:T(128)} %owner_map.9) | copy-start | bytes 772
  47.5 11.3 %copy-start.10 = (s32[1,16]{1,0:T(1,128)S(1)}, s32[1,16]{1,0:T(1,128)}, u32[]{:S(2)}) copy-start(s32[1,16]{1,0:T(1,128)} %refs_0_.5) | copy-start | bytes 196
  47.5 11.2 %collective-permute-start.19 = (f32[16,2,32,128]{3,2,1,0:T(8,128)S(1)}, f32[16,2,32,128]{3,2,1,0:T(8,128)S(1)}, u32[]{:S(2)}, u32[]{:S(2)}) collective-permute-start(f32[16,2,32,128]{3,2,1,0:T(8,128)S(1)} %bitcast.30), channel_id=1, source_target_pairs={{0,2},{2,0},{4,6},{6,4},{8,10},{10,8},{12,14},{14,12},{16,18},{18,... | collective-permute-start | bytes 1572872 | tf_op jit(solution)/shard_map/ppermute | solution.py:77
  50.6 5.3 %collective-permute-start.15 = (f32[4,8,8,128]{3,2,1,0:T(8,128)S(1)}, f32[4,8,8,128]{3,2,1,0:T(8,128)S(1)}, u32[]{:S(2)}, u32[]{:S(2)}) collective-permute-start(f32[4,8,8,128]{3,2,1,0:T(8,128)S(1)} %collective-permute-done.8.refs_7_), channel_id=1, source_target_pairs={{0,1},{1,0},{2,3},{3,2},{4,5},{5,4},{6,7},{7,6},{8,9},{9,8},{10,11... | collective-permute-start | bytes 393224 | tf_op jit(solution)/shard_map/ppermute | solution.py:68
  50.7 5.3 %collective-permute-start.16 = (f32[4,8,8,128]{3,2,1,0:T(8,128)S(1)}, f32[4,8,8,128]{3,2,1,0:T(8,128)S(1)}, u32[]{:S(2)}, u32[]{:S(2)}) collective-permute-start(f32[4,8,8,128]{3,2,1,0:T(8,128)S(1)} %collective-permute-done.9.refs_8_), channel_id=1, source_target_pairs={{0,1},{1,0},{2,3},{3,2},{4,5},{5,4},{6,7},{7,6},{8,9},{9,8},{10,11... | collective-permute-start | bytes 393224 | tf_op jit(solution)/shard_map/ppermute | solution.py:68
  51.2 4.8 %collective-permute-start.17 = (f32[4,8,8,128]{3,2,1,0:T(8,128)S(1)}, f32[4,8,8,128]{3,2,1,0:T(8,128)S(1)}, u32[]{:S(2)}, u32[]{:S(2)}) collective-permute-start(f32[4,8,8,128]{3,2,1,0:T(8,128)S(1)} %collective-permute-done.10.refs_9_), channel_id=1, source_target_pairs={{0,1},{1,0},{2,3},{3,2},{4,5},{5,4},{6,7},{7,6},{8,9},{9,8},{10,11... | collective-permute-start | bytes 393224 | tf_op jit(solution)/shard_map/ppermute | solution.py:68
  109.4 7.2 %collective-permute-start.20 = (f32[16,4,4,32,128]{4,3,2,1,0:T(8,128)S(1)}, f32[16,4,4,32,128]{4,3,2,1,0:T(8,128)S(1)}, u32[]{:S(2)}, u32[]{:S(2)}) collective-permute-start(f32[16,4,4,32,128]{4,3,2,1,0:T(8,128)S(1)} %get-tuple-element.30), channel_id=1, source_target_pairs={{0,1},{1,0},{2,3},{3,2},{4,5},{5,4},{6,7},{7,6},{8,9},{9,8},{10,11... | collective-permute-start | bytes 12582920 | tf_op jit(solution)/shard_map/ppermute | solution.py:68
  119.1 6.2 %collective-permute-start.21 = (f32[4,4,8,128]{3,2,1,0:T(8,128)S(1)}, f32[4,4,8,128]{3,2,1,0:T(8,128)S(1)}, u32[]{:S(2)}, u32[]{:S(2)}) collective-permute-start(f32[4,4,8,128]{3,2,1,0:T(8,128)S(1)} %get-tuple-element.32), channel_id=1, source_target_pairs={{0,4},{4,0},{8,12},{12,8},{1,5},{5,1},{9,13},{13,9},{2,6},{6,2},{1... | collective-permute-start | bytes 196616 | tf_op jit(solution)/shard_map/ppermute | solution.py:68
  121.6 7.8 %collective-permute-start.22 = (f32[4,4,8,128]{3,2,1,0:T(8,128)S(1)}, f32[4,4,8,128]{3,2,1,0:T(8,128)S(1)}, u32[]{:S(2)}, u32[]{:S(2)}) collective-permute-start(f32[4,4,8,128]{3,2,1,0:T(8,128)S(1)} %get-tuple-element.33), channel_id=1, source_target_pairs={{0,8},{4,12},{8,0},{12,4},{1,9},{5,13},{9,1},{13,5},{2,10},{6,14},... | collective-permute-start | bytes 196616 | tf_op jit(solution)/shard_map/ppermute | solution.py:68
  125.3 6.2 %collective-permute-start.23 = (f32[4,4,8,128]{3,2,1,0:T(8,128)S(1)}, f32[4,4,8,128]{3,2,1,0:T(8,128)S(1)}, u32[]{:S(2)}, u32[]{:S(2)}) collective-permute-start(f32[4,4,8,128]{3,2,1,0:T(8,128)S(1)} %get-tuple-element.34), channel_id=1, source_target_pairs={{0,12},{4,8},{8,4},{12,0},{1,13},{5,9},{9,5},{13,1},{2,14},{6,10},... | collective-permute-start | bytes 196616 | tf_op jit(solution)/shard_map/ppermute | solution.py:68

commit v4 on v3

v4 whole, which is shorter than its diff:
```python
import functools

import jax
import jax.numpy as jnp
import numpy as np
from jax import lax
from jax.experimental import pallas as pl
from jax.experimental.pallas import tpu as pltpu
from jax.sharding import PartitionSpec as P

KY = 4
REACH = 4

first_weights = (0.8, -0.2, 4.0 / 105.0, -1.0 / 280.0)
second_weights = (-205.0 / 72.0, 1.6, -0.2, 8.0 / 315.0, -1.0 / 560.0)

FIRST = first_weights[0]
SECOND = second_weights[1]
first_ratio = tuple(w / FIRST for w in first_weights)
second_ratio = tuple(w / SECOND for w in second_weights[1:])

SECOND_UNIT = 8064.0
FIRST_UNIT = 672.0
second_whole = (8064.0, -1008.0, 128.0, -9.0)
first_whole = (672.0, -168.0, 32.0, -3.0)

HOPS = 2
META = 4
MIB = 1024 * 1024

smem = pl.BlockSpec(memory_space=pltpu.SMEM)
vmem = pl.BlockSpec(memory_space=pltpu.VMEM)
anywhere = pl.BlockSpec(memory_space=pl.ANY)


def z_matrix(size):
    second = np.zeros((size, size))
    first = np.zeros((size, size))
    for r in range(1, REACH + 1):
        for z in range(size):
            if z + r < size:
                second[z + r, z] = second_whole[r - 1]
                first[z + r, z] = first_whole[r - 1]
            if z - r >= 0:
                second[z - r, z] = second_whole[r - 1]
                first[z - r, z] = -first_whole[r - 1]
    whole = np.concatenate([second, first], axis=1)
    return np.concatenate([whole, whole], axis=0).astype(jnp.bfloat16)


def y_matrix(across, layers):
    second = np.zeros((across, across))
    first = np.zeros((across, across))
    for r in range(1, REACH + 1):
        for y in range(across):
            if y + r < across:
                second[y, y + r] = second_whole[r - 1]
                first[y, y + r] = first_whole[r - 1]
            if y - r >= 0:
                second[y, y - r] = second_whole[r - 1]
                first[y, y - r] = -first_whole[r - 1]
    same = np.eye(layers)
    whole = np.concatenate([np.kron(same, second), np.kron(same, first)], axis=0)
    return np.concatenate([whole, whole], axis=1).astype(jnp.bfloat16)


def xor_swap(block, axis, bits):
    size = lax.axis_size(axis)
    return lax.ppermute(block, axis, [(i, i ^ bits) for i in range(size)])


def slabs_of(block, first_only=False):
    size = lax.axis_size("dom")
    pairs = lax.axis_size("pair")

    def shift(x, moves):
        if first_only:
            return lax.ppermute(x, ("dom", "pair"), [(i * pairs, j * pairs) for i, j in moves])
        return lax.ppermute(x, "dom", moves)

    if size == 1:
        return [block]
    if size == 2:
        return [block, shift(block, [(0, 1), (1, 0)])]
    up = [(i, i + 1) for i in range(size - 1)]
    down = [(i + 1, i) for i in range(size - 1)]
    found = [block]
    left = right = block
    for _ in range(HOPS):
        left = shift(left, up)
        right = shift(right, down)
        found = [left] + found + [right]
    return found


def serve(info, bricks, slots, wanted, stored, take):
    def one(m, counts):
        after = []
        for b, (at, base) in enumerate(wanted):
            local = info[META + info[META + bricks + at * slots + m]] - base
            mine = (local >= 0) & (local < stored)

            @pl.when(mine)
            def _(b=b, local=local):
                take(b, m, local, counts[b])

            after.append(counts[b] + mine.astype(jnp.int32))
        return tuple(after)

    lax.fori_loop(0, slots, one, (jnp.int32(0),) * len(wanted))


def pack_kernel(owners, columns, tables, info, table, *refs):
    outs, sems = refs[:-1], refs[-1]
    stored = table.shape[0]
    per_owner = outs[0].shape[0]
    base = (info[0] * columns + info[1]) * stored

    def take(b, m, local, rank):
        pltpu.make_async_copy(table.at[local], outs[b].at[rank], sems.at[b, rank]).start()

    serve(info, *tables, [(b, base) for b in range(owners)], stored, take)
    for b, out in enumerate(outs):
        for rank in range(per_owner):
            pltpu.make_async_copy(table.at[0], out.at[rank], sems.at[b, rank]).wait()


def unpack_kernel(owners, columns, tables, stored, info, *refs):
    blocks, out = refs[:-1], refs[-1]

    def take(b, m, local, rank):
        out[m] = blocks[b][rank]

    serve(info, *tables, sources(owners, columns, stored, info), stored, take)


def sources(owners, columns, stored, info):
    return [(0, ((info[0] ^ b) * columns + info[1]) * stored) for b in range(owners)]


def each(f, *lists):
    return [f(*items) for items in zip(*lists)]


def add(a, b):
    return each(lambda p, q: p + q, a, b)


def sub(a, b):
    return each(lambda p, q: p - q, a, b)


def mul(a, b):
    return each(lambda p, q: p * q, a, b)


def scaled(factor, a):
    return [factor * p for p in a]


def along_x(column):
    size = len(column) - 2 * REACH
    lap = slope = None
    for r in range(1, REACH + 1):
        ahead = column[REACH + r : REACH + r + size]
        behind = column[REACH - r : REACH - r + size]
        total, apart = add(ahead, behind), sub(ahead, behind)
        if r == 1:
            lap, slope = total, apart
        else:
            lap = add(lap, scaled(second_ratio[r - 1], total))
            slope = add(slope, scaled(first_ratio[r - 1], apart))
    return lap, slope


def z_slopes(high, low, zmat):
    both = jnp.concatenate([high, low], axis=1)
    return jnp.dot(both, zmat[...], preferred_element_type=jnp.float32)


def y_slopes(high, low, ymat):
    both = jnp.concatenate([high, low], axis=0)
    return jnp.dot(ymat[...], both, preferred_element_type=jnp.float32)


BLOCK = 16


def make_coefficients(
    mine, theirs, places, active, is_source, zmat, ymat, field, logs, square, centre, gx, gy, gz
):
    window, height, lanes = square.shape
    rows8 = height // 8
    zero = jnp.zeros((REACH, height, lanes), jnp.float32)
    for level in range(2):
        field[level, 0:REACH] = zero
        field[level, REACH + window : 2 * REACH + window] = zero
    logs[0:REACH] = zero
    logs[REACH + window : 2 * REACH + window] = zero

    for s in range(len(mine)):

        def fill(m, carry, s=s):
            x0 = places[s] + (m // KY) * 8
            y0 = pl.multiple_of((m % KY) * 8, 8)
            on = active(x0)
            for i in range(8):
                a = mine[s][m, i]
                b = theirs[s][m, i]
                courant = jnp.where(is_source, a, b)
                density = jnp.where(is_source, b, a)
                squared = jnp.where(on, courant * courant, 0.0)
                square[x0 + i, pl.ds(y0, 8), :] = SECOND * squared
                centre[x0 + i, pl.ds(y0, 8), :] = 2.0 + (3.0 * second_weights[0]) * squared
                logs[REACH + x0 + i, pl.ds(y0, 8), :] = jnp.where(
                    on, jnp.log(jnp.where(on, density, 1.0)), 0.0
                )
            return carry

        lax.fori_loop(0, mine[s].shape[0], fill, 0)

    def bend(b, carry):
        w = pl.multiple_of(b * BLOCK, BLOCK)
        value = logs[pl.ds(REACH + w, BLOCK)].reshape(BLOCK * height, lanes)
        high = value.astype(jnp.bfloat16)
        low = (value - high.astype(jnp.float32)).astype(jnp.bfloat16)
        z = z_slopes(high, low, zmat)
        for g in range(BLOCK // 4):
            n = 4 * height
            y = y_slopes(high[g * n : g * n + n], low[g * n : g * n + n], ymat)
            for q in range(rows8):
                part = slice(q * 8, q * 8 + 8)
                _, slope = along_x([logs[w + 4 * g + j, part, :] for j in range(4 + 2 * REACH)])
                for i in range(4):
                    x = w + 4 * g + i
                    at = i * height + q * 8
                    scale = (FIRST * FIRST / SECOND) * square[x, part, :]
                    whole = scale * (1.0 / (FIRST_UNIT * FIRST_UNIT))
                    gx[x, part, :] = scale * slope[i]
                    gy[x, part, :] = whole * y[n + at : n + at + 8]
                    gz[x, part, :] = whole * z[g * n + at : g * n + at + 8, lanes:]
        return carry

    lax.fori_loop(0, window // BLOCK, bend, 0)


def steps_kernel(sides, span, pulses_of, meta, zmat, ymat, *refs):
    begin, end, steps = span
    fresh = begin == 0
    count = 2 if sides else 2 * HOPS + 1
    injects, refs = refs[: len(pulses_of)], refs[len(pulses_of) :]
    rims, refs = refs[:count], refs[count:]
    if fresh:
        mine, theirs, refs = refs[:count], refs[count : 2 * count], refs[2 * count :]
        levels, refs = refs[:count], refs[count:]
        keep, send, field, square, centre, gx, gy, gz, logs, *refs = refs
    else:
        carried, square, centre, gx, gy, gz, keep, send, field, *refs = refs
    pulses, zbuf, ybuf, record, rim, sems, out_sems, in_sems = refs
    thick, lanes = rims[0].shape[2:]
    window, height = square.shape[:2]
    cols = thick // 8
    rows8 = height // 8
    column = meta[1]
    is_source = meta[2] == 0
    limit = meta[3]
    half_of = meta[2]
    sublane = lax.broadcasted_iota(jnp.int32, (8, lanes), 0)
    if sides:
        own_lo = column * thick
        places = [column * thick, (1 - column) * thick]
    else:
        own_lo = HOPS * thick
        places = [s * thick for s in range(count)]

    def active(w):
        x = w if sides else w + column * thick - own_lo
        return (x >= 0) & (x < limit)

    def lo_of(k):
        return jnp.maximum(0, own_lo - REACH * (steps - 1 - k))

    def hi_of(k):
        return jnp.minimum(window, own_lo + thick + REACH * (steps - 1 - k))

    def pulse_copies(k, slot, act):
        for inject, (k_lo, k_hi, row_lo) in zip(injects, pulses_of):

            @pl.when((k >= k_lo) & (k < k_hi))
            def _(inject=inject, k_lo=k_lo, row_lo=row_lo):
                there = pulses.at[slot, pl.ds(row_lo, inject.shape[1])]
                act(pltpu.make_async_copy(inject.at[k - k_lo], there, sems.at[slot]))

    def out_copies(k, slot):
        return [
            pltpu.make_async_copy(
                record.at[slot, pl.ds(0, cols)], keep.at[k - begin], out_sems.at[slot, 0]
            ),
            pltpu.make_async_copy(
                record.at[slot, pl.ds(cols, cols)], send.at[k - begin], out_sems.at[slot, 1]
            ),
        ]

    def in_copies(s):
        place = places[s] if isinstance(places[s], int) else pl.multiple_of(places[s], 8)
        copies = [
            pltpu.make_async_copy(
                rims[s].at[pl.ds(begin, end - begin)],
                rim.at[:, :, pl.ds(place, thick), :],
                in_sems.at[s, 2],
            )
        ]
        if fresh:
            copies += [
                pltpu.make_async_copy(
                    levels[s].at[level],
                    field.at[level, pl.ds(REACH + place, thick)],
                    in_sems.at[s, level],
                )
                for level in range(2)
            ]
        return copies

    pulse_copies(begin, 0, lambda copy: copy.start())
    for s in range(count):
        for copy in in_copies(s):
            copy.start()

    if fresh:
        make_coefficients(
            mine, theirs, places, active, is_source, zmat, ymat, field, logs, square, centre, gx, gy, gz
        )
    else:

        def bring(w, carry):
            for level in range(2):
                field[level, w] = carried[level, w]
            return carry

        lax.fori_loop(0, window + 2 * REACH, bring, 0, unroll=4)
    for s in range(count):
        for copy in in_copies(s):
            copy.wait()

    rim_low = (sublane == 0) & is_source
    rim_high = (sublane == 7) & is_source
    groups = BLOCK // 4

    def cut(level, b, at, size):
        w = b * BLOCK + at
        value = field[level, pl.ds(REACH + w, size)].reshape(size * height, lanes)
        high = value.astype(jnp.bfloat16)
        return high, (value - high.astype(jnp.float32)).astype(jnp.bfloat16)

    def store_ahead(level, b, slot):
        high, low = cut(level, b, 0, BLOCK)
        zbuf[slot] = z_slopes(high, low, zmat)
        n = 4 * height
        for g in range(groups):
            ybuf[slot, g] = y_slopes(high[g * n : g * n + n], low[g * n : g * n + n], ymat)

    def one_step(k, buf):
        old = lax.rem(k, 2)
        new = 1 - old
        slot = lax.rem(k, 2)
        pulse_copies(k, slot, lambda copy: copy.wait())
        pulse_copies(k + 1, 1 - slot, lambda copy: copy.start())

        @pl.when(k >= begin + 2)
        def _():
            for copy in out_copies(k - 2, slot):
                copy.wait()

        first = lo_of(k) // BLOCK
        last = (hi_of(k) + BLOCK - 1) // BLOCK

        first_next = lo_of(k + 1) // BLOCK

        def block(b, bslot):
            w = pl.multiple_of(b * BLOCK, BLOCK)
            on = active(w) | active(w + BLOCK - 8)
            at_end = b == last - 1
            after = jnp.where(at_end, first_next, b + 1)
            level = jnp.where(at_end, old, new)
            is_own = (w >= own_lo) & (w < own_lo + thick)

            @pl.when(on)
            def _():
                top, rest = cut(level, after, 0, BLOCK)
                n = 4 * height
                for g in range(groups):
                    following_y = y_slopes(top[g * n : g * n + n], rest[g * n : g * n + n], ymat)
                    half = jnp.where(half_of == g % 2, 0, cols)
                    to = jnp.where(is_own, half + (w - own_lo) // 8 + g // 2, 2 * cols)
                    xs = [w + g * 4 + i for i in range(4)]
                    for q in range(rows8):
                        part = slice(q * 8, q * 8 + 8)
                        column_x = [
                            field[new, w + g * 4 + j, part, :] for j in range(4 + 2 * REACH)
                        ]
                        lap, dx = along_x(column_x)
                        mid = column_x[REACH : REACH + 4]
                        at = [(g * 4 + i) * height + q * 8 for i in range(4)]
                        aty = [i * height + q * 8 for i in range(4)]
                        z2 = [zbuf[bslot, p : p + 8, 0:lanes] for p in at]
                        z1 = [zbuf[bslot, p : p + 8, lanes:] for p in at]
                        y2 = [ybuf[bslot, g, p : p + 8, :] for p in aty]
                        y1 = [ybuf[bslot, g, 4 * height + p : 4 * height + p + 8, :] for p in aty]
                        lap = add(lap, scaled(1.0 / SECOND_UNIT, add(z2, y2)))
                        value = sub(
                            mul([centre[x, part, :] for x in xs], mid),
                            [field[old, REACH + x, part, :] for x in xs],
                        )
                        value = add(
                            value,
                            [
                                pulses[slot, pl.ds(pl.multiple_of(x * height + q * 8, 8), 8), :]
                                for x in xs
                            ],
                        )
                        value = add(value, mul([square[x, part, :] for x in xs], lap))
                        drift = mul([gx[x, part, :] for x in xs], dx)
                        drift = add(drift, mul([gy[x, part, :] for x in xs], y1))
                        drift = add(drift, mul([gz[x, part, :] for x in xs], z1))
                        value = sub(value, drift)
                        if q == 0:
                            low = [
                                jnp.broadcast_to(rim[k - begin, 0, pl.ds(x, 1), :], (8, lanes)) for x in xs
                            ]
                            value = each(lambda p, v: jnp.where(rim_low, p, v), low, value)
                        if q == rows8 - 1:
                            high = [
                                jnp.broadcast_to(rim[k - begin, 1, pl.ds(x, 1), :], (8, lanes)) for x in xs
                            ]
                            value = each(lambda p, v: jnp.where(rim_high, p, v), high, value)
                        for i in range(4):
                            field[old, REACH + xs[i], part, :] = value[i]
                            record[slot, to, i, part, :] = value[i]
                    ybuf[1 - bslot, g] = following_y
                zbuf[1 - bslot] = z_slopes(top, rest, zmat)

            for half in range(BLOCK // 8):
                x8 = w + half * 8

                @pl.when(on & jnp.logical_not(active(x8)))
                def _(x8=x8, half=half):
                    field[old, pl.ds(REACH + x8, 8)] = jnp.zeros((8, height, lanes), jnp.float32)
                    for g in range(2):
                        to = jnp.where(is_own, jnp.where(half_of == g, 0, cols) + (x8 - own_lo) // 8, 2 * cols)
                        record[slot, to] = jnp.zeros((4, height, lanes), jnp.float32)

            @pl.when(jnp.logical_not(on))
            def _():
                field[old, pl.ds(REACH + w, BLOCK)] = jnp.zeros((BLOCK, height, lanes), jnp.float32)
                for g in range(groups):
                    half = jnp.where(half_of == g % 2, 0, cols)
                    to = jnp.where(is_own, half + (w - own_lo) // 8 + g // 2, 2 * cols)
                    record[slot, to] = jnp.zeros((4, height, lanes), jnp.float32)
                store_ahead(level, after, 1 - bslot)

            return 1 - bslot

        buf = lax.fori_loop(first, last, block, buf)
        for copy in out_copies(k, slot):
            copy.start()
        return buf

    store_ahead(1 - begin % 2, lo_of(begin) // BLOCK, 0)
    lax.fori_loop(begin, end, one_step, 0)
    for k in (end - 2, end - 1):
        for copy in out_copies(k, k % 2):
            copy.wait()


def multiply(keep, got, start, total):
    steps, cols, half, height, lanes = keep.shape
    for c in range(cols):
        for i in range(half):

            def one(k, value, c=c, i=i):
                return value + keep[k, c, i] * got[k, c, i]

            first = start[c, i] if start is not None else jnp.zeros((height, lanes), jnp.float32)
            total[c, i] = lax.fori_loop(0, steps, one, first, unroll=4)


def multiply_kernel(keep, got, total):
    multiply(keep, got, None, total)


def image_kernel(owners, columns, tables, stored, info, before, keep, got, *refs):
    outs, total = refs[:owners], refs[owners]
    half = keep.shape[2]
    brick_y = outs[0].shape[2]
    multiply(keep, got, before, total)

    def take(b, m, local, rank):
        y = pl.multiple_of((m % KY) * brick_y, brick_y)
        for i in range(half):
            outs[b][rank, i] = total[m // KY, i, pl.ds(y, brick_y), :]

    serve(info, *tables, sources(owners, columns, stored, info), stored, take)


def sum_kernel(owners, columns, tables, info, *refs):
    blocks, out = refs[:-1], refs[-1]
    stored = out.shape[0]
    base = (info[0] * columns + info[1]) * stored
    out[...] = jnp.zeros_like(out)

    def take(b, m, local, rank):
        out[local] += blocks[b][rank]

    serve(info, *tables, [(b, base) for b in range(owners)], stored, take)


def call(kernel, out_shape, in_specs, out_specs, scratch=(), mib=8, flops=1):
    return pl.pallas_call(
        kernel,
        out_shape=out_shape,
        in_specs=in_specs,
        out_specs=out_specs,
        scratch_shapes=list(scratch),
        compiler_params=pltpu.CompilerParams(vmem_limit_bytes=mib * MIB),
        cost_estimate=pl.CostEstimate(flops=flops, bytes_accessed=1, transcendentals=0),
    )


def run_steps(sides, span, pulses_of, shape, meta, injects, rims, inputs):
    f32 = jnp.float32
    begin, end, steps = span
    window, height, lanes = shape
    count = len(rims)
    thick = window // count
    cols = thick // 8
    fresh = begin == 0
    kept = jax.ShapeDtypeStruct((end - begin, cols, 4, height, lanes), f32)
    padded = (window + 2 * REACH, height, lanes)
    outs, specs, scratch = [kept, kept], [anywhere, anywhere], []
    if fresh:
        if end < steps:
            outs += [jax.ShapeDtypeStruct((2,) + padded, f32)] + [jax.ShapeDtypeStruct(shape, f32)] * 5
            specs += [vmem] * 6
        else:
            scratch = [pltpu.VMEM((2,) + padded, f32)] + [pltpu.VMEM(shape, f32)] * 5
        scratch += [pltpu.VMEM(padded, f32)]
        in_specs = [vmem] * (2 * count) + [anywhere] * count
    else:
        scratch = [pltpu.VMEM((2,) + padded, f32)]
        in_specs = [vmem] * 6
    return call(
        functools.partial(steps_kernel, sides, span, pulses_of),
        outs,
        [smem, vmem, vmem] + [anywhere] * (len(injects) + count) + in_specs,
        specs,
        scratch
        + [
            pltpu.VMEM((2, window * height, lanes), f32),
            pltpu.VMEM((2, BLOCK * height, 2 * lanes), f32),
            pltpu.VMEM((2, BLOCK // 4, 8 * height, lanes), f32),
            pltpu.VMEM((2, 2 * cols + 1, 4, height, lanes), f32),
            pltpu.VMEM((end - begin, 2, window, lanes), f32),
            pltpu.SemaphoreType.DMA((2,)),
            pltpu.SemaphoreType.DMA((2, 2)),
            pltpu.SemaphoreType.DMA((count, 3)),
        ],
        mib=12 + window // 4,
        flops=(end - begin) * window * height * lanes * 2048,
    )(meta, z_matrix(lanes), y_matrix(height, 4), *injects, *rims, *inputs)


def injection(window, offset, split, late, height, lanes, is_source, source_cell, receivers, pulses, recorded):
    steps, spots = recorded.shape
    none = jnp.full((spots - 1,), -1, jnp.int32)
    cells = jnp.where(is_source, jnp.concatenate([source_cell, none]), receivers)
    source_values = jnp.concatenate([-pulses[:, None], jnp.zeros((steps, spots - 1), jnp.float32)], axis=1)
    values = jnp.where(is_source, source_values, recorded)
    z = cells % lanes
    rows = cells // lanes - offset * height
    rows = jnp.where(cells >= 0, rows, -1)
    every = lax.broadcasted_iota(jnp.int32, (window * height, spots), 0)
    which_row = (every == rows[None, :]).astype(jnp.bfloat16)
    which_lane = (z[:, None] == lax.broadcasted_iota(jnp.int32, (spots, lanes), 1)).astype(jnp.float32)
    high = lax.reduce_precision(values, 8, 7)
    low = lax.reduce_precision(values - high, 8, 7)
    both = jnp.concatenate([high, low], axis=1)
    spread = both[:, :, None] * jnp.concatenate([which_lane, which_lane], axis=0)[None]
    spread = spread.astype(jnp.bfloat16)
    twice = jnp.concatenate([which_row, which_row], axis=1)

    def product(rows, spread):
        return jnp.einsum("rp,kpz->krz", rows, spread, preferred_element_type=jnp.float32)

    lo, hi = late
    return (
        product(twice, spread[:split]),
        product(twice[lo * height : hi * height], spread[split:]),
    )


def per_device(
    velocity,
    density,
    owner_map,
    footprint,
    aperture,
    source_cell,
    receiver_cells,
    wavelet,
    traces,
    states,
    stored_rims,
):
    f32 = jnp.float32
    owners = lax.axis_size("shot")
    columns = lax.axis_size("dom")
    column = lax.axis_index("dom")
    pair = lax.axis_index("pair")
    shot = lax.axis_index("shot")
    stored, brick_x, brick_y, lanes = velocity.shape
    half_x = brick_x // 2
    slots = footprint.shape[1]
    per_owner = slots // owners
    thick = slots // KY * brick_x
    height = KY * brick_y
    steps = wavelet.shape[1]
    sides = columns == 2
    meta = jnp.stack(
        [shot.astype(jnp.int32), column.astype(jnp.int32), pair.astype(jnp.int32), aperture[0] * brick_x]
    )
    tables = (owner_map.shape[0], slots)

    table = jnp.where(pair == 0, velocity, density)
    prints = [footprint[0]] + [xor_swap(footprint[0], "shot", b) for b in range(1, owners)]
    info = jnp.concatenate([meta, owner_map, *prints])
    split = 12 if sides else 8
    if sides:
        offset = 0
        window = 2 * thick
        late = (0, window)
    else:
        offset = (column - HOPS) * thick
        window = (2 * HOPS + 1) * thick
        deep = REACH * (steps - 1 - split)
        late = (HOPS * thick - deep, (HOPS + 1) * thick + deep)
    early_inject, late_inject = injection(
        window, offset, split, late, height, lanes, pair == 0,
        source_cell, receiver_cells[0], wavelet[0], traces[0],
    )
    brick = jax.ShapeDtypeStruct((per_owner, brick_x, brick_y, lanes), f32)

    fields = slabs_of(states[0, 0])
    packed = call(
        functools.partial(pack_kernel, owners, columns, tables),
        [brick] * owners,
        [smem, anywhere],
        [anywhere] * owners,
        [pltpu.SemaphoreType.DMA((owners, per_owner))],
    )(info, table)
    got = [packed[0]] + [xor_swap(packed[b], "shot", b) for b in range(1, owners)]
    bricks = call(
        functools.partial(unpack_kernel, owners, columns, tables, stored),
        jax.ShapeDtypeStruct((slots, brick_x, brick_y, lanes), f32),
        [smem] + [vmem] * owners,
        vmem,
    )(info, *got)
    mine = slabs_of(bricks)
    shape = (window, height, lanes)
    if sides:
        rims_here, _ = lax.optimization_barrier((stored_rims[0], info))
        rim_slabs = slabs_of(rims_here, first_only=True)
        mine[1], early_inject, late_inject, rim_slabs[1] = lax.optimization_barrier(
            (mine[1], early_inject, late_inject, rim_slabs[1])
        )
        theirs = [xor_swap(slab, "pair", 1) for slab in mine]
        keep, send, *carried = run_steps(
            sides, (0, split, steps), [(0, split, 0)], shape, meta, [early_inject], rim_slabs,
            [*mine, *theirs, *fields],
        )
        partner = xor_swap(send, "pair", 1)
        keep_last, send_last = run_steps(
            sides, (split, steps, steps), [(split, steps, 0)], shape, meta, [late_inject], rim_slabs,
            carried,
        )
        total = call(
            multiply_kernel, jax.ShapeDtypeStruct(keep.shape[1:], f32), [vmem] * 2, vmem, mib=16
        )(keep, partner)
    else:
        theirs = [xor_swap(slab, "pair", 1) for slab in mine]
        keep_last, send_last = run_steps(
            sides, (0, steps, steps), [(0, split, 0), (split, steps, late[0] * height)], shape, meta,
            [early_inject, late_inject], slabs_of(stored_rims[0], first_only=True),
            [*mine, *theirs, *fields],
        )
        total = jnp.zeros(keep_last.shape[1:], f32)
    partner_last = xor_swap(send_last, "pair", 1)

    part = jax.ShapeDtypeStruct((per_owner, half_x, brick_y, lanes), f32)
    images = call(
        functools.partial(image_kernel, owners, columns, tables, stored),
        [part] * owners,
        [smem] + [vmem] * 3,
        [vmem] * owners,
        [pltpu.VMEM(total.shape, f32)],
        mib=16,
    )(info, total, keep_last, partner_last)
    returned = [images[0]] + [xor_swap(images[b], "shot", b) for b in range(1, owners)]
    return call(
        functools.partial(sum_kernel, owners, columns, tables),
        jax.ShapeDtypeStruct((stored, half_x, brick_y, lanes), f32),
        [smem] + [vmem] * owners,
        vmem,
    )(info, *returned)


def solution(mesh):
    placed = (
        P(("groups", "shot", "dom"), None, None, None),
        P(("groups", "shot", "dom"), None, None, None),
        P("groups"),
        P(("groups", "shot"), "dom"),
        P(("groups", "shot")),
        P(("groups", "shot")),
        P(("groups", "shot"), None),
        P(("groups", "shot"), None),
        P(("groups", "shot"), None, None),
        P(("groups", "shot"), "pair", None, "dom", None, None),
        P(("groups", "shot"), None, None, "dom", None),
    )
    return jax.shard_map(
        per_device,
        mesh=mesh,
        in_specs=placed,
        out_specs=P(("groups", "shot", "dom"), "pair", None, None),
        check_vma=False,
    )
```

time: 134 us -> 111 us (0.83)
  Pallas kernels: 61.1 us -> 50.7 us
  starting transfers between devices: 26.9 us -> 22.1 us
  waiting for transfers between devices: 25 us -> 21 us
  local copies, waits for them, and re-layouts: 3.98 us -> 0.86 us
    pallas_call x5 -> x7, Pallas kernels: 61.1 us -> 50.7 us  [the longest x2 42.3 us: run_steps(): call(functools.partial(steps_kernel, sides, span, pulses_of), outs, [smem...]
    ppermute x22 -> x13, starting transfers between devices: 24 us -> 17.5 us  [xor_swap(): return lax.ppermute(block, axis, [(i, i ^ bits) for i in range(size)])]
    ppermute x22 -> x13, waiting for transfers between devices: 22.2 us -> 17 us  [xor_swap(): return lax.ppermute(block, axis, [(i, i ^ bits) for i in range(size)])]
    ppermute x1 -> x2, waiting for transfers between devices: 0.01 us -> 3.95 us  [shift(): return lax.ppermute(x, 'dom', moves)]
    unnamed x22 -> x8, local copies, waits for them, and re-layouts: 3.89 us -> 0.01 us
    ppermute x1, waiting for transfers between devices: 2.75 us -> 0.01 us  [shift(): lax.ppermute(x, ('dom', 'pair'), [(i * pairs, j * pairs) for i, j in moves])]
    ppermute x1 -> x2, starting transfers between devices: 0.32 us -> 2.31 us  [shift(): return lax.ppermute(x, 'dom', moves)]
  transfers between devices with their start and end apart: 24 -> 16, of which waited for: 7 -> 7; matrix products, arithmetic and copies ran while one was open for 12% -> 14% of each run, Pallas kernels for 4% -> 12%
where the time goes in v4:
time: 111 us
  Pallas kernels  50.7 us (46%)
  starting transfers between devices  22.1 us (20%)
  waiting for transfers between devices  21 us (19%)
  matrix products  11.6 us (10%)
  other arithmetic  3.43 us (3%)
  between operations  1.47 us (1%)
    pallas_call x2, Pallas kernels, run_steps(): call(functools.partial(steps_kernel, sides, span, pulses_of), outs, [smem...  42.3 us
    ppermute x13, starting transfers between devices, xor_swap(): return lax.ppermute(block, axis, [(i, i ^ bits) for i in range(size)])  17.5 us
    ppermute x13, waiting for transfers between devices, xor_swap(): return lax.ppermute(block, axis, [(i, i ^ bits) for i in range(size)])  17 us
    dot_general x2, matrix products, product(): jnp.einsum('rp,kpz->krz', rows, spread, preferred_element_type=jnp.float32)  11.6 us
    ppermute x2, waiting for transfers between devices, shift(): return lax.ppermute(x, 'dom', moves)  3.95 us
    pallas_call x1, Pallas kernels, per_device(): call(functools.partial(pack_kernel, owners, columns, tables), [brick] * o...  2.36 us
    ppermute x2, starting transfers between devices, shift(): return lax.ppermute(x, 'dom', moves)  2.31 us
    ppermute x1, starting transfers between devices, shift(): lax.ppermute(x, ('dom', 'pair'), [(i * pairs, j * pairs) for i, j in moves])  2.23 us
  transfers between devices with their start and end apart: 16, of which 7 were waited for; matrix products, arithmetic and copies ran while one was open for 14% of the time, Pallas kernels for 12%

profile of v4, /device:TPU:0, one launch (start us, length us, event | category | flops | bytes accessed | tf_op | source)
XLA Modules:
  0.0 111.1 jit_solution(9222883875652538454)
XLA Ops:
  0.0 5.0 %collective-permute-start.2 = (s32[16]{0:T(128)}, s32[16]{0:T(128)S(1)}, u32[]{:S(2)}, u32[]{:S(2)}) collective-permute-start(s32[16]{0:T(128)} %bitcast.35), channel_id=1, source_target_pairs={{0,12},{4,8},{8,4},{12,0},{1,13},{5,9},{9,5},{13,1},{2,14},{6,10},... | collective-permute-start | bytes 200 | tf_op jit(solution)/shard_map/ppermute | solution.py:69
  5.0 0.0 collective-permute-start.1
  5.1 0.6 collective-permute-start
  5.6 1.7 %collective-permute-start.10 = (f32[2,32,32,128]{3,2,1,0:T(8,128)}, f32[2,32,32,128]{3,2,1,0:T(8,128)S(1)}, u32[]{:S(2)}, u32[]{:S(2)}) collective-permute-start(f32[2,32,32,128]{3,2,1,0:T(8,128)} %bitcast.32), channel_id=1, source_target_pairs={{0,2},{2,0},{1,3},{3,1},{4,6},{6,4},{5,7},{7,5},{8,10},{10,8},{9,1... | collective-permute-start | bytes 3145736 | tf_op jit(solution)/shard_map/ppermute | solution.py:79
  8.6 0.7 negate_bitcast_fusion
  9.3 0.1 copy.25
  9.4 0.8 iota_compare_fusion
  10.2 0.8 fusion.8
  11.0 1.0 broadcast_select_fusion.table
  12.0 0.0 collective-permute-done.2
  12.0 0.0 collective-permute-done.1
  12.0 0.0 collective-permute-done
  12.0 0.8 concatenate.25.info
  12.8 2.4 %shard_map.145 = (f32[4,8,8,128]{3,2,1,0:T(8,128)S(1)}, f32[4,8,8,128]{3,2,1,0:T(8,128)S(1)}, f32[4,8,8,128]{3,2,1,0:T(8,128)S(1)}, f32[4,8,8,128]{3,2,1,0:T(8,128)S(1)}) custom-call(s32[132]{0:T(256)S(1)} %concatenate.25.info, f32[8,8,8,128]{3,2,1,0:T(8,128)S(1)} %broadcast_select_fusion.table), custom_call_target="tpu_custom_call" | custom-call | flops 1 | bytes 1 | tf_op jit(solution)/shard_map/pallas_call | solution.py:653
  15.2 1.3 %collective-permute-start.3 = (f32[4,8,8,128]{3,2,1,0:T(8,128)S(1)}, f32[4,8,8,128]{3,2,1,0:T(8,128)S(1)}, u32[]{:S(2)}, u32[]{:S(2)}) collective-permute-start(f32[4,8,8,128]{3,2,1,0:T(8,128)S(1)} %get-tuple-element.29), channel_id=1, source_target_pairs={{0,4},{4,0},{8,12},{12,8},{1,5},{5,1},{9,13},{13,9},{2,6},{6,2},{1... | collective-permute-start | bytes 393224 | tf_op jit(solution)/shard_map/ppermute | solution.py:69
  16.5 2.9 %collective-permute-start.4 = (f32[4,8,8,128]{3,2,1,0:T(8,128)S(1)}, f32[4,8,8,128]{3,2,1,0:T(8,128)S(1)}, u32[]{:S(2)}, u32[]{:S(2)}) collective-permute-start(f32[4,8,8,128]{3,2,1,0:T(8,128)S(1)} %get-tuple-element.30), channel_id=1, source_target_pairs={{0,8},{4,12},{8,0},{12,4},{1,9},{5,13},{9,1},{13,5},{2,10},{6,14},... | collective-permute-start | bytes 393224 | tf_op jit(solution)/shard_map/ppermute | solution.py:69
  19.4 0.2 collective-permute-start.5
  19.7 2.2 %collective-permute-start.7 = (f32[16,2,32,128]{3,2,1,0:T(8,128)}, f32[16,2,32,128]{3,2,1,0:T(8,128)S(1)}, u32[]{:S(2)}, u32[]{:S(2)}) collective-permute-start(f32[16,2,32,128]{3,2,1,0:T(8,128)} %bitcast.29), channel_id=1, source_target_pairs={{0,2},{2,0},{4,6},{6,4},{8,10},{10,8},{12,14},{14,12},{16,18},{18,... | collective-permute-start | bytes 1572872 | tf_op jit(solution)/shard_map/ppermute | solution.py:78
  21.9 0.0 collective-permute-done.3.refs_1_
  21.9 7.3 %collective-permute-done.4.refs_2_ = f32[4,8,8,128]{3,2,1,0:T(8,128)S(1)} collective-permute-done((f32[4,8,8,128]{3,2,1,0:T(8,128)S(1)}, f32[4,8,8,128]{3,2,1,0:T(8,128)S(1)}, u32[]{:S(2)}, u32[]{:S(2)}) %collective-permute-start.4) | collective-permute-done | bytes 131104 | tf_op jit(solution)/shard_map/ppermute | solution.py:69
  29.3 0.0 collective-permute-done.5.refs_3_
  29.3 1.5 %shard_map.146.refs_3_ = f32[16,8,8,128]{3,2,1,0:T(8,128)S(1)} custom-call(s32[132]{0:T(256)S(1)} %concatenate.25.info, f32[4,8,8,128]{3,2,1,0:T(8,128)S(1)} %get-tuple-element.28.refs_0_, f32[4,8,8,128]{3,2,1,0:T(8,128)S(1)} %collective-permute-done.3.refs_1_, f32[4,8,8,128]{3,2,1,0:T(8,128)S(1)} %collective-permute-done.4.refs_2_, ...), custom_call_target="tpu_custom_call" | custom-call | flops 1 | bytes 1 | tf_op jit(solution)/shard_map/pallas_call | solution.py:661
  30.8 0.6 collective-permute-start.6
  31.4 9.2 %fusion.2.refs_0_ = f32[12,2048,128]{2,1,0:T(8,128)} fusion(pred[2048,512]{1,0:T(32,128)(4,1)S(1)} %iota_compare_fusion, f32[1024,128]{0,1:T(8,128)S(1)} %add_convert_fusion, f32[16,1024]{1,0:T(8,128)S(1)} %pad_maximum_fusion), kind=kOutput, calls=%fused_computation.4 | convolution fusion | flops 6448742400 | bytes 14221312 | tf_op jit(solution)/shard_map/rp,kpz->krz/dot_general | solution.py:592
  40.6 0.0 copy-start
  40.6 0.0 copy-start.1
  40.6 0.0 copy-start.2
  40.6 0.0 copy-start.3
  40.6 2.4 %fusion.7.refs_0_ = f32[4,2048,128]{2,1,0:T(8,128)S(1)} fusion(pred[2048,512]{1,0:T(32,128)(4,1)S(1)} %iota_compare_fusion, f32[1024,128]{0,1:T(8,128)S(1)} %add_convert_fusion, f32[16,1024]{1,0:T(8,128)S(1)} %pad_maximum_fusion), kind=kOutput, calls=%fused_computation.10 | convolution fusion | flops 2153775104 | bytes 5832704 | tf_op jit(solution)/shard_map/rp,kpz->krz/dot_general | solution.py:592
  43.0 0.1 collective-permute-start.8
  43.1 0.0 collective-permute-done.7.refs_2_
  43.1 3.9 %collective-permute-done.6.refs_4_ = f32[16,8,8,128]{3,2,1,0:T(8,128)S(1)} collective-permute-done((f32[16,8,8,128]{3,2,1,0:T(8,128)S(1)}, f32[16,8,8,128]{3,2,1,0:T(8,128)S(1)}, u32[]{:S(2)}, u32[]{:S(2)}) %collective-permute-start.6) | collective-permute-done | bytes 524320 | tf_op jit(solution)/shard_map/ppermute | solution.py:79
  47.0 0.0 collective-permute-start.9
  47.0 0.1 pad_add_fusion.meta
  47.1 0.0 collective-permute-done.8.refs_5_
  47.1 0.0 collective-permute-done.10.refs_8_
  47.1 1.8 %collective-permute-done.9.refs_6_ = f32[16,8,8,128]{3,2,1,0:T(8,128)S(1)} collective-permute-done((f32[16,8,8,128]{3,2,1,0:T(8,128)S(1)}, f32[16,8,8,128]{3,2,1,0:T(8,128)S(1)}, u32[]{:S(2)}, u32[]{:S(2)}) %collective-permute-start.9) | collective-permute-done | bytes 524320 | tf_op jit(solution)/shard_map/ppermute | solution.py:69
  48.9 0.0 copy-done
  48.9 0.0 copy-done.1
  48.9 0.0 copy-done.2
  48.9 0.0 copy-done.3
  49.0 33.3 %shard_map.147 = (f32[12,4,4,32,128]{4,3,2,1,0:T(8,128)S(1)}, f32[12,4,4,32,128]{4,3,2,1,0:T(8,128)S(1)}, f32[2,72,32,128]{3,2,1,0:T(8,128)S(1)}, f32[64,32,128]...) custom-call(s32[4]{0:T(128)S(1)} %pad_add_fusion.meta, ...), custom_call_target="tpu_custom_call" | custom-call | flops 6442450944 | bytes 1 | tf_op jit(solution)/shard_map/pallas_call | solution.py:551
  82.2 0.2 collective-permute-start.11
  82.4 9.1 %shard_map.149 = (f32[4,4,4,32,128]{4,3,2,1,0:T(8,128)S(1)}, f32[4,4,4,32,128]{4,3,2,1,0:T(8,128)S(1)}) custom-call(s32[4]{0:T(128)S(1)} %pad_add_fusion.meta, bf16[256,256]{1,0:T(8,128)(2,1)S(1)} %copy-done.2, bf16[256,256]{1,0:T(8,128)(2,1)S(1)} %copy-done.1, f32[4,2048,128]{2,1,0:T(8,128)S(1)} %fusion.7.refs_0_, f32[16,2,32,128]{3,2,1,0:T(8,128)S(1)} %bitcast.31, ...), custom_call_target="tpu_custom_call" | custom-call | flops 2147483648 | bytes 1 | tf_op jit(solution)/shard_map/pallas_call | solution.py:551
  91.5 0.5 collective-permute-start.12
  92.0 0.0 collective-permute-done.11.got
  92.0 0.5 shard_map.148.before
  92.5 1.8 %collective-permute-done.12.got = f32[4,4,4,32,128]{4,3,2,1,0:T(8,128)S(1)} collective-permute-done((f32[4,4,4,32,128]{4,3,2,1,0:T(8,128)S(1)}, f32[4,4,4,32,128]{4,3,2,1,0:T(8,128)S(1)}, u32[]{:S(2)}, u32[]{:S(2)}) %collective-permute-start.12) | collective-permute-done | bytes 1048608 | tf_op jit(solution)/shard_map/ppermute | solution.py:69
  94.3 1.7 %shard_map.150 = (f32[4,4,8,128]{3,2,1,0:T(8,128)S(1)}, f32[4,4,8,128]{3,2,1,0:T(8,128)S(1)}, f32[4,4,8,128]{3,2,1,0:T(8,128)S(1)}, f32[4,4,8,128]{3,2,1,0:T(8,128)S(1)}) custom-call(s32[132]{0:T(256)S(1)} %concatenate.25.info, f32[4,4,32,128]{3,2,1,0:T(8,128)S(1)} %shard_map.148.before, f32[4,4,4,32,128]{4,3,2,1,0:T(8,128)S(1)} %get-tuple-element.45.keep, ...), custom_call_target="tpu_custom_call" | custom-call | flops 1 | bytes 1 | tf_op jit(solution)/shard_map/pallas_call | solution.py:699
  96.0 4.3 %collective-permute-start.13 = (f32[4,4,8,128]{3,2,1,0:T(8,128)S(1)}, f32[4,4,8,128]{3,2,1,0:T(8,128)S(1)}, u32[]{:S(2)}, u32[]{:S(2)}) collective-permute-start(f32[4,4,8,128]{3,2,1,0:T(8,128)S(1)} %get-tuple-element.48), channel_id=1, source_target_pairs={{0,4},{4,0},{8,12},{12,8},{1,5},{5,1},{9,13},{13,9},{2,6},{6,2},{1... | collective-permute-start | bytes 196616 | tf_op jit(solution)/shard_map/ppermute | solution.py:69
  100.3 2.4 %collective-permute-start.14 = (f32[4,4,8,128]{3,2,1,0:T(8,128)S(1)}, f32[4,4,8,128]{3,2,1,0:T(8,128)S(1)}, u32[]{:S(2)}, u32[]{:S(2)}) collective-permute-start(f32[4,4,8,128]{3,2,1,0:T(8,128)S(1)} %get-tuple-element.49), channel_id=1, source_target_pairs={{0,8},{4,12},{8,0},{12,4},{1,9},{5,13},{9,1},{13,5},{2,10},{6,14},... | collective-permute-start | bytes 196616 | tf_op jit(solution)/shard_map/ppermute | solution.py:69
  102.7 0.0 collective-permute-start.15
  102.8 0.2 collective-permute-done.13.refs_1_
  102.9 5.1 %collective-permute-done.14.refs_2_ = f32[4,4,8,128]{3,2,1,0:T(8,128)S(1)} collective-permute-done((f32[4,4,8,128]{3,2,1,0:T(8,128)S(1)}, f32[4,4,8,128]{3,2,1,0:T(8,128)S(1)}, u32[]{:S(2)}, u32[]{:S(2)}) %collective-permute-start.14) | collective-permute-done | bytes 65568 | tf_op jit(solution)/shard_map/ppermute | solution.py:69
  108.1 0.8 collective-permute-done.15.refs_3_
  108.8 2.2 %shard_map.151 = f32[8,4,8,128]{3,2,1,0:T(8,128)} custom-call(s32[132]{0:T(256)S(1)} %concatenate.25.info, f32[4,4,8,128]{3,2,1,0:T(8,128)S(1)} %get-tuple-element.47.refs_0_, f32[4,4,8,128]{3,2,1,0:T(8,128)S(1)} %collective-permute-done.13.refs_1_, f32[4,4,8,128]{3,2,1,0:T(8,128)S(1)} %collective-permute-done.14.refs_2_, ...), custom_call_target="tpu_custom_call" | custom-call | flops 1 | bytes 1 | tf_op jit(solution)/shard_map/pallas_call | solution.py:708
  (4 shorter events, 0.1 us)
Async XLA Ops:
  0.0 12.0 %collective-permute-start.2 = (s32[16]{0:T(128)}, s32[16]{0:T(128)S(1)}, u32[]{:S(2)}, u32[]{:S(2)}) collective-permute-start(s32[16]{0:T(128)} %bitcast.35), channel_id=1, source_target_pairs={{0,12},{4,8},{8,4},{12,0},{1,13},{5,9},{9,5},{13,1},{2,14},{6,10},... | collective-permute-start | bytes 200 | tf_op jit(solution)/shard_map/ppermute | solution.py:69
  5.0 6.9 %collective-permute-start.1 = (s32[16]{0:T(128)}, s32[16]{0:T(128)S(1)}, u32[]{:S(2)}, u32[]{:S(2)}) collective-permute-start(s32[16]{0:T(128)} %bitcast.36), channel_id=1, source_target_pairs={{0,8},{4,12},{8,0},{12,4},{1,9},{5,13},{9,1},{13,5},{2,10},{6,14},... | collective-permute-start | bytes 200 | tf_op jit(solution)/shard_map/ppermute | solution.py:69
  5.1 6.9 %collective-permute-start = (s32[16]{0:T(128)}, s32[16]{0:T(128)S(1)}, u32[]{:S(2)}, u32[]{:S(2)}) collective-permute-start(s32[16]{0:T(128)} %bitcast.37), channel_id=1, source_target_pairs={{0,4},{4,0},{8,12},{12,8},{1,5},{5,1},{9,13},{13,9},{2,6},{6,2},{1... | collective-permute-start | bytes 200 | tf_op jit(solution)/shard_map/ppermute | solution.py:69
  5.6 41.5 %collective-permute-start.10 = (f32[2,32,32,128]{3,2,1,0:T(8,128)}, f32[2,32,32,128]{3,2,1,0:T(8,128)S(1)}, u32[]{:S(2)}, u32[]{:S(2)}) collective-permute-start(f32[2,32,32,128]{3,2,1,0:T(8,128)} %bitcast.32), channel_id=1, source_target_pairs={{0,2},{2,0},{1,3},{3,1},{4,6},{6,4},{5,7},{7,5},{8,10},{10,8},{9,1... | collective-permute-start | bytes 3145736 | tf_op jit(solution)/shard_map/ppermute | solution.py:79
  15.2 6.8 %collective-permute-start.3 = (f32[4,8,8,128]{3,2,1,0:T(8,128)S(1)}, f32[4,8,8,128]{3,2,1,0:T(8,128)S(1)}, u32[]{:S(2)}, u32[]{:S(2)}) collective-permute-start(f32[4,8,8,128]{3,2,1,0:T(8,128)S(1)} %get-tuple-element.29), channel_id=1, source_target_pairs={{0,4},{4,0},{8,12},{12,8},{1,5},{5,1},{9,13},{13,9},{2,6},{6,2},{1... | collective-permute-start | bytes 393224 | tf_op jit(solution)/shard_map/ppermute | solution.py:69
  16.5 12.8 %collective-permute-start.4 = (f32[4,8,8,128]{3,2,1,0:T(8,128)S(1)}, f32[4,8,8,128]{3,2,1,0:T(8,128)S(1)}, u32[]{:S(2)}, u32[]{:S(2)}) collective-permute-start(f32[4,8,8,128]{3,2,1,0:T(8,128)S(1)} %get-tuple-element.30), channel_id=1, source_target_pairs={{0,8},{4,12},{8,0},{12,4},{1,9},{5,13},{9,1},{13,5},{2,10},{6,14},... | collective-permute-start | bytes 393224 | tf_op jit(solution)/shard_map/ppermute | solution.py:69
  19.4 9.8 %collective-permute-start.5 = (f32[4,8,8,128]{3,2,1,0:T(8,128)S(1)}, f32[4,8,8,128]{3,2,1,0:T(8,128)S(1)}, u32[]{:S(2)}, u32[]{:S(2)}) collective-permute-start(f32[4,8,8,128]{3,2,1,0:T(8,128)S(1)} %get-tuple-element.31), channel_id=1, source_target_pairs={{0,12},{4,8},{8,4},{12,0},{1,13},{5,9},{9,5},{13,1},{2,14},{6,10},... | collective-permute-start | bytes 393224 | tf_op jit(solution)/shard_map/ppermute | solution.py:69
  19.7 23.4 %collective-permute-start.7 = (f32[16,2,32,128]{3,2,1,0:T(8,128)}, f32[16,2,32,128]{3,2,1,0:T(8,128)S(1)}, u32[]{:S(2)}, u32[]{:S(2)}) collective-permute-start(f32[16,2,32,128]{3,2,1,0:T(8,128)} %bitcast.29), channel_id=1, source_target_pairs={{0,2},{2,0},{4,6},{6,4},{8,10},{10,8},{12,14},{14,12},{16,18},{18,... | collective-permute-start | bytes 1572872 | tf_op jit(solution)/shard_map/ppermute | solution.py:78
  30.8 16.2 %collective-permute-start.6 = (f32[16,8,8,128]{3,2,1,0:T(8,128)S(1)}, f32[16,8,8,128]{3,2,1,0:T(8,128)S(1)}, u32[]{:S(2)}, u32[]{:S(2)}) collective-permute-start(f32[16,8,8,128]{3,2,1,0:T(8,128)S(1)} %shard_map.146.refs_3_), channel_id=1, source_target_pairs={{0,2},{2,0},{1,3},{3,1},{4,6},{6,4},{5,7},{7,5},{8,10},{10,8},{9,1... | collective-permute-start | bytes 1572872 | tf_op jit(solution)/shard_map/ppermute | solution.py:79
  40.6 8.3 %copy-start = (f32[1,16,2,32,128]{4,3,2,1,0:T(8,128)S(1)}, f32[1,16,2,32,128]{4,3,2,1,0:T(8,128)}, u32[]{:S(2)}) copy-start(f32[1,16,2,32,128]{4,3,2,1,0:T(8,128)} %param.25) | copy-start | bytes 1572868
  40.6 8.3 %copy-start.1 = (bf16[256,256]{1,0:T(8,128)(2,1)S(1)}, bf16[256,256]{1,0:T(8,128)(2,1)}, u32[]{:S(2)}) copy-start(bf16[256,256]{1,0:T(8,128)(2,1)} %constant.53.clone.ymat) | copy-start | bytes 393220
  40.6 8.3 %copy-start.2 = (bf16[256,256]{1,0:T(8,128)(2,1)S(1)}, bf16[256,256]{1,0:T(8,128)(2,1)}, u32[]{:S(2)}) copy-start(bf16[256,256]{1,0:T(8,128)(2,1)} %constant.52.clone.zmat) | copy-start | bytes 393220
  40.6 8.3 %copy-start.3 = (f32[1,1,2,32,32,128]{5,4,3,2,1,0:T(8,128)S(1)}, f32[1,1,2,32,32,128]{5,4,3,2,1,0:T(8,128)}, u32[]{:S(2)}) copy-start(f32[1,1,2,32,32,128]{5,4,3,2,1,0:T(8,128)} %param.24) | copy-start | bytes 3145732
  43.0 4.1 %collective-permute-start.8 = (f32[16,8,8,128]{3,2,1,0:T(8,128)S(1)}, f32[16,8,8,128]{3,2,1,0:T(8,128)S(1)}, u32[]{:S(2)}, u32[]{:S(2)}) collective-permute-start(f32[16,8,8,128]{3,2,1,0:T(8,128)S(1)} %shard_map.146.refs_3_), channel_id=1, source_target_pairs={{0,1},{1,0},{2,3},{3,2},{4,5},{5,4},{6,7},{7,6},{8,9},{9,8},{10,11... | collective-permute-start | bytes 1572872 | tf_op jit(solution)/shard_map/ppermute | solution.py:69
  47.0 1.9 %collective-permute-start.9 = (f32[16,8,8,128]{3,2,1,0:T(8,128)S(1)}, f32[16,8,8,128]{3,2,1,0:T(8,128)S(1)}, u32[]{:S(2)}, u32[]{:S(2)}) collective-permute-start(f32[16,8,8,128]{3,2,1,0:T(8,128)S(1)} %collective-permute-done.6.refs_4_), channel_id=1, source_target_pairs={{0,1},{1,0},{2,3},{3,2},{4,5},{5,4},{6,7},{7,6},{8,9},{9,8},{10,11... | collective-permute-start | bytes 1572872 | tf_op jit(solution)/shard_map/ppermute | solution.py:69
  82.2 9.8 %collective-permute-start.11 = (f32[12,4,4,32,128]{4,3,2,1,0:T(8,128)S(1)}, f32[12,4,4,32,128]{4,3,2,1,0:T(8,128)S(1)}, u32[]{:S(2)}, u32[]{:S(2)}) collective-permute-start(f32[12,4,4,32,128]{4,3,2,1,0:T(8,128)S(1)} %get-tuple-element.37), channel_id=1, source_target_pairs={{0,1},{1,0},{2,3},{3,2},{4,5},{5,4},{6,7},{7,6},{8,9},{9,8},{10,11... | collective-permute-start | bytes 9437192 | tf_op jit(solution)/shard_map/ppermute | solution.py:69
  91.5 2.7 %collective-permute-start.12 = (f32[4,4,4,32,128]{4,3,2,1,0:T(8,128)S(1)}, f32[4,4,4,32,128]{4,3,2,1,0:T(8,128)S(1)}, u32[]{:S(2)}, u32[]{:S(2)}) collective-permute-start(f32[4,4,4,32,128]{4,3,2,1,0:T(8,128)S(1)} %get-tuple-element.46), channel_id=1, source_target_pairs={{0,1},{1,0},{2,3},{3,2},{4,5},{5,4},{6,7},{7,6},{8,9},{9,8},{10,11... | collective-permute-start | bytes 3145736 | tf_op jit(solution)/shard_map/ppermute | solution.py:69
  96.0 6.9 %collective-permute-start.13 = (f32[4,4,8,128]{3,2,1,0:T(8,128)S(1)}, f32[4,4,8,128]{3,2,1,0:T(8,128)S(1)}, u32[]{:S(2)}, u32[]{:S(2)}) collective-permute-start(f32[4,4,8,128]{3,2,1,0:T(8,128)S(1)} %get-tuple-element.48), channel_id=1, source_target_pairs={{0,4},{4,0},{8,12},{12,8},{1,5},{5,1},{9,13},{13,9},{2,6},{6,2},{1... | collective-permute-start | bytes 196616 | tf_op jit(solution)/shard_map/ppermute | solution.py:69
  100.3 7.7 %collective-permute-start.14 = (f32[4,4,8,128]{3,2,1,0:T(8,128)S(1)}, f32[4,4,8,128]{3,2,1,0:T(8,128)S(1)}, u32[]{:S(2)}, u32[]{:S(2)}) collective-permute-start(f32[4,4,8,128]{3,2,1,0:T(8,128)S(1)} %get-tuple-element.49), channel_id=1, source_target_pairs={{0,8},{4,12},{8,0},{12,4},{1,9},{5,13},{9,1},{13,5},{2,10},{6,14},... | collective-permute-start | bytes 196616 | tf_op jit(solution)/shard_map/ppermute | solution.py:69
  102.7 6.1 %collective-permute-start.15 = (f32[4,4,8,128]{3,2,1,0:T(8,128)S(1)}, f32[4,4,8,128]{3,2,1,0:T(8,128)S(1)}, u32[]{:S(2)}, u32[]{:S(2)}) collective-permute-start(f32[4,4,8,128]{3,2,1,0:T(8,128)S(1)} %get-tuple-element.50), channel_id=1, source_target_pairs={{0,12},{4,8},{8,4},{12,0},{1,13},{5,9},{9,5},{13,1},{2,14},{6,10},... | collective-permute-start | bytes 196616 | tf_op jit(solution)/shard_map/ppermute | solution.py:69

commit v5 on v4

--- a/solution.py
+++ b/solution.py
@@ -14,15 +14,10 @@
 first_weights = (0.8, -0.2, 4.0 / 105.0, -1.0 / 280.0)
 second_weights = (-205.0 / 72.0, 1.6, -0.2, 8.0 / 315.0, -1.0 / 560.0)
 
-FIRST = first_weights[0]
-SECOND = second_weights[1]
-first_ratio = tuple(w / FIRST for w in first_weights)
-second_ratio = tuple(w / SECOND for w in second_weights[1:])
-
-SECOND_UNIT = 8064.0
-FIRST_UNIT = 672.0
-second_whole = (8064.0, -1008.0, 128.0, -9.0)
-first_whole = (672.0, -168.0, 32.0, -3.0)
+FIRST = first_weights[2]
+SECOND = second_weights[3]
+first_ratio = (21.0, -5.25, 1.0, -0.09375)
+second_ratio = (63.0, -7.875, 1.0, -0.0703125)
 
 HOPS = 2
 META = 4
@@ -39,11 +34,11 @@
     for r in range(1, REACH + 1):
         for z in range(size):
             if z + r < size:
-                second[z + r, z] = second_whole[r - 1]
-                first[z + r, z] = first_whole[r - 1]
+                second[z + r, z] = second_ratio[r - 1]
+                first[z + r, z] = first_ratio[r - 1]
             if z - r >= 0:
-                second[z - r, z] = second_whole[r - 1]
-                first[z - r, z] = -first_whole[r - 1]
+                second[z - r, z] = second_ratio[r - 1]
+                first[z - r, z] = -first_ratio[r - 1]
     whole = np.concatenate([second, first], axis=1)
     return np.concatenate([whole, whole], axis=0).astype(jnp.bfloat16)
 
@@ -54,11 +49,11 @@
     for r in range(1, REACH + 1):
         for y in range(across):
             if y + r < across:
-                second[y, y + r] = second_whole[r - 1]
-                first[y, y + r] = first_whole[r - 1]
+                second[y, y + r] = second_ratio[r - 1]
+                first[y, y + r] = first_ratio[r - 1]
             if y - r >= 0:
-                second[y, y - r] = second_whole[r - 1]
-                first[y, y - r] = -first_whole[r - 1]
+                second[y, y - r] = second_ratio[r - 1]
+                first[y, y - r] = -first_ratio[r - 1]
     same = np.eye(layers)
     whole = np.concatenate([np.kron(same, second), np.kron(same, first)], axis=0)
     return np.concatenate([whole, whole], axis=1).astype(jnp.bfloat16)
@@ -111,12 +106,13 @@
 
 
 def pack_kernel(owners, columns, tables, info, table, *refs):
-    outs, sems = refs[:-1], refs[-1]
+    outs, rows, sems = refs[:owners], refs[owners], refs[owners + 1]
     stored = table.shape[0]
     per_owner = outs[0].shape[0]
     base = (info[0] * columns + info[1]) * stored
 
     def take(b, m, local, rank):
+        rows[b * per_owner + rank] = local
         pltpu.make_async_copy(table.at[local], outs[b].at[rank], sems.at[b, rank]).start()
 
     serve(info, *tables, [(b, base) for b in range(owners)], stored, take)
@@ -126,9 +122,11 @@
 
 
 def unpack_kernel(owners, columns, tables, stored, info, *refs):
-    blocks, out = refs[:-1], refs[-1]
+    blocks, out, places = refs[:owners], refs[owners], refs[owners + 1]
+    per_owner = blocks[0].shape[0]
 
     def take(b, m, local, rank):
+        places[b * per_owner + rank] = m
         out[m] = blocks[b][rank]
 
     serve(info, *tables, sources(owners, columns, stored, info), stored, take)
@@ -161,11 +159,11 @@
 def along_x(column):
     size = len(column) - 2 * REACH
     lap = slope = None
-    for r in range(1, REACH + 1):
+    for r in (3, 1, 2, 4):
         ahead = column[REACH + r : REACH + r + size]
         behind = column[REACH - r : REACH - r + size]
         total, apart = add(ahead, behind), sub(ahead, behind)
-        if r == 1:
+        if r == 3:
             lap, slope = total, apart
         else:
             lap = add(lap, scaled(second_ratio[r - 1], total))
@@ -179,8 +177,11 @@
 
 
 def y_slopes(high, low, ymat):
-    both = jnp.concatenate([high, low], axis=0)
-    return jnp.dot(ymat[...], both, preferred_element_type=jnp.float32)
+    n = ymat.shape[0] // 2
+    both = [
+        jnp.concatenate([high[at : at + n], low[at : at + n]], axis=0) for at in range(0, 2 * n, n)
+    ]
+    return jnp.dot(ymat[...], jnp.concatenate(both, axis=1), preferred_element_type=jnp.float32)
 
 
 BLOCK = 16
@@ -225,9 +226,12 @@
         high = value.astype(jnp.bfloat16)
         low = (value - high.astype(jnp.float32)).astype(jnp.bfloat16)
         z = z_slopes(high, low, zmat)
+        n = 4 * height
         for g in range(BLOCK // 4):
-            n = 4 * height
-            y = y_slopes(high[g * n : g * n + n], low[g * n : g * n + n], ymat)
+            if g % 2 == 0:
+                pair = slice(g * n, g * n + 2 * n)
+                y = y_slopes(high[pair], low[pair], ymat)
+            side = slice(g % 2 * lanes, g % 2 * lanes + lanes)
             for q in range(rows8):
                 part = slice(q * 8, q * 8 + 8)
                 _, slope = along_x([logs[w + 4 * g + j, part, :] for j in range(4 + 2 * REACH)])
@@ -235,10 +239,9 @@
                     x = w + 4 * g + i
                     at = i * height + q * 8
                     scale = (FIRST * FIRST / SECOND) * square[x, part, :]
-                    whole = scale * (1.0 / (FIRST_UNIT * FIRST_UNIT))
                     gx[x, part, :] = scale * slope[i]
-                    gy[x, part, :] = whole * y[n + at : n + at + 8]
-                    gz[x, part, :] = whole * z[g * n + at : g * n + at + 8, lanes:]
+                    gy[x, part, :] = scale * y[n + at : n + at + 8, side]
+                    gz[x, part, :] = scale * z[g * n + at : g * n + at + 8, lanes:]
         return carry
 
     lax.fori_loop(0, window // BLOCK, bend, 0)
@@ -355,14 +358,15 @@
     def store_ahead(level, b, slot):
         high, low = cut(level, b, 0, BLOCK)
         zbuf[slot] = z_slopes(high, low, zmat)
-        n = 4 * height
-        for g in range(groups):
-            ybuf[slot, g] = y_slopes(high[g * n : g * n + n], low[g * n : g * n + n], ymat)
+        n = 8 * height
+        for h in range(groups // 2):
+            pair = slice(h * n, h * n + n)
+            ybuf[slot, h] = y_slopes(high[pair], low[pair], ymat)
 
     def one_step(k, buf):
         old = lax.rem(k, 2)
         new = 1 - old
-        slot = lax.rem(k, 2)
+        slot = lax.rem(k - begin, 2)
         pulse_copies(k, slot, lambda copy: copy.wait())
         pulse_copies(k + 1, 1 - slot, lambda copy: copy.start())
 
@@ -389,7 +393,7 @@
                 top, rest = cut(level, after, 0, BLOCK)
                 n = 4 * height
                 for g in range(groups):
-                    following_y = y_slopes(top[g * n : g * n + n], rest[g * n : g * n + n], ymat)
+                    side = slice(g % 2 * lanes, g % 2 * lanes + lanes)
                     half = jnp.where(half_of == g % 2, 0, cols)
                     to = jnp.where(is_own, half + (w - own_lo) // 8 + g // 2, 2 * cols)
                     xs = [w + g * 4 + i for i in range(4)]
@@ -404,9 +408,9 @@
                         aty = [i * height + q * 8 for i in range(4)]
                         z2 = [zbuf[bslot, p : p + 8, 0:lanes] for p in at]
                         z1 = [zbuf[bslot, p : p + 8, lanes:] for p in at]
-                        y2 = [ybuf[bslot, g, p : p + 8, :] for p in aty]
-                        y1 = [ybuf[bslot, g, 4 * height + p : 4 * height + p + 8, :] for p in aty]
-                        lap = add(lap, scaled(1.0 / SECOND_UNIT, add(z2, y2)))
+                        y2 = [ybuf[bslot, g // 2, p : p + 8, side] for p in aty]
+                        y1 = [ybuf[bslot, g // 2, n + p : n + p + 8, side] for p in aty]
+                        lap = add(lap, add(z2, y2))
                         value = sub(
                             mul([centre[x, part, :] for x in xs], mid),
                             [field[old, REACH + x, part, :] for x in xs],
@@ -436,8 +440,9 @@
                         for i in range(4):
                             field[old, REACH + xs[i], part, :] = value[i]
                             record[slot, to, i, part, :] = value[i]
-                    ybuf[1 - bslot, g] = following_y
                 zbuf[1 - bslot] = z_slopes(top, rest, zmat)
+                for h in range(groups // 2):
+                    ybuf[1 - bslot, h] = y_slopes(top[h * 2 * n : h * 2 * n + 2 * n], rest[h * 2 * n : h * 2 * n + 2 * n], ymat)
 
             for half in range(BLOCK // 8):
                 x8 = w + half * 8
@@ -468,7 +473,7 @@
     store_ahead(1 - begin % 2, lo_of(begin) // BLOCK, 0)
     lax.fori_loop(begin, end, one_step, 0)
     for k in (end - 2, end - 1):
-        for copy in out_copies(k, k % 2):
+        for copy in out_copies(k, (k - begin) % 2):
             copy.wait()
 
 
@@ -488,30 +493,25 @@
     multiply(keep, got, None, total)
 
 
-def image_kernel(owners, columns, tables, stored, info, before, keep, got, *refs):
+def image_kernel(owners, places, before, keep, got, *refs):
     outs, total = refs[:owners], refs[owners]
-    half = keep.shape[2]
-    brick_y = outs[0].shape[2]
+    per_owner, half, brick_y = outs[0].shape[:3]
     multiply(keep, got, before, total)
-
-    def take(b, m, local, rank):
-        y = pl.multiple_of((m % KY) * brick_y, brick_y)
-        for i in range(half):
-            outs[b][rank, i] = total[m // KY, i, pl.ds(y, brick_y), :]
-
-    serve(info, *tables, sources(owners, columns, stored, info), stored, take)
-
-
-def sum_kernel(owners, columns, tables, info, *refs):
+    for b in range(owners):
+        for rank in range(per_owner):
+            m = places[b * per_owner + rank]
+            y = pl.multiple_of((m % KY) * brick_y, brick_y)
+            for i in range(half):
+                outs[b][rank, i] = total[m // KY, i, pl.ds(y, brick_y), :]
+
+
+def sum_kernel(owners, rows, *refs):
     blocks, out = refs[:-1], refs[-1]
-    stored = out.shape[0]
-    base = (info[0] * columns + info[1]) * stored
+    per_owner = blocks[0].shape[0]
     out[...] = jnp.zeros_like(out)
-
-    def take(b, m, local, rank):
-        out[local] += blocks[b][rank]
-
-    serve(info, *tables, [(b, base) for b in range(owners)], stored, take)
+    for b in range(owners):
+        for rank in range(per_owner):
+            out[rows[b * per_owner + rank]] += blocks[b][rank]
 
 
 def call(kernel, out_shape, in_specs, out_specs, scratch=(), mib=8, flops=1):
@@ -557,7 +557,7 @@
         + [
             pltpu.VMEM((2, window * height, lanes), f32),
             pltpu.VMEM((2, BLOCK * height, 2 * lanes), f32),
-            pltpu.VMEM((2, BLOCK // 4, 8 * height, lanes), f32),
+            pltpu.VMEM((2, BLOCK // 8, 8 * height, 2 * lanes), f32),
             pltpu.VMEM((2, 2 * cols + 1, 4, height, lanes), f32),
             pltpu.VMEM((end - begin, 2, window, lanes), f32),
             pltpu.SemaphoreType.DMA((2,)),
@@ -633,7 +633,7 @@
     table = jnp.where(pair == 0, velocity, density)
     prints = [footprint[0]] + [xor_swap(footprint[0], "shot", b) for b in range(1, owners)]
     info = jnp.concatenate([meta, owner_map, *prints])
-    split = 12 if sides else 8
+    split = 13 if sides else 8
     if sides:
         offset = 0
         window = 2 * thick
@@ -650,19 +650,20 @@
     brick = jax.ShapeDtypeStruct((per_owner, brick_x, brick_y, lanes), f32)
 
     fields = slabs_of(states[0, 0])
-    packed = call(
+    listed = jax.ShapeDtypeStruct((slots,), jnp.int32)
+    *packed, rows = call(
         functools.partial(pack_kernel, owners, columns, tables),
-        [brick] * owners,
+        [brick] * owners + [listed],
         [smem, anywhere],
-        [anywhere] * owners,
+        [anywhere] * owners + [smem],
         [pltpu.SemaphoreType.DMA((owners, per_owner))],
     )(info, table)
     got = [packed[0]] + [xor_swap(packed[b], "shot", b) for b in range(1, owners)]
-    bricks = call(
+    bricks, places = call(
         functools.partial(unpack_kernel, owners, columns, tables, stored),
-        jax.ShapeDtypeStruct((slots, brick_x, brick_y, lanes), f32),
+        [jax.ShapeDtypeStruct((slots, brick_x, brick_y, lanes), f32), listed],
         [smem] + [vmem] * owners,
-        vmem,
+        [vmem, smem],
     )(info, *got)
     mine = slabs_of(bricks)
     shape = (window, height, lanes)
@@ -697,20 +698,20 @@
 
     part = jax.ShapeDtypeStruct((per_owner, half_x, brick_y, lanes), f32)
     images = call(
-        functools.partial(image_kernel, owners, columns, tables, stored),
+        functools.partial(image_kernel, owners),
         [part] * owners,
         [smem] + [vmem] * 3,
         [vmem] * owners,
         [pltpu.VMEM(total.shape, f32)],
         mib=16,
-    )(info, total, keep_last, partner_last)
+    )(places, total, keep_last, partner_last)
     returned = [images[0]] + [xor_swap(images[b], "shot", b) for b in range(1, owners)]
     return call(
-        functools.partial(sum_kernel, owners, columns, tables),
+        functools.partial(sum_kernel, owners),
         jax.ShapeDtypeStruct((stored, half_x, brick_y, lanes), f32),
         [smem] + [vmem] * owners,
         vmem,
-    )(info, *returned)
+    )(rows, *returned)
 
 
 def solution(mesh):

time: 111 us -> 104 us (0.937)
  Pallas kernels: 50.7 us -> 47.2 us
  waiting for transfers between devices: 21 us -> 17.6 us
  starting transfers between devices: 22.1 us -> 19.8 us
  matrix products: 11.6 us -> 13.1 us
    pallas_call x2, Pallas kernels: 42.3 us -> 39.4 us  [run_steps(): call(functools.partial(steps_kernel, sides, span, pulses_of), outs, [smem...]
    ppermute x2, waiting for transfers between devices: 3.95 us -> 1.21 us  [shift(): return lax.ppermute(x, 'dom', moves)]
    ppermute x13, starting transfers between devices: 17.5 us -> 15.3 us  [xor_swap(): return lax.ppermute(block, axis, [(i, i ^ bits) for i in range(size)])]
    dot_general x2, matrix products: 11.6 us -> 13.1 us  [product(): jnp.einsum('rp,kpz->krz', rows, spread, preferred_element_type=jnp.float32)]
    pallas_call x3, Pallas kernels: 5.49 us -> 4.33 us  [the longest x1 2.13 us: per_device(): call(functools.partial(unpack_kernel, owners, columns, tables, stored), [...]
  transfers between devices with their start and end apart: 16 -> 16, of which waited for: 7 -> 7; matrix products, arithmetic and copies ran while one was open for 14% -> 17% of each run, Pallas kernels for 12% -> 12%
where the time goes in v5:
time: 104 us; the launch traced here: 103 us
  Pallas kernels  47.2 us (45%)
  starting transfers between devices  19.8 us (19%)
  waiting for transfers between devices  17.6 us (17%)
  matrix products  13.1 us (13%)
  other arithmetic  3.43 us (3%)
  between operations  1.47 us (1%)
    pallas_call x2, Pallas kernels, run_steps(): call(functools.partial(steps_kernel, sides, span, pulses_of), outs, [smem...  39.4 us
    ppermute x13, waiting for transfers between devices, xor_swap(): return lax.ppermute(block, axis, [(i, i ^ bits) for i in range(size)])  16.4 us
    ppermute x13, starting transfers between devices, xor_swap(): return lax.ppermute(block, axis, [(i, i ^ bits) for i in range(size)])  15.3 us
    dot_general x2, matrix products, product(): jnp.einsum('rp,kpz->krz', rows, spread, preferred_element_type=jnp.float32)  13.1 us
    pallas_call x1, Pallas kernels, per_device(): call(functools.partial(pack_kernel, owners, columns, tables), [brick] * o...  2.96 us
    ppermute x2, starting transfers between devices, shift(): return lax.ppermute(x, 'dom', moves)  2.31 us
    ppermute x1, starting transfers between devices, shift(): lax.ppermute(x, ('dom', 'pair'), [(i * pairs, j * pairs) for i, j in moves])  2.23 us
    pallas_call x1, Pallas kernels, per_device(): call(functools.partial(unpack_kernel, owners, columns, tables, stored), [...  2.13 us
  transfers between devices with their start and end apart: 16, of which 7 were waited for; matrix products, arithmetic and copies ran while one was open for 17% of the time, Pallas kernels for 12%

profile of v5, /device:TPU:0, one launch (start us, length us, event | category | flops | bytes accessed | tf_op | source)
XLA Modules:
  0.0 103.4 jit_solution(16073189299245720103)
XLA Ops:
  0.0 5.0 %collective-permute-start.2 = (s32[16]{0:T(128)}, s32[16]{0:T(128)S(1)}, u32[]{:S(2)}, u32[]{:S(2)}) collective-permute-start(s32[16]{0:T(128)} %bitcast.35), channel_id=1, source_target_pairs={{0,12},{4,8},{8,4},{12,0},{1,13},{5,9},{9,5},{13,1},{2,14},{6,10},... | collective-permute-start | bytes 200 | tf_op jit(solution)/shard_map/ppermute | solution.py:64
  5.0 0.0 collective-permute-start.1
  5.1 0.6 collective-permute-start
  5.6 1.7 %collective-permute-start.10 = (f32[2,32,32,128]{3,2,1,0:T(8,128)}, f32[2,32,32,128]{3,2,1,0:T(8,128)S(1)}, u32[]{:S(2)}, u32[]{:S(2)}) collective-permute-start(f32[2,32,32,128]{3,2,1,0:T(8,128)} %bitcast.32), channel_id=1, source_target_pairs={{0,2},{2,0},{1,3},{3,1},{4,6},{6,4},{5,7},{7,5},{8,10},{10,8},{9,1... | collective-permute-start | bytes 3145736 | tf_op jit(solution)/shard_map/ppermute | solution.py:74
  8.6 0.7 negate_bitcast_fusion
  9.3 0.1 copy.25
  9.4 0.8 iota_compare_fusion
  10.2 0.8 fusion.8
  11.0 1.0 broadcast_select_fusion.table
  12.0 0.0 collective-permute-done.2
  12.0 0.0 collective-permute-done.1
  12.0 0.0 collective-permute-done
  12.0 0.8 concatenate.25.info
  12.8 3.0 %shard_map.145 = (f32[4,8,8,128]{3,2,1,0:T(8,128)S(1)}, f32[4,8,8,128]{3,2,1,0:T(8,128)S(1)}, f32[4,8,8,128]{3,2,1,0:T(8,128)S(1)}, f32[4,8,8,128]{3,2,1,0:T(8,128)S(1)}, s32[16]{0:T(128)S(1)}) custom-call(s32[132]{0:T(256)S(1)} %concatenate.25.info, f32[8,8,8,128]{3,2,1,0:T(8,128)S(1)} %broadcast_select_fusion.table), custom_call_target="tpu_custom_call" | custom-call | flops 1 | bytes 1 | tf_op jit(solution)/shard_map/pallas_call | solution.py:654
  15.8 1.3 %collective-permute-start.3 = (f32[4,8,8,128]{3,2,1,0:T(8,128)S(1)}, f32[4,8,8,128]{3,2,1,0:T(8,128)S(1)}, u32[]{:S(2)}, u32[]{:S(2)}) collective-permute-start(f32[4,8,8,128]{3,2,1,0:T(8,128)S(1)} %get-tuple-element.33), channel_id=1, source_target_pairs={{0,4},{4,0},{8,12},{12,8},{1,5},{5,1},{9,13},{13,9},{2,6},{6,2},{1... | collective-permute-start | bytes 393224 | tf_op jit(solution)/shard_map/ppermute | solution.py:64
  17.1 2.9 %collective-permute-start.4 = (f32[4,8,8,128]{3,2,1,0:T(8,128)S(1)}, f32[4,8,8,128]{3,2,1,0:T(8,128)S(1)}, u32[]{:S(2)}, u32[]{:S(2)}) collective-permute-start(f32[4,8,8,128]{3,2,1,0:T(8,128)S(1)} %get-tuple-element.34), channel_id=1, source_target_pairs={{0,8},{4,12},{8,0},{12,4},{1,9},{5,13},{9,1},{13,5},{2,10},{6,14},... | collective-permute-start | bytes 393224 | tf_op jit(solution)/shard_map/ppermute | solution.py:64
  20.0 0.2 collective-permute-start.5
  20.3 2.2 %collective-permute-start.7 = (f32[16,2,32,128]{3,2,1,0:T(8,128)}, f32[16,2,32,128]{3,2,1,0:T(8,128)S(1)}, u32[]{:S(2)}, u32[]{:S(2)}) collective-permute-start(f32[16,2,32,128]{3,2,1,0:T(8,128)} %bitcast.29), channel_id=1, source_target_pairs={{0,2},{2,0},{4,6},{6,4},{8,10},{10,8},{12,14},{14,12},{16,18},{18,... | collective-permute-start | bytes 1572872 | tf_op jit(solution)/shard_map/ppermute | solution.py:73
  22.5 0.0 collective-permute-done.3.refs_1_
  22.6 7.3 %collective-permute-done.4.refs_2_ = f32[4,8,8,128]{3,2,1,0:T(8,128)S(1)} collective-permute-done((f32[4,8,8,128]{3,2,1,0:T(8,128)S(1)}, f32[4,8,8,128]{3,2,1,0:T(8,128)S(1)}, u32[]{:S(2)}, u32[]{:S(2)}) %collective-permute-start.4) | collective-permute-done | bytes 131104 | tf_op jit(solution)/shard_map/ppermute | solution.py:64
  29.9 0.0 collective-permute-done.5.refs_3_
  29.9 2.1 %shard_map.146 = (f32[16,8,8,128]{3,2,1,0:T(8,128)S(1)}, s32[16]{0:T(128)S(1)}) custom-call(s32[132]{0:T(256)S(1)} %concatenate.25.info, f32[4,8,8,128]{3,2,1,0:T(8,128)S(1)} %get-tuple-element.32.refs_0_, f32[4,8,8,128]{3,2,1,0:T(8,128)S(1)} %collective-permute-done.3.refs_1_, f32[4,8,8,128]{3,2,1,0:T(8,128)S(1)} %collective-permute-done.4.refs_2_, ...), custom_call_target="tpu_custom_call" | custom-call | flops 1 | bytes 1 | tf_op jit(solution)/shard_map/pallas_call | solution.py:662
  32.0 0.6 collective-permute-start.6
  32.6 10.7 %fusion.2.refs_0_ = f32[13,2048,128]{2,1,0:T(8,128)} fusion(pred[2048,512]{1,0:T(32,128)(4,1)S(1)} %iota_compare_fusion, f32[1024,128]{0,1:T(8,128)S(1)} %add_convert_fusion, f32[16,1024]{1,0:T(8,128)S(1)} %pad_maximum_fusion), kind=kOutput, calls=%fused_computation.4 | convolution fusion | flops 6985613312 | bytes 15269888 | tf_op jit(solution)/shard_map/rp,kpz->krz/dot_general | solution.py:592
  43.3 0.0 copy-start
  43.3 0.0 copy-start.1
  43.3 0.0 copy-start.2
  43.3 0.0 copy-start.3
  43.4 2.4 %fusion.7.refs_0_ = f32[3,2048,128]{2,1,0:T(8,128)S(1)} fusion(pred[2048,512]{1,0:T(32,128)(4,1)S(1)} %iota_compare_fusion, f32[1024,128]{0,1:T(8,128)S(1)} %add_convert_fusion, f32[16,1024]{1,0:T(8,128)S(1)} %pad_maximum_fusion), kind=kOutput, calls=%fused_computation.10 | convolution fusion | flops 1616904192 | bytes 4784128 | tf_op jit(solution)/shard_map/rp,kpz->krz/dot_general | solution.py:592
  45.7 0.1 collective-permute-start.8
  45.8 0.0 collective-permute-done.7.refs_2_
  45.8 1.2 %collective-permute-done.6.refs_4_ = f32[16,8,8,128]{3,2,1,0:T(8,128)S(1)} collective-permute-done((f32[16,8,8,128]{3,2,1,0:T(8,128)S(1)}, f32[16,8,8,128]{3,2,1,0:T(8,128)S(1)}, u32[]{:S(2)}, u32[]{:S(2)}) %collective-permute-start.6) | collective-permute-done | bytes 524320 | tf_op jit(solution)/shard_map/ppermute | solution.py:74
  47.0 0.0 collective-permute-start.9
  47.0 0.1 pad_add_fusion.meta
  47.1 0.6 collective-permute-done.8.refs_5_
  47.7 0.0 collective-permute-done.10.refs_8_
  47.7 1.2 %collective-permute-done.9.refs_6_ = f32[16,8,8,128]{3,2,1,0:T(8,128)S(1)} collective-permute-done((f32[16,8,8,128]{3,2,1,0:T(8,128)S(1)}, f32[16,8,8,128]{3,2,1,0:T(8,128)S(1)}, u32[]{:S(2)}, u32[]{:S(2)}) %collective-permute-start.9) | collective-permute-done | bytes 524320 | tf_op jit(solution)/shard_map/ppermute | solution.py:64
  48.9 0.0 copy-done
  48.9 0.0 copy-done.1
  48.9 0.0 copy-done.2
  48.9 0.0 copy-done.3
  49.0 33.0 %shard_map.147 = (f32[13,4,4,32,128]{4,3,2,1,0:T(8,128)S(1)}, f32[13,4,4,32,128]{4,3,2,1,0:T(8,128)S(1)}, f32[2,72,32,128]{3,2,1,0:T(8,128)S(1)}, f32[64,32,128]...) custom-call(s32[4]{0:T(128)S(1)} %pad_add_fusion.meta, ...), custom_call_target="tpu_custom_call" | custom-call | flops 6979321856 | bytes 1 | tf_op jit(solution)/shard_map/pallas_call | solution.py:551
  82.0 0.2 collective-permute-start.11
  82.2 6.3 %shard_map.149 = (f32[3,4,4,32,128]{4,3,2,1,0:T(8,128)S(1)}, f32[3,4,4,32,128]{4,3,2,1,0:T(8,128)S(1)}) custom-call(s32[4]{0:T(128)S(1)} %pad_add_fusion.meta, bf16[256,256]{1,0:T(8,128)(2,1)S(1)} %copy-done.2, bf16[256,256]{1,0:T(8,128)(2,1)S(1)} %copy-done.1, f32[3,2048,128]{2,1,0:T(8,128)S(1)} %fusion.7.refs_0_, f32[16,2,32,128]{3,2,1,0:T(8,128)S(1)} %bitcast.31, ...), custom_call_target="tpu_custom_call" | custom-call | flops 1610612736 | bytes 1 | tf_op jit(solution)/shard_map/pallas_call | solution.py:551
  88.5 0.4 collective-permute-start.12
  89.0 0.0 collective-permute-done.11.got
  89.0 0.5 shard_map.148.before
  89.5 1.4 %collective-permute-done.12.got = f32[3,4,4,32,128]{4,3,2,1,0:T(8,128)S(1)} collective-permute-done((f32[3,4,4,32,128]{4,3,2,1,0:T(8,128)S(1)}, f32[3,4,4,32,128]{4,3,2,1,0:T(8,128)S(1)}, u32[]{:S(2)}, u32[]{:S(2)}) %collective-permute-start.12) | collective-permute-done | bytes 786464 | tf_op jit(solution)/shard_map/ppermute | solution.py:64
  90.9 0.9 shard_map.150
  91.9 1.6 %collective-permute-start.13 = (f32[4,4,8,128]{3,2,1,0:T(8,128)S(1)}, f32[4,4,8,128]{3,2,1,0:T(8,128)S(1)}, u32[]{:S(2)}, u32[]{:S(2)}) collective-permute-start(f32[4,4,8,128]{3,2,1,0:T(8,128)S(1)} %get-tuple-element.54), channel_id=1, source_target_pairs={{0,4},{4,0},{8,12},{12,8},{1,5},{5,1},{9,13},{13,9},{2,6},{6,2},{1... | collective-permute-start | bytes 196616 | tf_op jit(solution)/shard_map/ppermute | solution.py:64
  93.4 2.6 %collective-permute-start.14 = (f32[4,4,8,128]{3,2,1,0:T(8,128)S(1)}, f32[4,4,8,128]{3,2,1,0:T(8,128)S(1)}, u32[]{:S(2)}, u32[]{:S(2)}) collective-permute-start(f32[4,4,8,128]{3,2,1,0:T(8,128)S(1)} %get-tuple-element.55), channel_id=1, source_target_pairs={{0,8},{4,12},{8,0},{12,4},{1,9},{5,13},{9,1},{13,5},{2,10},{6,14},... | collective-permute-start | bytes 196616 | tf_op jit(solution)/shard_map/ppermute | solution.py:64
  96.0 0.3 collective-permute-start.15
  96.3 0.0 collective-permute-done.13.refs_1_
  96.3 4.8 %collective-permute-done.14.refs_2_ = f32[4,4,8,128]{3,2,1,0:T(8,128)S(1)} collective-permute-done((f32[4,4,8,128]{3,2,1,0:T(8,128)S(1)}, f32[4,4,8,128]{3,2,1,0:T(8,128)S(1)}, u32[]{:S(2)}, u32[]{:S(2)}) %collective-permute-start.14) | collective-permute-done | bytes 65568 | tf_op jit(solution)/shard_map/ppermute | solution.py:64
  101.2 1.0 collective-permute-done.15.refs_3_
  102.2 1.3 %shard_map.151 = f32[8,4,8,128]{3,2,1,0:T(8,128)} custom-call(s32[16]{0:T(128)S(1)} %get-tuple-element.31.rows, f32[4,4,8,128]{3,2,1,0:T(8,128)S(1)} %get-tuple-element.53.refs_0_, f32[4,4,8,128]{3,2,1,0:T(8,128)S(1)} %collective-permute-done.13.refs_1_, f32[4,4,8,128]{3,2,1,0:T(8,128)S(1)} %collective-permute-done.14.refs_2_, ...), custom_call_target="tpu_custom_call" | custom-call | flops 1 | bytes 1 | tf_op jit(solution)/shard_map/pallas_call | solution.py:709
  (4 shorter events, 0.1 us)
Async XLA Ops:
  0.0 12.0 %collective-permute-start.2 = (s32[16]{0:T(128)}, s32[16]{0:T(128)S(1)}, u32[]{:S(2)}, u32[]{:S(2)}) collective-permute-start(s32[16]{0:T(128)} %bitcast.35), channel_id=1, source_target_pairs={{0,12},{4,8},{8,4},{12,0},{1,13},{5,9},{9,5},{13,1},{2,14},{6,10},... | collective-permute-start | bytes 200 | tf_op jit(solution)/shard_map/ppermute | solution.py:64
  5.0 6.9 %collective-permute-start.1 = (s32[16]{0:T(128)}, s32[16]{0:T(128)S(1)}, u32[]{:S(2)}, u32[]{:S(2)}) collective-permute-start(s32[16]{0:T(128)} %bitcast.36), channel_id=1, source_target_pairs={{0,8},{4,12},{8,0},{12,4},{1,9},{5,13},{9,1},{13,5},{2,10},{6,14},... | collective-permute-start | bytes 200 | tf_op jit(solution)/shard_map/ppermute | solution.py:64
  5.1 6.9 %collective-permute-start = (s32[16]{0:T(128)}, s32[16]{0:T(128)S(1)}, u32[]{:S(2)}, u32[]{:S(2)}) collective-permute-start(s32[16]{0:T(128)} %bitcast.37), channel_id=1, source_target_pairs={{0,4},{4,0},{8,12},{12,8},{1,5},{5,1},{9,13},{13,9},{2,6},{6,2},{1... | collective-permute-start | bytes 200 | tf_op jit(solution)/shard_map/ppermute | solution.py:64
  5.6 42.1 %collective-permute-start.10 = (f32[2,32,32,128]{3,2,1,0:T(8,128)}, f32[2,32,32,128]{3,2,1,0:T(8,128)S(1)}, u32[]{:S(2)}, u32[]{:S(2)}) collective-permute-start(f32[2,32,32,128]{3,2,1,0:T(8,128)} %bitcast.32), channel_id=1, source_target_pairs={{0,2},{2,0},{1,3},{3,1},{4,6},{6,4},{5,7},{7,5},{8,10},{10,8},{9,1... | collective-permute-start | bytes 3145736 | tf_op jit(solution)/shard_map/ppermute | solution.py:74
  15.8 6.8 %collective-permute-start.3 = (f32[4,8,8,128]{3,2,1,0:T(8,128)S(1)}, f32[4,8,8,128]{3,2,1,0:T(8,128)S(1)}, u32[]{:S(2)}, u32[]{:S(2)}) collective-permute-start(f32[4,8,8,128]{3,2,1,0:T(8,128)S(1)} %get-tuple-element.33), channel_id=1, source_target_pairs={{0,4},{4,0},{8,12},{12,8},{1,5},{5,1},{9,13},{13,9},{2,6},{6,2},{1... | collective-permute-start | bytes 393224 | tf_op jit(solution)/shard_map/ppermute | solution.py:64
  17.1 12.8 %collective-permute-start.4 = (f32[4,8,8,128]{3,2,1,0:T(8,128)S(1)}, f32[4,8,8,128]{3,2,1,0:T(8,128)S(1)}, u32[]{:S(2)}, u32[]{:S(2)}) collective-permute-start(f32[4,8,8,128]{3,2,1,0:T(8,128)S(1)} %get-tuple-element.34), channel_id=1, source_target_pairs={{0,8},{4,12},{8,0},{12,4},{1,9},{5,13},{9,1},{13,5},{2,10},{6,14},... | collective-permute-start | bytes 393224 | tf_op jit(solution)/shard_map/ppermute | solution.py:64
  20.0 9.8 %collective-permute-start.5 = (f32[4,8,8,128]{3,2,1,0:T(8,128)S(1)}, f32[4,8,8,128]{3,2,1,0:T(8,128)S(1)}, u32[]{:S(2)}, u32[]{:S(2)}) collective-permute-start(f32[4,8,8,128]{3,2,1,0:T(8,128)S(1)} %get-tuple-element.35), channel_id=1, source_target_pairs={{0,12},{4,8},{8,4},{12,0},{1,13},{5,9},{9,5},{13,1},{2,14},{6,10},... | collective-permute-start | bytes 393224 | tf_op jit(solution)/shard_map/ppermute | solution.py:64
  20.3 25.5 %collective-permute-start.7 = (f32[16,2,32,128]{3,2,1,0:T(8,128)}, f32[16,2,32,128]{3,2,1,0:T(8,128)S(1)}, u32[]{:S(2)}, u32[]{:S(2)}) collective-permute-start(f32[16,2,32,128]{3,2,1,0:T(8,128)} %bitcast.29), channel_id=1, source_target_pairs={{0,2},{2,0},{4,6},{6,4},{8,10},{10,8},{12,14},{14,12},{16,18},{18,... | collective-permute-start | bytes 1572872 | tf_op jit(solution)/shard_map/ppermute | solution.py:73
  32.0 15.0 %collective-permute-start.6 = (f32[16,8,8,128]{3,2,1,0:T(8,128)S(1)}, f32[16,8,8,128]{3,2,1,0:T(8,128)S(1)}, u32[]{:S(2)}, u32[]{:S(2)}) collective-permute-start(f32[16,8,8,128]{3,2,1,0:T(8,128)S(1)} %get-tuple-element.37.refs_3_), channel_id=1, source_target_pairs={{0,2},{2,0},{1,3},{3,1},{4,6},{6,4},{5,7},{7,5},{8,10},{10,8},{9,1... | collective-permute-start | bytes 1572872 | tf_op jit(solution)/shard_map/ppermute | solution.py:74
  43.3 5.6 %copy-start = (f32[1,16,2,32,128]{4,3,2,1,0:T(8,128)S(1)}, f32[1,16,2,32,128]{4,3,2,1,0:T(8,128)}, u32[]{:S(2)}) copy-start(f32[1,16,2,32,128]{4,3,2,1,0:T(8,128)} %param.25) | copy-start | bytes 1572868
  43.3 5.6 %copy-start.1 = (bf16[256,256]{1,0:T(8,128)(2,1)S(1)}, bf16[256,256]{1,0:T(8,128)(2,1)}, u32[]{:S(2)}) copy-start(bf16[256,256]{1,0:T(8,128)(2,1)} %constant.53.clone.ymat) | copy-start | bytes 393220
  43.3 5.6 %copy-start.2 = (bf16[256,256]{1,0:T(8,128)(2,1)S(1)}, bf16[256,256]{1,0:T(8,128)(2,1)}, u32[]{:S(2)}) copy-start(bf16[256,256]{1,0:T(8,128)(2,1)} %constant.52.clone.zmat) | copy-start | bytes 393220
  43.3 5.6 %copy-start.3 = (f32[1,1,2,32,32,128]{5,4,3,2,1,0:T(8,128)S(1)}, f32[1,1,2,32,32,128]{5,4,3,2,1,0:T(8,128)}, u32[]{:S(2)}) copy-start(f32[1,1,2,32,32,128]{5,4,3,2,1,0:T(8,128)} %param.24) | copy-start | bytes 3145732
  45.7 2.0 %collective-permute-start.8 = (f32[16,8,8,128]{3,2,1,0:T(8,128)S(1)}, f32[16,8,8,128]{3,2,1,0:T(8,128)S(1)}, u32[]{:S(2)}, u32[]{:S(2)}) collective-permute-start(f32[16,8,8,128]{3,2,1,0:T(8,128)S(1)} %get-tuple-element.37.refs_3_), channel_id=1, source_target_pairs={{0,1},{1,0},{2,3},{3,2},{4,5},{5,4},{6,7},{7,6},{8,9},{9,8},{10,11... | collective-permute-start | bytes 1572872 | tf_op jit(solution)/shard_map/ppermute | solution.py:64
  47.0 1.9 %collective-permute-start.9 = (f32[16,8,8,128]{3,2,1,0:T(8,128)S(1)}, f32[16,8,8,128]{3,2,1,0:T(8,128)S(1)}, u32[]{:S(2)}, u32[]{:S(2)}) collective-permute-start(f32[16,8,8,128]{3,2,1,0:T(8,128)S(1)} %collective-permute-done.6.refs_4_), channel_id=1, source_target_pairs={{0,1},{1,0},{2,3},{3,2},{4,5},{5,4},{6,7},{7,6},{8,9},{9,8},{10,11... | collective-permute-start | bytes 1572872 | tf_op jit(solution)/shard_map/ppermute | solution.py:64
  82.0 7.0 %collective-permute-start.11 = (f32[13,4,4,32,128]{4,3,2,1,0:T(8,128)S(1)}, f32[13,4,4,32,128]{4,3,2,1,0:T(8,128)S(1)}, u32[]{:S(2)}, u32[]{:S(2)}) collective-permute-start(f32[13,4,4,32,128]{4,3,2,1,0:T(8,128)S(1)} %get-tuple-element.43), channel_id=1, source_target_pairs={{0,1},{1,0},{2,3},{3,2},{4,5},{5,4},{6,7},{7,6},{8,9},{9,8},{10,11... | collective-permute-start | bytes 10223624 | tf_op jit(solution)/shard_map/ppermute | solution.py:64
  88.5 2.4 %collective-permute-start.12 = (f32[3,4,4,32,128]{4,3,2,1,0:T(8,128)S(1)}, f32[3,4,4,32,128]{4,3,2,1,0:T(8,128)S(1)}, u32[]{:S(2)}, u32[]{:S(2)}) collective-permute-start(f32[3,4,4,32,128]{4,3,2,1,0:T(8,128)S(1)} %get-tuple-element.52), channel_id=1, source_target_pairs={{0,1},{1,0},{2,3},{3,2},{4,5},{5,4},{6,7},{7,6},{8,9},{9,8},{10,11... | collective-permute-start | bytes 2359304 | tf_op jit(solution)/shard_map/ppermute | solution.py:64
  91.9 4.5 %collective-permute-start.13 = (f32[4,4,8,128]{3,2,1,0:T(8,128)S(1)}, f32[4,4,8,128]{3,2,1,0:T(8,128)S(1)}, u32[]{:S(2)}, u32[]{:S(2)}) collective-permute-start(f32[4,4,8,128]{3,2,1,0:T(8,128)S(1)} %get-tuple-element.54), channel_id=1, source_target_pairs={{0,4},{4,0},{8,12},{12,8},{1,5},{5,1},{9,13},{13,9},{2,6},{6,2},{1... | collective-permute-start | bytes 196616 | tf_op jit(solution)/shard_map/ppermute | solution.py:64
  93.4 7.7 %collective-permute-start.14 = (f32[4,4,8,128]{3,2,1,0:T(8,128)S(1)}, f32[4,4,8,128]{3,2,1,0:T(8,128)S(1)}, u32[]{:S(2)}, u32[]{:S(2)}) collective-permute-start(f32[4,4,8,128]{3,2,1,0:T(8,128)S(1)} %get-tuple-element.55), channel_id=1, source_target_pairs={{0,8},{4,12},{8,0},{12,4},{1,9},{5,13},{9,1},{13,5},{2,10},{6,14},... | collective-permute-start | bytes 196616 | tf_op jit(solution)/shard_map/ppermute | solution.py:64
  96.0 6.1 %collective-permute-start.15 = (f32[4,4,8,128]{3,2,1,0:T(8,128)S(1)}, f32[4,4,8,128]{3,2,1,0:T(8,128)S(1)}, u32[]{:S(2)}, u32[]{:S(2)}) collective-permute-start(f32[4,4,8,128]{3,2,1,0:T(8,128)S(1)} %get-tuple-element.56), channel_id=1, source_target_pairs={{0,12},{4,8},{8,4},{12,0},{1,13},{5,9},{9,5},{13,1},{2,14},{6,10},... | collective-permute-start | bytes 196616 | tf_op jit(solution)/shard_map/ppermute | solution.py:64

commit v6 on v5

--- a/solution.py
+++ b/solution.py
@@ -244,7 +244,7 @@
                     gz[x, part, :] = scale * z[g * n + at : g * n + at + 8, lanes:]
         return carry
 
-    lax.fori_loop(0, window // BLOCK, bend, 0)
+    lax.fori_loop(0, window // BLOCK, bend, 0, unroll=2)
 
 
 def steps_kernel(sides, span, pulses_of, meta, zmat, ymat, *refs):
@@ -569,7 +569,7 @@
     )(meta, z_matrix(lanes), y_matrix(height, 4), *injects, *rims, *inputs)
 
 
-def injection(window, offset, split, late, height, lanes, is_source, source_cell, receivers, pulses, recorded):
+def injection(window, offset, spans, late, height, lanes, is_source, source_cell, receivers, pulses, recorded):
     steps, spots = recorded.shape
     none = jnp.full((spots - 1,), -1, jnp.int32)
     cells = jnp.where(is_source, jnp.concatenate([source_cell, none]), receivers)
@@ -592,10 +592,9 @@
         return jnp.einsum("rp,kpz->krz", rows, spread, preferred_element_type=jnp.float32)
 
     lo, hi = late
-    return (
-        product(twice, spread[:split]),
-        product(twice[lo * height : hi * height], spread[split:]),
-    )
+    found = [product(twice, spread[first:last]) for first, last in spans[:-1]]
+    first, last = spans[-1]
+    return found + [product(twice[lo * height : hi * height], spread[first:last])]
 
 
 def per_device(
@@ -631,8 +630,10 @@
     tables = (owner_map.shape[0], slots)
 
     table = jnp.where(pair == 0, velocity, density)
-    prints = [footprint[0]] + [xor_swap(footprint[0], "shot", b) for b in range(1, owners)]
-    info = jnp.concatenate([meta, owner_map, *prints])
+    prints = footprint[0]
+    for bits in range(owners.bit_length() - 1):
+        prints = jnp.concatenate([prints, xor_swap(prints, "shot", 1 << bits)])
+    info = jnp.concatenate([meta, owner_map, prints])
     split = 13 if sides else 8
     if sides:
         offset = 0
@@ -643,10 +644,11 @@
         window = (2 * HOPS + 1) * thick
         deep = REACH * (steps - 1 - split)
         late = (HOPS * thick - deep, (HOPS + 1) * thick + deep)
-    early_inject, late_inject = injection(
-        window, offset, split, late, height, lanes, pair == 0,
-        source_cell, receiver_cells[0], wavelet[0], traces[0],
+    spots, info = lax.optimization_barrier(
+        ((source_cell, receiver_cells[0], wavelet[0], traces[0]), info)
     )
+    spans = ((0, 3), (3, 13), (13, steps)) if sides else ((0, split), (split, steps))
+    injects = injection(window, offset, spans, late, height, lanes, pair == 0, *spots)
     brick = jax.ShapeDtypeStruct((per_owner, brick_x, brick_y, lanes), f32)
 
     fields = slabs_of(states[0, 0])
@@ -659,6 +661,8 @@
         [pltpu.SemaphoreType.DMA((owners, per_owner))],
     )(info, table)
     got = [packed[0]] + [xor_swap(packed[b], "shot", b) for b in range(1, owners)]
+    if sides:
+        got[0], injects[0] = lax.optimization_barrier((got[0], injects[0]))
     bricks, places = call(
         functools.partial(unpack_kernel, owners, columns, tables, stored),
         [jax.ShapeDtypeStruct((slots, brick_x, brick_y, lanes), f32), listed],
@@ -670,17 +674,16 @@
     if sides:
         rims_here, _ = lax.optimization_barrier((stored_rims[0], info))
         rim_slabs = slabs_of(rims_here, first_only=True)
-        mine[1], early_inject, late_inject, rim_slabs[1] = lax.optimization_barrier(
-            (mine[1], early_inject, late_inject, rim_slabs[1])
-        )
-        theirs = [xor_swap(slab, "pair", 1) for slab in mine]
+        theirs = [xor_swap(mine[0], "pair", 1)]
+        mine[1], injects, rim_slabs[1] = lax.optimization_barrier((mine[1], injects, rim_slabs[1]))
+        theirs.append(xor_swap(mine[1], "pair", 1))
         keep, send, *carried = run_steps(
-            sides, (0, split, steps), [(0, split, 0)], shape, meta, [early_inject], rim_slabs,
+            sides, (0, split, steps), [(*spans[0], 0), (*spans[1], 0)], shape, meta, injects[:2], rim_slabs,
             [*mine, *theirs, *fields],
         )
         partner = xor_swap(send, "pair", 1)
         keep_last, send_last = run_steps(
-            sides, (split, steps, steps), [(split, steps, 0)], shape, meta, [late_inject], rim_slabs,
+            sides, (split, steps, steps), [(split, steps, 0)], shape, meta, injects[2:], rim_slabs,
             carried,
         )
         total = call(
@@ -690,7 +693,7 @@
         theirs = [xor_swap(slab, "pair", 1) for slab in mine]
         keep_last, send_last = run_steps(
             sides, (0, steps, steps), [(0, split, 0), (split, steps, late[0] * height)], shape, meta,
-            [early_inject, late_inject], slabs_of(stored_rims[0], first_only=True),
+            injects, slabs_of(stored_rims[0], first_only=True),
             [*mine, *theirs, *fields],
         )
         total = jnp.zeros(keep_last.shape[1:], f32)

time: 104 us -> 101 us (0.971)
  starting transfers between devices: 19.8 us -> 25.7 us
  Pallas kernels: 47.2 us -> 41.9 us
  waiting for transfers between devices: 17.6 us -> 14.7 us
    ppermute x13 -> x12, starting transfers between devices: 15.3 us -> 21.2 us  [xor_swap(): return lax.ppermute(block, axis, [(i, i ^ bits) for i in range(size)])]
    pallas_call x2, Pallas kernels: 39.4 us -> 33.9 us  [run_steps(): call(functools.partial(steps_kernel, sides, span, pulses_of), outs, [smem...]
    ppermute x13 -> x12, waiting for transfers between devices: 16.4 us -> 13.4 us  [xor_swap(): return lax.ppermute(block, axis, [(i, i ^ bits) for i in range(size)])]
    dot_general x2 -> x3, matrix products: 13.1 us -> 13 us  [product(): jnp.einsum('rp,kpz->krz', rows, spread, preferred_element_type=jnp.float32)]
  transfers between devices with their start and end apart: 16 -> 15, of which waited for: 7 -> 8; matrix products, arithmetic and copies ran while one was open for 17% -> 17% of each run, Pallas kernels for 12% -> 12%
where the time goes in v6:
time: 101 us
  Pallas kernels  41.9 us (41%)
  starting transfers between devices  25.7 us (25%)
  waiting for transfers between devices  14.7 us (15%)
  matrix products  13 us (13%)
  other arithmetic  3.42 us (3%)
  between operations  1.48 us (1%)
    pallas_call x2, Pallas kernels, run_steps(): call(functools.partial(steps_kernel, sides, span, pulses_of), outs, [smem...  33.9 us
    ppermute x12, starting transfers between devices, xor_swap(): return lax.ppermute(block, axis, [(i, i ^ bits) for i in range(size)])  21.2 us
    ppermute x12, waiting for transfers between devices, xor_swap(): return lax.ppermute(block, axis, [(i, i ^ bits) for i in range(size)])  13.4 us
    dot_general x3, matrix products, product(): jnp.einsum('rp,kpz->krz', rows, spread, preferred_element_type=jnp.float32)  13 us
    pallas_call x1, Pallas kernels, per_device(): call(functools.partial(pack_kernel, owners, columns, tables), [brick] * o...  2.96 us
    ppermute x1, starting transfers between devices, shift(): lax.ppermute(x, ('dom', 'pair'), [(i * pairs, j * pairs) for i, j in moves])  2.45 us
    pallas_call x1, Pallas kernels, per_device(): call(functools.partial(unpack_kernel, owners, columns, tables, stored), [...  2.31 us
    ppermute x2, starting transfers between devices, shift(): return lax.ppermute(x, 'dom', moves)  2.1 us
  transfers between devices with their start and end apart: 15, of which 8 were waited for; matrix products, arithmetic and copies ran while one was open for 17% of the time, Pallas kernels for 12%

profile of v6, /device:TPU:0, one launch (start us, length us, event | category | flops | bytes accessed | tf_op | source)
XLA Modules:
  0.0 100.9 jit_solution(7874044456260041688)
XLA Ops:
  0.0 3.0 %collective-permute-start = (s32[16]{0:T(128)}, s32[16]{0:T(128)S(1)}, u32[]{:S(2)}, u32[]{:S(2)}) collective-permute-start(s32[16]{0:T(128)} %bitcast.33), channel_id=1, source_target_pairs={{0,4},{4,0},{8,12},{12,8},{1,5},{5,1},{9,13},{13,9},{2,6},{6,2},{1... | collective-permute-start | bytes 200 | tf_op jit(solution)/shard_map/ppermute | solution.py:64
  3.0 1.5 %collective-permute-start.9 = (f32[2,32,32,128]{3,2,1,0:T(8,128)}, f32[2,32,32,128]{3,2,1,0:T(8,128)S(1)}, u32[]{:S(2)}, u32[]{:S(2)}) collective-permute-start(f32[2,32,32,128]{3,2,1,0:T(8,128)} %bitcast.29), channel_id=1, source_target_pairs={{0,2},{2,0},{1,3},{3,1},{4,6},{6,4},{5,7},{7,5},{8,10},{10,8},{9,1... | collective-permute-start | bytes 3145736 | tf_op jit(solution)/shard_map/ppermute | solution.py:74
  5.2 1.0 broadcast_select_fusion.table
  6.8 0.0 collective-permute-done
  6.8 0.7 pad_add_fusion
  7.6 2.6 %collective-permute-start.1 = (s32[32]{0:T(128)S(1)}, s32[32]{0:T(128)S(1)}, u32[]{:S(2)}, u32[]{:S(2)}) collective-permute-start(s32[32]{0:T(128)S(1)} %pad_add_fusion), channel_id=1, source_target_pairs={{0,8},{4,12},{8,0},{12,4},{1,9},{5,13},{9,1},{13,5},{2,10},{6,14},... | collective-permute-start | bytes 392 | tf_op jit(solution)/shard_map/ppermute | solution.py:64
  10.1 1.9 %collective-permute-done.1 = s32[32]{0:T(128)S(1)} collective-permute-done((s32[32]{0:T(128)S(1)}, s32[32]{0:T(128)S(1)}, u32[]{:S(2)}, u32[]{:S(2)}) %collective-permute-start.1) | collective-permute-done | bytes 160 | tf_op jit(solution)/shard_map/ppermute | solution.py:64
  12.0 0.8 concatenate.29.info
  12.7 0.7 negate_bitcast_fusion
  13.5 0.1 copy.27
  13.6 3.0 %shard_map.145 = (f32[4,8,8,128]{3,2,1,0:T(8,128)S(1)}, f32[4,8,8,128]{3,2,1,0:T(8,128)S(1)}, f32[4,8,8,128]{3,2,1,0:T(8,128)S(1)}, f32[4,8,8,128]{3,2,1,0:T(8,128)S(1)}, s32[16]{0:T(128)S(1)}) custom-call(s32[132]{0:T(256)S(1)} %concatenate.29.info, f32[8,8,8,128]{3,2,1,0:T(8,128)S(1)} %broadcast_select_fusion.table), custom_call_target="tpu_custom_call" | custom-call | flops 1 | bytes 1 | tf_op jit(solution)/shard_map/pallas_call | solution.py:656
  16.5 0.5 collective-permute-start.2
  17.0 2.6 %collective-permute-start.3 = (f32[4,8,8,128]{3,2,1,0:T(8,128)S(1)}, f32[4,8,8,128]{3,2,1,0:T(8,128)S(1)}, u32[]{:S(2)}, u32[]{:S(2)}) collective-permute-start(f32[4,8,8,128]{3,2,1,0:T(8,128)S(1)} %get-tuple-element.48), channel_id=1, source_target_pairs={{0,8},{4,12},{8,0},{12,4},{1,9},{5,13},{9,1},{13,5},{2,10},{6,14},... | collective-permute-start | bytes 393224 | tf_op jit(solution)/shard_map/ppermute | solution.py:64
  19.6 1.3 %collective-permute-start.4 = (f32[4,8,8,128]{3,2,1,0:T(8,128)S(1)}, f32[4,8,8,128]{3,2,1,0:T(8,128)S(1)}, u32[]{:S(2)}, u32[]{:S(2)}) collective-permute-start(f32[4,8,8,128]{3,2,1,0:T(8,128)S(1)} %get-tuple-element.49), channel_id=1, source_target_pairs={{0,12},{4,8},{8,4},{12,0},{1,13},{5,9},{9,5},{13,1},{2,14},{6,10},... | collective-permute-start | bytes 393224 | tf_op jit(solution)/shard_map/ppermute | solution.py:64
  21.0 2.4 %collective-permute-start.6 = (f32[16,2,32,128]{3,2,1,0:T(8,128)}, f32[16,2,32,128]{3,2,1,0:T(8,128)S(1)}, u32[]{:S(2)}, u32[]{:S(2)}) collective-permute-start(f32[16,2,32,128]{3,2,1,0:T(8,128)} %bitcast.26), channel_id=1, source_target_pairs={{0,2},{2,0},{4,6},{6,4},{8,10},{10,8},{12,14},{14,12},{16,18},{18,... | collective-permute-start | bytes 1572872 | tf_op jit(solution)/shard_map/ppermute | solution.py:73
  23.5 0.8 iota_compare_fusion
  24.4 2.4 %fusion.10.refs_0_ = f32[3,2048,128]{2,1,0:T(8,128)S(1)} fusion(pred[2048,512]{1,0:T(32,128)(4,1)S(1)} %iota_compare_fusion, f32[1024,128]{0,1:T(8,128)S(1)} %add_convert_fusion, f32[16,1024]{1,0:T(8,128)S(1)} %pad_maximum_fusion), kind=kOutput, calls=%fused_computation.13 | convolution fusion | flops 1616904192 | bytes 4784128 | tf_op jit(solution)/shard_map/rp,kpz->krz/dot_general | solution.py:592
  26.8 0.0 collective-permute-done.2.refs_1_
  26.8 3.1 %collective-permute-done.3.refs_2_ = f32[4,8,8,128]{3,2,1,0:T(8,128)S(1)} collective-permute-done((f32[4,8,8,128]{3,2,1,0:T(8,128)S(1)}, f32[4,8,8,128]{3,2,1,0:T(8,128)S(1)}, u32[]{:S(2)}, u32[]{:S(2)}) %collective-permute-start.3) | collective-permute-done | bytes 131104 | tf_op jit(solution)/shard_map/ppermute | solution.py:64
  29.8 0.0 collective-permute-done.4.refs_3_
  29.8 2.3 %shard_map.146 = (f32[16,8,8,128]{3,2,1,0:T(8,128)S(1)}, s32[16]{0:T(128)S(1)}) custom-call(s32[132]{0:T(256)S(1)} %concatenate.29.info, f32[4,8,8,128]{3,2,1,0:T(8,128)S(1)} %get-tuple-element.46.refs_0_, f32[4,8,8,128]{3,2,1,0:T(8,128)S(1)} %collective-permute-done.2.refs_1_, f32[4,8,8,128]{3,2,1,0:T(8,128)S(1)} %collective-permute-done.3.refs_2_, ...), custom_call_target="tpu_custom_call" | custom-call | flops 1 | bytes 1 | tf_op jit(solution)/shard_map/pallas_call | solution.py:666
  32.2 0.6 collective-permute-start.5
  32.8 8.2 %fusion.3.refs_1_ = f32[10,2048,128]{2,1,0:T(8,128)} fusion(pred[2048,512]{1,0:T(32,128)(4,1)S(1)} %iota_compare_fusion, f32[1024,128]{0,1:T(8,128)S(1)} %add_convert_fusion, f32[16,1024]{1,0:T(8,128)S(1)} %pad_maximum_fusion), kind=kOutput, calls=%fused_computation.5 | convolution fusion | flops 5375000576 | bytes 12124160 | tf_op jit(solution)/shard_map/rp,kpz->krz/dot_general | solution.py:592
  41.0 0.0 copy-start
  41.0 0.0 copy-start.1
  41.0 0.0 copy-start.2
  41.0 0.0 copy-start.3
  41.0 2.4 %fusion.11.refs_0_ = f32[3,2048,128]{2,1,0:T(8,128)S(1)} fusion(pred[2048,512]{1,0:T(32,128)(4,1)S(1)} %iota_compare_fusion, f32[1024,128]{0,1:T(8,128)S(1)} %add_convert_fusion, f32[16,1024]{1,0:T(8,128)S(1)} %pad_maximum_fusion), kind=kOutput, calls=%fused_computation.14 | convolution fusion | flops 1616904192 | bytes 4784128 | tf_op jit(solution)/shard_map/rp,kpz->krz/dot_general | solution.py:592
  43.4 0.1 collective-permute-start.7
  43.4 0.0 collective-permute-done.6.refs_3_.refs_2_
  43.5 1.3 %collective-permute-done.5.refs_5_ = f32[16,8,8,128]{3,2,1,0:T(8,128)S(1)} collective-permute-done((f32[16,8,8,128]{3,2,1,0:T(8,128)S(1)}, f32[16,8,8,128]{3,2,1,0:T(8,128)S(1)}, u32[]{:S(2)}, u32[]{:S(2)}) %collective-permute-start.5) | collective-permute-done | bytes 524320 | tf_op jit(solution)/shard_map/ppermute | solution.py:74
  44.7 0.0 collective-permute-start.8
  44.7 0.1 pad_add_fusion.1.meta
  44.8 0.6 collective-permute-done.7.refs_6_
  45.3 0.0 collective-permute-done.9.refs_9_
  45.3 1.3 %collective-permute-done.8.refs_7_ = f32[16,8,8,128]{3,2,1,0:T(8,128)S(1)} collective-permute-done((f32[16,8,8,128]{3,2,1,0:T(8,128)S(1)}, f32[16,8,8,128]{3,2,1,0:T(8,128)S(1)}, u32[]{:S(2)}, u32[]{:S(2)}) %collective-permute-start.8) | collective-permute-done | bytes 524320 | tf_op jit(solution)/shard_map/ppermute | solution.py:64
  46.6 0.0 copy-done
  46.6 0.0 copy-done.1
  46.6 0.0 copy-done.2
  46.6 0.0 copy-done.3
  46.6 28.0 %shard_map.147 = (f32[13,4,4,32,128]{4,3,2,1,0:T(8,128)S(1)}, f32[13,4,4,32,128]{4,3,2,1,0:T(8,128)S(1)}, f32[2,72,32,128]{3,2,1,0:T(8,128)S(1)}, f32[64,32,128]...) custom-call(s32[4]{0:T(128)S(1)} %pad_add_fusion.1.meta, ...), custom_call_target="tpu_custom_call" | custom-call | flops 6979321856 | bytes 1 | tf_op jit(solution)/shard_map/pallas_call | solution.py:551
  74.6 0.2 collective-permute-start.10
  74.8 5.9 %shard_map.149 = (f32[3,4,4,32,128]{4,3,2,1,0:T(8,128)S(1)}, f32[3,4,4,32,128]{4,3,2,1,0:T(8,128)S(1)}) custom-call(s32[4]{0:T(128)S(1)} %pad_add_fusion.1.meta, bf16[256,256]{1,0:T(8,128)(2,1)S(1)} %copy-done.2, bf16[256,256]{1,0:T(8,128)(2,1)S(1)} %copy-done.1, f32[3,2048,128]{2,1,0:T(8,128)S(1)} %fusion.11.refs_0_, f32[16,2,32,128]{3,2,1,0:T(8,128)S(1)} %bitcast.28, ...), custom_call_target="tpu_custom_call" | custom-call | flops 1610612736 | bytes 1 | tf_op jit(solution)/shard_map/pallas_call | solution.py:551
  80.7 0.4 collective-permute-start.11
  81.2 0.0 collective-permute-done.10.got
  81.2 0.5 shard_map.148.before
  81.7 1.4 %collective-permute-done.11.got = f32[3,4,4,32,128]{4,3,2,1,0:T(8,128)S(1)} collective-permute-done((f32[3,4,4,32,128]{4,3,2,1,0:T(8,128)S(1)}, f32[3,4,4,32,128]{4,3,2,1,0:T(8,128)S(1)}, u32[]{:S(2)}, u32[]{:S(2)}) %collective-permute-start.11) | collective-permute-done | bytes 786464 | tf_op jit(solution)/shard_map/ppermute | solution.py:64
  83.1 0.9 shard_map.150
  84.0 2.1 %collective-permute-start.12 = (f32[4,4,8,128]{3,2,1,0:T(8,128)S(1)}, f32[4,4,8,128]{3,2,1,0:T(8,128)S(1)}, u32[]{:S(2)}, u32[]{:S(2)}) collective-permute-start(f32[4,4,8,128]{3,2,1,0:T(8,128)S(1)} %get-tuple-element.70), channel_id=1, source_target_pairs={{0,4},{4,0},{8,12},{12,8},{1,5},{5,1},{9,13},{13,9},{2,6},{6,2},{1... | collective-permute-start | bytes 196616 | tf_op jit(solution)/shard_map/ppermute | solution.py:64
  86.2 6.9 %collective-permute-start.13 = (f32[4,4,8,128]{3,2,1,0:T(8,128)S(1)}, f32[4,4,8,128]{3,2,1,0:T(8,128)S(1)}, u32[]{:S(2)}, u32[]{:S(2)}) collective-permute-start(f32[4,4,8,128]{3,2,1,0:T(8,128)S(1)} %get-tuple-element.71), channel_id=1, source_target_pairs={{0,8},{4,12},{8,0},{12,4},{1,9},{5,13},{9,1},{13,5},{2,10},{6,14},... | collective-permute-start | bytes 196616 | tf_op jit(solution)/shard_map/ppermute | solution.py:64
  93.0 1.4 %collective-permute-start.14 = (f32[4,4,8,128]{3,2,1,0:T(8,128)S(1)}, f32[4,4,8,128]{3,2,1,0:T(8,128)S(1)}, u32[]{:S(2)}, u32[]{:S(2)}) collective-permute-start(f32[4,4,8,128]{3,2,1,0:T(8,128)S(1)} %get-tuple-element.72), channel_id=1, source_target_pairs={{0,12},{4,8},{8,4},{12,0},{1,13},{5,9},{9,5},{13,1},{2,14},{6,10},... | collective-permute-start | bytes 196616 | tf_op jit(solution)/shard_map/ppermute | solution.py:64
  94.4 0.0 collective-permute-done.12.refs_1_
  94.4 1.2 %collective-permute-done.13.refs_2_ = f32[4,4,8,128]{3,2,1,0:T(8,128)S(1)} collective-permute-done((f32[4,4,8,128]{3,2,1,0:T(8,128)S(1)}, f32[4,4,8,128]{3,2,1,0:T(8,128)S(1)}, u32[]{:S(2)}, u32[]{:S(2)}) %collective-permute-start.13) | collective-permute-done | bytes 65568 | tf_op jit(solution)/shard_map/ppermute | solution.py:64
  95.7 4.0 %collective-permute-done.14.refs_3_ = f32[4,4,8,128]{3,2,1,0:T(8,128)S(1)} collective-permute-done((f32[4,4,8,128]{3,2,1,0:T(8,128)S(1)}, f32[4,4,8,128]{3,2,1,0:T(8,128)S(1)}, u32[]{:S(2)}, u32[]{:S(2)}) %collective-permute-start.14) | collective-permute-done | bytes 65568 | tf_op jit(solution)/shard_map/ppermute | solution.py:64
  99.7 1.3 %shard_map.151 = f32[8,4,8,128]{3,2,1,0:T(8,128)} custom-call(s32[16]{0:T(128)S(1)} %get-tuple-element.40.rows, f32[4,4,8,128]{3,2,1,0:T(8,128)S(1)} %get-tuple-element.69.refs_0_, f32[4,4,8,128]{3,2,1,0:T(8,128)S(1)} %collective-permute-done.12.refs_1_, f32[4,4,8,128]{3,2,1,0:T(8,128)S(1)} %collective-permute-done.13.refs_2_, ...), custom_call_target="tpu_custom_call" | custom-call | flops 1 | bytes 1 | tf_op jit(solution)/shard_map/pallas_call | solution.py:712
  (5 shorter events, 0.1 us)
Async XLA Ops:
  0.0 6.8 %collective-permute-start = (s32[16]{0:T(128)}, s32[16]{0:T(128)S(1)}, u32[]{:S(2)}, u32[]{:S(2)}) collective-permute-start(s32[16]{0:T(128)} %bitcast.33), channel_id=1, source_target_pairs={{0,4},{4,0},{8,12},{12,8},{1,5},{5,1},{9,13},{13,9},{2,6},{6,2},{1... | collective-permute-start | bytes 200 | tf_op jit(solution)/shard_map/ppermute | solution.py:64
  3.0 42.3 %collective-permute-start.9 = (f32[2,32,32,128]{3,2,1,0:T(8,128)}, f32[2,32,32,128]{3,2,1,0:T(8,128)S(1)}, u32[]{:S(2)}, u32[]{:S(2)}) collective-permute-start(f32[2,32,32,128]{3,2,1,0:T(8,128)} %bitcast.29), channel_id=1, source_target_pairs={{0,2},{2,0},{1,3},{3,1},{4,6},{6,4},{5,7},{7,5},{8,10},{10,8},{9,1... | collective-permute-start | bytes 3145736 | tf_op jit(solution)/shard_map/ppermute | solution.py:74
  7.6 4.4 %collective-permute-start.1 = (s32[32]{0:T(128)S(1)}, s32[32]{0:T(128)S(1)}, u32[]{:S(2)}, u32[]{:S(2)}) collective-permute-start(s32[32]{0:T(128)S(1)} %pad_add_fusion), channel_id=1, source_target_pairs={{0,8},{4,12},{8,0},{12,4},{1,9},{5,13},{9,1},{13,5},{2,10},{6,14},... | collective-permute-start | bytes 392 | tf_op jit(solution)/shard_map/ppermute | solution.py:64
  16.5 10.2 %collective-permute-start.2 = (f32[4,8,8,128]{3,2,1,0:T(8,128)S(1)}, f32[4,8,8,128]{3,2,1,0:T(8,128)S(1)}, u32[]{:S(2)}, u32[]{:S(2)}) collective-permute-start(f32[4,8,8,128]{3,2,1,0:T(8,128)S(1)} %get-tuple-element.47), channel_id=1, source_target_pairs={{0,4},{4,0},{8,12},{12,8},{1,5},{5,1},{9,13},{13,9},{2,6},{6,2},{1... | collective-permute-start | bytes 393224 | tf_op jit(solution)/shard_map/ppermute | solution.py:64
  17.0 12.8 %collective-permute-start.3 = (f32[4,8,8,128]{3,2,1,0:T(8,128)S(1)}, f32[4,8,8,128]{3,2,1,0:T(8,128)S(1)}, u32[]{:S(2)}, u32[]{:S(2)}) collective-permute-start(f32[4,8,8,128]{3,2,1,0:T(8,128)S(1)} %get-tuple-element.48), channel_id=1, source_target_pairs={{0,8},{4,12},{8,0},{12,4},{1,9},{5,13},{9,1},{13,5},{2,10},{6,14},... | collective-permute-start | bytes 393224 | tf_op jit(solution)/shard_map/ppermute | solution.py:64
  19.6 10.2 %collective-permute-start.4 = (f32[4,8,8,128]{3,2,1,0:T(8,128)S(1)}, f32[4,8,8,128]{3,2,1,0:T(8,128)S(1)}, u32[]{:S(2)}, u32[]{:S(2)}) collective-permute-start(f32[4,8,8,128]{3,2,1,0:T(8,128)S(1)} %get-tuple-element.49), channel_id=1, source_target_pairs={{0,12},{4,8},{8,4},{12,0},{1,13},{5,9},{9,5},{13,1},{2,14},{6,10},... | collective-permute-start | bytes 393224 | tf_op jit(solution)/shard_map/ppermute | solution.py:64
  21.0 22.4 %collective-permute-start.6 = (f32[16,2,32,128]{3,2,1,0:T(8,128)}, f32[16,2,32,128]{3,2,1,0:T(8,128)S(1)}, u32[]{:S(2)}, u32[]{:S(2)}) collective-permute-start(f32[16,2,32,128]{3,2,1,0:T(8,128)} %bitcast.26), channel_id=1, source_target_pairs={{0,2},{2,0},{4,6},{6,4},{8,10},{10,8},{12,14},{14,12},{16,18},{18,... | collective-permute-start | bytes 1572872 | tf_op jit(solution)/shard_map/ppermute | solution.py:73
  32.2 12.5 %collective-permute-start.5 = (f32[16,8,8,128]{3,2,1,0:T(8,128)S(1)}, f32[16,8,8,128]{3,2,1,0:T(8,128)S(1)}, u32[]{:S(2)}, u32[]{:S(2)}) collective-permute-start(f32[16,8,8,128]{3,2,1,0:T(8,128)S(1)} %get-tuple-element.51.refs_4_), channel_id=1, source_target_pairs={{0,2},{2,0},{1,3},{3,1},{4,6},{6,4},{5,7},{7,5},{8,10},{10,8},{9,1... | collective-permute-start | bytes 1572872 | tf_op jit(solution)/shard_map/ppermute | solution.py:74
  41.0 5.7 %copy-start = (f32[1,16,2,32,128]{4,3,2,1,0:T(8,128)S(1)}, f32[1,16,2,32,128]{4,3,2,1,0:T(8,128)}, u32[]{:S(2)}) copy-start(f32[1,16,2,32,128]{4,3,2,1,0:T(8,128)} %param.25) | copy-start | bytes 1572868
  41.0 5.7 %copy-start.1 = (bf16[256,256]{1,0:T(8,128)(2,1)S(1)}, bf16[256,256]{1,0:T(8,128)(2,1)}, u32[]{:S(2)}) copy-start(bf16[256,256]{1,0:T(8,128)(2,1)} %constant.53.clone.ymat) | copy-start | bytes 393220
  41.0 5.7 %copy-start.2 = (bf16[256,256]{1,0:T(8,128)(2,1)S(1)}, bf16[256,256]{1,0:T(8,128)(2,1)}, u32[]{:S(2)}) copy-start(bf16[256,256]{1,0:T(8,128)(2,1)} %constant.52.clone.zmat) | copy-start | bytes 393220
  41.0 5.7 %copy-start.3 = (f32[1,1,2,32,32,128]{5,4,3,2,1,0:T(8,128)S(1)}, f32[1,1,2,32,32,128]{5,4,3,2,1,0:T(8,128)}, u32[]{:S(2)}) copy-start(f32[1,1,2,32,32,128]{5,4,3,2,1,0:T(8,128)} %param.24) | copy-start | bytes 3145732
  43.4 2.0 %collective-permute-start.7 = (f32[16,8,8,128]{3,2,1,0:T(8,128)S(1)}, f32[16,8,8,128]{3,2,1,0:T(8,128)S(1)}, u32[]{:S(2)}, u32[]{:S(2)}) collective-permute-start(f32[16,8,8,128]{3,2,1,0:T(8,128)S(1)} %get-tuple-element.51.refs_4_), channel_id=1, source_target_pairs={{0,1},{1,0},{2,3},{3,2},{4,5},{5,4},{6,7},{7,6},{8,9},{9,8},{10,11... | collective-permute-start | bytes 1572872 | tf_op jit(solution)/shard_map/ppermute | solution.py:64
  44.7 1.9 %collective-permute-start.8 = (f32[16,8,8,128]{3,2,1,0:T(8,128)S(1)}, f32[16,8,8,128]{3,2,1,0:T(8,128)S(1)}, u32[]{:S(2)}, u32[]{:S(2)}) collective-permute-start(f32[16,8,8,128]{3,2,1,0:T(8,128)S(1)} %collective-permute-done.5.refs_5_), channel_id=1, source_target_pairs={{0,1},{1,0},{2,3},{3,2},{4,5},{5,4},{6,7},{7,6},{8,9},{9,8},{10,11... | collective-permute-start | bytes 1572872 | tf_op jit(solution)/shard_map/ppermute | solution.py:64
  74.6 6.5 %collective-permute-start.10 = (f32[13,4,4,32,128]{4,3,2,1,0:T(8,128)S(1)}, f32[13,4,4,32,128]{4,3,2,1,0:T(8,128)S(1)}, u32[]{:S(2)}, u32[]{:S(2)}) collective-permute-start(f32[13,4,4,32,128]{4,3,2,1,0:T(8,128)S(1)} %get-tuple-element.59), channel_id=1, source_target_pairs={{0,1},{1,0},{2,3},{3,2},{4,5},{5,4},{6,7},{7,6},{8,9},{9,8},{10,11... | collective-permute-start | bytes 10223624 | tf_op jit(solution)/shard_map/ppermute | solution.py:64
  80.7 2.4 %collective-permute-start.11 = (f32[3,4,4,32,128]{4,3,2,1,0:T(8,128)S(1)}, f32[3,4,4,32,128]{4,3,2,1,0:T(8,128)S(1)}, u32[]{:S(2)}, u32[]{:S(2)}) collective-permute-start(f32[3,4,4,32,128]{4,3,2,1,0:T(8,128)S(1)} %get-tuple-element.68), channel_id=1, source_target_pairs={{0,1},{1,0},{2,3},{3,2},{4,5},{5,4},{6,7},{7,6},{8,9},{9,8},{10,11... | collective-permute-start | bytes 2359304 | tf_op jit(solution)/shard_map/ppermute | solution.py:64
  84.0 10.4 %collective-permute-start.12 = (f32[4,4,8,128]{3,2,1,0:T(8,128)S(1)}, f32[4,4,8,128]{3,2,1,0:T(8,128)S(1)}, u32[]{:S(2)}, u32[]{:S(2)}) collective-permute-start(f32[4,4,8,128]{3,2,1,0:T(8,128)S(1)} %get-tuple-element.70), channel_id=1, source_target_pairs={{0,4},{4,0},{8,12},{12,8},{1,5},{5,1},{9,13},{13,9},{2,6},{6,2},{1... | collective-permute-start | bytes 196616 | tf_op jit(solution)/shard_map/ppermute | solution.py:64
  86.2 9.5 %collective-permute-start.13 = (f32[4,4,8,128]{3,2,1,0:T(8,128)S(1)}, f32[4,4,8,128]{3,2,1,0:T(8,128)S(1)}, u32[]{:S(2)}, u32[]{:S(2)}) collective-permute-start(f32[4,4,8,128]{3,2,1,0:T(8,128)S(1)} %get-tuple-element.71), channel_id=1, source_target_pairs={{0,8},{4,12},{8,0},{12,4},{1,9},{5,13},{9,1},{13,5},{2,10},{6,14},... | collective-permute-start | bytes 196616 | tf_op jit(solution)/shard_map/ppermute | solution.py:64
  93.0 6.6 %collective-permute-start.14 = (f32[4,4,8,128]{3,2,1,0:T(8,128)S(1)}, f32[4,4,8,128]{3,2,1,0:T(8,128)S(1)}, u32[]{:S(2)}, u32[]{:S(2)}) collective-permute-start(f32[4,4,8,128]{3,2,1,0:T(8,128)S(1)} %get-tuple-element.72), channel_id=1, source_target_pairs={{0,12},{4,8},{8,4},{12,0},{1,13},{5,9},{9,5},{13,1},{2,14},{6,10},... | collective-permute-start | bytes 196616 | tf_op jit(solution)/shard_map/ppermute | solution.py:64

commit v7 on v6

--- a/solution.py
+++ b/solution.py
@@ -218,7 +218,7 @@
                 )
             return carry
 
-        lax.fori_loop(0, mine[s].shape[0], fill, 0)
+        lax.fori_loop(0, mine[s].shape[0], fill, 0, unroll=2)
 
     def bend(b, carry):
         w = pl.multiple_of(b * BLOCK, BLOCK)
@@ -244,7 +244,7 @@
                     gz[x, part, :] = scale * z[g * n + at : g * n + at + 8, lanes:]
         return carry
 
-    lax.fori_loop(0, window // BLOCK, bend, 0, unroll=2)
+    lax.fori_loop(0, window // BLOCK, bend, 0, unroll=2 if window // BLOCK % 4 else 4)
 
 
 def steps_kernel(sides, span, pulses_of, meta, zmat, ymat, *refs):
@@ -341,9 +341,6 @@
             return carry
 
         lax.fori_loop(0, window + 2 * REACH, bring, 0, unroll=4)
-    for s in range(count):
-        for copy in in_copies(s):
-            copy.wait()
 
     rim_low = (sublane == 0) & is_source
     rim_high = (sublane == 7) & is_source
@@ -423,9 +420,9 @@
                             ],
                         )
                         value = add(value, mul([square[x, part, :] for x in xs], lap))
-                        drift = mul([gx[x, part, :] for x in xs], dx)
-                        drift = add(drift, mul([gy[x, part, :] for x in xs], y1))
+                        drift = mul([gy[x, part, :] for x in xs], y1)
                         drift = add(drift, mul([gz[x, part, :] for x in xs], z1))
+                        drift = add(drift, mul([gx[x, part, :] for x in xs], dx))
                         value = sub(value, drift)
                         if q == 0:
                             low = [
@@ -470,7 +467,12 @@
             copy.start()
         return buf
 
+    for s in range(count):
+        for copy in in_copies(s)[1:]:
+            copy.wait()
     store_ahead(1 - begin % 2, lo_of(begin) // BLOCK, 0)
+    for s in range(count):
+        in_copies(s)[0].wait()
     lax.fori_loop(begin, end, one_step, 0)
     for k in (end - 2, end - 1):
         for copy in out_copies(k, (k - begin) % 2):

time: 101 us -> 101 us (level)
  Pallas kernels: 41.9 us -> 47.9 us
  starting transfers between devices: 25.7 us -> 19.9 us
    pallas_call x2, Pallas kernels: 33.9 us -> 39.9 us  [run_steps(): call(functools.partial(steps_kernel, sides, span, pulses_of), outs, [smem...]
    ppermute x12, starting transfers between devices: 21.2 us -> 15.4 us  [xor_swap(): return lax.ppermute(block, axis, [(i, i ^ bits) for i in range(size)])]
where the time goes in v7:
time: 101 us
  Pallas kernels  47.9 us (47%)
  starting transfers between devices  19.9 us (20%)
  waiting for transfers between devices  14.7 us (15%)
  matrix products  13 us (13%)
  other arithmetic  3.42 us (3%)
  between operations  1.49 us (1%)
    pallas_call x2, Pallas kernels, run_steps(): call(functools.partial(steps_kernel, sides, span, pulses_of), outs, [smem...  39.9 us
    ppermute x12, starting transfers between devices, xor_swap(): return lax.ppermute(block, axis, [(i, i ^ bits) for i in range(size)])  15.4 us
    ppermute x12, waiting for transfers between devices, xor_swap(): return lax.ppermute(block, axis, [(i, i ^ bits) for i in range(size)])  13.4 us
    dot_general x3, matrix products, product(): jnp.einsum('rp,kpz->krz', rows, spread, preferred_element_type=jnp.float32)  13 us
    pallas_call x1, Pallas kernels, per_device(): call(functools.partial(pack_kernel, owners, columns, tables), [brick] * o...  2.96 us
    ppermute x1, starting transfers between devices, shift(): lax.ppermute(x, ('dom', 'pair'), [(i * pairs, j * pairs) for i, j in moves])  2.45 us
    pallas_call x1, Pallas kernels, per_device(): call(functools.partial(unpack_kernel, owners, columns, tables, stored), [...  2.31 us
    ppermute x2, starting transfers between devices, shift(): return lax.ppermute(x, 'dom', moves)  2.1 us
  transfers between devices with their start and end apart: 15, of which 8 were waited for; matrix products, arithmetic and copies ran while one was open for 17% of the time, Pallas kernels for 12%

profile of v7, /device:TPU:0, one launch (start us, length us, event | category | flops | bytes accessed | tf_op | source)
XLA Modules:
  0.0 101.2 jit_solution(5990082493851786725)
XLA Ops:
  0.0 3.0 %collective-permute-start = (s32[16]{0:T(128)}, s32[16]{0:T(128)S(1)}, u32[]{:S(2)}, u32[]{:S(2)}) collective-permute-start(s32[16]{0:T(128)} %bitcast.33), channel_id=1, source_target_pairs={{0,4},{4,0},{8,12},{12,8},{1,5},{5,1},{9,13},{13,9},{2,6},{6,2},{1... | collective-permute-start | bytes 200 | tf_op jit(solution)/shard_map/ppermute | solution.py:64
  3.0 1.5 %collective-permute-start.9 = (f32[2,32,32,128]{3,2,1,0:T(8,128)}, f32[2,32,32,128]{3,2,1,0:T(8,128)S(1)}, u32[]{:S(2)}, u32[]{:S(2)}) collective-permute-start(f32[2,32,32,128]{3,2,1,0:T(8,128)} %bitcast.29), channel_id=1, source_target_pairs={{0,2},{2,0},{1,3},{3,1},{4,6},{6,4},{5,7},{7,5},{8,10},{10,8},{9,1... | collective-permute-start | bytes 3145736 | tf_op jit(solution)/shard_map/ppermute | solution.py:74
  5.2 1.0 broadcast_select_fusion.table
  6.8 0.0 collective-permute-done
  6.8 0.7 pad_add_fusion
  7.6 2.6 %collective-permute-start.1 = (s32[32]{0:T(128)S(1)}, s32[32]{0:T(128)S(1)}, u32[]{:S(2)}, u32[]{:S(2)}) collective-permute-start(s32[32]{0:T(128)S(1)} %pad_add_fusion), channel_id=1, source_target_pairs={{0,8},{4,12},{8,0},{12,4},{1,9},{5,13},{9,1},{13,5},{2,10},{6,14},... | collective-permute-start | bytes 392 | tf_op jit(solution)/shard_map/ppermute | solution.py:64
  10.1 1.9 %collective-permute-done.1 = s32[32]{0:T(128)S(1)} collective-permute-done((s32[32]{0:T(128)S(1)}, s32[32]{0:T(128)S(1)}, u32[]{:S(2)}, u32[]{:S(2)}) %collective-permute-start.1) | collective-permute-done | bytes 160 | tf_op jit(solution)/shard_map/ppermute | solution.py:64
  12.0 0.8 concatenate.29.info
  12.7 0.7 negate_bitcast_fusion
  13.5 0.1 copy.27
  13.6 3.0 %shard_map.145 = (f32[4,8,8,128]{3,2,1,0:T(8,128)S(1)}, f32[4,8,8,128]{3,2,1,0:T(8,128)S(1)}, f32[4,8,8,128]{3,2,1,0:T(8,128)S(1)}, f32[4,8,8,128]{3,2,1,0:T(8,128)S(1)}, s32[16]{0:T(128)S(1)}) custom-call(s32[132]{0:T(256)S(1)} %concatenate.29.info, f32[8,8,8,128]{3,2,1,0:T(8,128)S(1)} %broadcast_select_fusion.table), custom_call_target="tpu_custom_call" | custom-call | flops 1 | bytes 1 | tf_op jit(solution)/shard_map/pallas_call | solution.py:658
  16.5 0.5 collective-permute-start.2
  17.0 2.6 %collective-permute-start.3 = (f32[4,8,8,128]{3,2,1,0:T(8,128)S(1)}, f32[4,8,8,128]{3,2,1,0:T(8,128)S(1)}, u32[]{:S(2)}, u32[]{:S(2)}) collective-permute-start(f32[4,8,8,128]{3,2,1,0:T(8,128)S(1)} %get-tuple-element.48), channel_id=1, source_target_pairs={{0,8},{4,12},{8,0},{12,4},{1,9},{5,13},{9,1},{13,5},{2,10},{6,14},... | collective-permute-start | bytes 393224 | tf_op jit(solution)/shard_map/ppermute | solution.py:64
  19.6 1.3 %collective-permute-start.4 = (f32[4,8,8,128]{3,2,1,0:T(8,128)S(1)}, f32[4,8,8,128]{3,2,1,0:T(8,128)S(1)}, u32[]{:S(2)}, u32[]{:S(2)}) collective-permute-start(f32[4,8,8,128]{3,2,1,0:T(8,128)S(1)} %get-tuple-element.49), channel_id=1, source_target_pairs={{0,12},{4,8},{8,4},{12,0},{1,13},{5,9},{9,5},{13,1},{2,14},{6,10},... | collective-permute-start | bytes 393224 | tf_op jit(solution)/shard_map/ppermute | solution.py:64
  21.0 2.4 %collective-permute-start.6 = (f32[16,2,32,128]{3,2,1,0:T(8,128)}, f32[16,2,32,128]{3,2,1,0:T(8,128)S(1)}, u32[]{:S(2)}, u32[]{:S(2)}) collective-permute-start(f32[16,2,32,128]{3,2,1,0:T(8,128)} %bitcast.26), channel_id=1, source_target_pairs={{0,2},{2,0},{4,6},{6,4},{8,10},{10,8},{12,14},{14,12},{16,18},{18,... | collective-permute-start | bytes 1572872 | tf_op jit(solution)/shard_map/ppermute | solution.py:73
  23.5 0.8 iota_compare_fusion
  24.4 2.4 %fusion.10.refs_0_ = f32[3,2048,128]{2,1,0:T(8,128)S(1)} fusion(pred[2048,512]{1,0:T(32,128)(4,1)S(1)} %iota_compare_fusion, f32[1024,128]{0,1:T(8,128)S(1)} %add_convert_fusion, f32[16,1024]{1,0:T(8,128)S(1)} %pad_maximum_fusion), kind=kOutput, calls=%fused_computation.13 | convolution fusion | flops 1616904192 | bytes 4784128 | tf_op jit(solution)/shard_map/rp,kpz->krz/dot_general | solution.py:594
  26.8 0.0 collective-permute-done.2.refs_1_
  26.8 3.1 %collective-permute-done.3.refs_2_ = f32[4,8,8,128]{3,2,1,0:T(8,128)S(1)} collective-permute-done((f32[4,8,8,128]{3,2,1,0:T(8,128)S(1)}, f32[4,8,8,128]{3,2,1,0:T(8,128)S(1)}, u32[]{:S(2)}, u32[]{:S(2)}) %collective-permute-start.3) | collective-permute-done | bytes 131104 | tf_op jit(solution)/shard_map/ppermute | solution.py:64
  29.8 0.0 collective-permute-done.4.refs_3_
  29.8 2.3 %shard_map.146 = (f32[16,8,8,128]{3,2,1,0:T(8,128)S(1)}, s32[16]{0:T(128)S(1)}) custom-call(s32[132]{0:T(256)S(1)} %concatenate.29.info, f32[4,8,8,128]{3,2,1,0:T(8,128)S(1)} %get-tuple-element.46.refs_0_, f32[4,8,8,128]{3,2,1,0:T(8,128)S(1)} %collective-permute-done.2.refs_1_, f32[4,8,8,128]{3,2,1,0:T(8,128)S(1)} %collective-permute-done.3.refs_2_, ...), custom_call_target="tpu_custom_call" | custom-call | flops 1 | bytes 1 | tf_op jit(solution)/shard_map/pallas_call | solution.py:668
  32.2 0.6 collective-permute-start.5
  32.8 8.2 %fusion.3.refs_1_ = f32[10,2048,128]{2,1,0:T(8,128)} fusion(pred[2048,512]{1,0:T(32,128)(4,1)S(1)} %iota_compare_fusion, f32[1024,128]{0,1:T(8,128)S(1)} %add_convert_fusion, f32[16,1024]{1,0:T(8,128)S(1)} %pad_maximum_fusion), kind=kOutput, calls=%fused_computation.5 | convolution fusion | flops 5375000576 | bytes 12124160 | tf_op jit(solution)/shard_map/rp,kpz->krz/dot_general | solution.py:594
  41.0 0.0 copy-start
  41.0 0.0 copy-start.1
  41.0 0.0 copy-start.2
  41.0 0.0 copy-start.3
  41.0 2.4 %fusion.11.refs_0_ = f32[3,2048,128]{2,1,0:T(8,128)S(1)} fusion(pred[2048,512]{1,0:T(32,128)(4,1)S(1)} %iota_compare_fusion, f32[1024,128]{0,1:T(8,128)S(1)} %add_convert_fusion, f32[16,1024]{1,0:T(8,128)S(1)} %pad_maximum_fusion), kind=kOutput, calls=%fused_computation.14 | convolution fusion | flops 1616904192 | bytes 4784128 | tf_op jit(solution)/shard_map/rp,kpz->krz/dot_general | solution.py:594
  43.4 0.1 collective-permute-start.7
  43.4 0.0 collective-permute-done.6.refs_3_.refs_2_
  43.5 1.3 %collective-permute-done.5.refs_5_ = f32[16,8,8,128]{3,2,1,0:T(8,128)S(1)} collective-permute-done((f32[16,8,8,128]{3,2,1,0:T(8,128)S(1)}, f32[16,8,8,128]{3,2,1,0:T(8,128)S(1)}, u32[]{:S(2)}, u32[]{:S(2)}) %collective-permute-start.5) | collective-permute-done | bytes 524320 | tf_op jit(solution)/shard_map/ppermute | solution.py:74
  44.7 0.0 collective-permute-start.8
  44.7 0.1 pad_add_fusion.1.meta
  44.8 0.6 collective-permute-done.7.refs_6_
  45.3 0.0 collective-permute-done.9.refs_9_
  45.3 1.3 %collective-permute-done.8.refs_7_ = f32[16,8,8,128]{3,2,1,0:T(8,128)S(1)} collective-permute-done((f32[16,8,8,128]{3,2,1,0:T(8,128)S(1)}, f32[16,8,8,128]{3,2,1,0:T(8,128)S(1)}, u32[]{:S(2)}, u32[]{:S(2)}) %collective-permute-start.8) | collective-permute-done | bytes 524320 | tf_op jit(solution)/shard_map/ppermute | solution.py:64
  46.6 0.0 copy-done
  46.6 0.0 copy-done.1
  46.6 0.0 copy-done.2
  46.6 0.0 copy-done.3
  46.6 33.5 %shard_map.147 = (f32[13,4,4,32,128]{4,3,2,1,0:T(8,128)S(1)}, f32[13,4,4,32,128]{4,3,2,1,0:T(8,128)S(1)}, f32[2,72,32,128]{3,2,1,0:T(8,128)S(1)}, f32[64,32,128]...) custom-call(s32[4]{0:T(128)S(1)} %pad_add_fusion.1.meta, ...), custom_call_target="tpu_custom_call" | custom-call | flops 6979321856 | bytes 1 | tf_op jit(solution)/shard_map/pallas_call | solution.py:553
  80.2 0.2 collective-permute-start.10
  80.4 6.4 %shard_map.149 = (f32[3,4,4,32,128]{4,3,2,1,0:T(8,128)S(1)}, f32[3,4,4,32,128]{4,3,2,1,0:T(8,128)S(1)}) custom-call(s32[4]{0:T(128)S(1)} %pad_add_fusion.1.meta, bf16[256,256]{1,0:T(8,128)(2,1)S(1)} %copy-done.2, bf16[256,256]{1,0:T(8,128)(2,1)S(1)} %copy-done.1, f32[3,2048,128]{2,1,0:T(8,128)S(1)} %fusion.11.refs_0_, f32[16,2,32,128]{3,2,1,0:T(8,128)S(1)} %bitcast.28, ...), custom_call_target="tpu_custom_call" | custom-call | flops 1610612736 | bytes 1 | tf_op jit(solution)/shard_map/pallas_call | solution.py:553
  86.7 0.4 collective-permute-start.11
  87.2 0.0 collective-permute-done.10.got
  87.2 0.5 shard_map.148.before
  87.7 1.4 %collective-permute-done.11.got = f32[3,4,4,32,128]{4,3,2,1,0:T(8,128)S(1)} collective-permute-done((f32[3,4,4,32,128]{4,3,2,1,0:T(8,128)S(1)}, f32[3,4,4,32,128]{4,3,2,1,0:T(8,128)S(1)}, u32[]{:S(2)}, u32[]{:S(2)}) %collective-permute-start.11) | collective-permute-done | bytes 786464 | tf_op jit(solution)/shard_map/ppermute | solution.py:64
  89.1 0.9 shard_map.150
  90.1 0.1 collective-permute-start.12
  90.1 3.2 %collective-permute-start.13 = (f32[4,4,8,128]{3,2,1,0:T(8,128)S(1)}, f32[4,4,8,128]{3,2,1,0:T(8,128)S(1)}, u32[]{:S(2)}, u32[]{:S(2)}) collective-permute-start(f32[4,4,8,128]{3,2,1,0:T(8,128)S(1)} %get-tuple-element.71), channel_id=1, source_target_pairs={{0,8},{4,12},{8,0},{12,4},{1,9},{5,13},{9,1},{13,5},{2,10},{6,14},... | collective-permute-start | bytes 196616 | tf_op jit(solution)/shard_map/ppermute | solution.py:64
  93.3 1.4 %collective-permute-start.14 = (f32[4,4,8,128]{3,2,1,0:T(8,128)S(1)}, f32[4,4,8,128]{3,2,1,0:T(8,128)S(1)}, u32[]{:S(2)}, u32[]{:S(2)}) collective-permute-start(f32[4,4,8,128]{3,2,1,0:T(8,128)S(1)} %get-tuple-element.72), channel_id=1, source_target_pairs={{0,12},{4,8},{8,4},{12,0},{1,13},{5,9},{9,5},{13,1},{2,14},{6,10},... | collective-permute-start | bytes 196616 | tf_op jit(solution)/shard_map/ppermute | solution.py:64
  94.7 0.0 collective-permute-done.12.refs_1_
  94.7 1.2 %collective-permute-done.13.refs_2_ = f32[4,4,8,128]{3,2,1,0:T(8,128)S(1)} collective-permute-done((f32[4,4,8,128]{3,2,1,0:T(8,128)S(1)}, f32[4,4,8,128]{3,2,1,0:T(8,128)S(1)}, u32[]{:S(2)}, u32[]{:S(2)}) %collective-permute-start.13) | collective-permute-done | bytes 65568 | tf_op jit(solution)/shard_map/ppermute | solution.py:64
  95.9 4.0 %collective-permute-done.14.refs_3_ = f32[4,4,8,128]{3,2,1,0:T(8,128)S(1)} collective-permute-done((f32[4,4,8,128]{3,2,1,0:T(8,128)S(1)}, f32[4,4,8,128]{3,2,1,0:T(8,128)S(1)}, u32[]{:S(2)}, u32[]{:S(2)}) %collective-permute-start.14) | collective-permute-done | bytes 65568 | tf_op jit(solution)/shard_map/ppermute | solution.py:64
  99.9 1.3 %shard_map.151 = f32[8,4,8,128]{3,2,1,0:T(8,128)} custom-call(s32[16]{0:T(128)S(1)} %get-tuple-element.40.rows, f32[4,4,8,128]{3,2,1,0:T(8,128)S(1)} %get-tuple-element.69.refs_0_, f32[4,4,8,128]{3,2,1,0:T(8,128)S(1)} %collective-permute-done.12.refs_1_, f32[4,4,8,128]{3,2,1,0:T(8,128)S(1)} %collective-permute-done.13.refs_2_, ...), custom_call_target="tpu_custom_call" | custom-call | flops 1 | bytes 1 | tf_op jit(solution)/shard_map/pallas_call | solution.py:714
  (5 shorter events, 0.1 us)
Async XLA Ops:
  0.0 6.8 %collective-permute-start = (s32[16]{0:T(128)}, s32[16]{0:T(128)S(1)}, u32[]{:S(2)}, u32[]{:S(2)}) collective-permute-start(s32[16]{0:T(128)} %bitcast.33), channel_id=1, source_target_pairs={{0,4},{4,0},{8,12},{12,8},{1,5},{5,1},{9,13},{13,9},{2,6},{6,2},{1... | collective-permute-start | bytes 200 | tf_op jit(solution)/shard_map/ppermute | solution.py:64
  3.0 42.3 %collective-permute-start.9 = (f32[2,32,32,128]{3,2,1,0:T(8,128)}, f32[2,32,32,128]{3,2,1,0:T(8,128)S(1)}, u32[]{:S(2)}, u32[]{:S(2)}) collective-permute-start(f32[2,32,32,128]{3,2,1,0:T(8,128)} %bitcast.29), channel_id=1, source_target_pairs={{0,2},{2,0},{1,3},{3,1},{4,6},{6,4},{5,7},{7,5},{8,10},{10,8},{9,1... | collective-permute-start | bytes 3145736 | tf_op jit(solution)/shard_map/ppermute | solution.py:74
  7.6 4.4 %collective-permute-start.1 = (s32[32]{0:T(128)S(1)}, s32[32]{0:T(128)S(1)}, u32[]{:S(2)}, u32[]{:S(2)}) collective-permute-start(s32[32]{0:T(128)S(1)} %pad_add_fusion), channel_id=1, source_target_pairs={{0,8},{4,12},{8,0},{12,4},{1,9},{5,13},{9,1},{13,5},{2,10},{6,14},... | collective-permute-start | bytes 392 | tf_op jit(solution)/shard_map/ppermute | solution.py:64
  16.5 10.2 %collective-permute-start.2 = (f32[4,8,8,128]{3,2,1,0:T(8,128)S(1)}, f32[4,8,8,128]{3,2,1,0:T(8,128)S(1)}, u32[]{:S(2)}, u32[]{:S(2)}) collective-permute-start(f32[4,8,8,128]{3,2,1,0:T(8,128)S(1)} %get-tuple-element.47), channel_id=1, source_target_pairs={{0,4},{4,0},{8,12},{12,8},{1,5},{5,1},{9,13},{13,9},{2,6},{6,2},{1... | collective-permute-start | bytes 393224 | tf_op jit(solution)/shard_map/ppermute | solution.py:64
  17.0 12.8 %collective-permute-start.3 = (f32[4,8,8,128]{3,2,1,0:T(8,128)S(1)}, f32[4,8,8,128]{3,2,1,0:T(8,128)S(1)}, u32[]{:S(2)}, u32[]{:S(2)}) collective-permute-start(f32[4,8,8,128]{3,2,1,0:T(8,128)S(1)} %get-tuple-element.48), channel_id=1, source_target_pairs={{0,8},{4,12},{8,0},{12,4},{1,9},{5,13},{9,1},{13,5},{2,10},{6,14},... | collective-permute-start | bytes 393224 | tf_op jit(solution)/shard_map/ppermute | solution.py:64
  19.6 10.2 %collective-permute-start.4 = (f32[4,8,8,128]{3,2,1,0:T(8,128)S(1)}, f32[4,8,8,128]{3,2,1,0:T(8,128)S(1)}, u32[]{:S(2)}, u32[]{:S(2)}) collective-permute-start(f32[4,8,8,128]{3,2,1,0:T(8,128)S(1)} %get-tuple-element.49), channel_id=1, source_target_pairs={{0,12},{4,8},{8,4},{12,0},{1,13},{5,9},{9,5},{13,1},{2,14},{6,10},... | collective-permute-start | bytes 393224 | tf_op jit(solution)/shard_map/ppermute | solution.py:64
  21.0 22.4 %collective-permute-start.6 = (f32[16,2,32,128]{3,2,1,0:T(8,128)}, f32[16,2,32,128]{3,2,1,0:T(8,128)S(1)}, u32[]{:S(2)}, u32[]{:S(2)}) collective-permute-start(f32[16,2,32,128]{3,2,1,0:T(8,128)} %bitcast.26), channel_id=1, source_target_pairs={{0,2},{2,0},{4,6},{6,4},{8,10},{10,8},{12,14},{14,12},{16,18},{18,... | collective-permute-start | bytes 1572872 | tf_op jit(solution)/shard_map/ppermute | solution.py:73
  32.2 12.5 %collective-permute-start.5 = (f32[16,8,8,128]{3,2,1,0:T(8,128)S(1)}, f32[16,8,8,128]{3,2,1,0:T(8,128)S(1)}, u32[]{:S(2)}, u32[]{:S(2)}) collective-permute-start(f32[16,8,8,128]{3,2,1,0:T(8,128)S(1)} %get-tuple-element.51.refs_4_), channel_id=1, source_target_pairs={{0,2},{2,0},{1,3},{3,1},{4,6},{6,4},{5,7},{7,5},{8,10},{10,8},{9,1... | collective-permute-start | bytes 1572872 | tf_op jit(solution)/shard_map/ppermute | solution.py:74
  41.0 5.7 %copy-start = (f32[1,16,2,32,128]{4,3,2,1,0:T(8,128)S(1)}, f32[1,16,2,32,128]{4,3,2,1,0:T(8,128)}, u32[]{:S(2)}) copy-start(f32[1,16,2,32,128]{4,3,2,1,0:T(8,128)} %param.25) | copy-start | bytes 1572868
  41.0 5.7 %copy-start.1 = (bf16[256,256]{1,0:T(8,128)(2,1)S(1)}, bf16[256,256]{1,0:T(8,128)(2,1)}, u32[]{:S(2)}) copy-start(bf16[256,256]{1,0:T(8,128)(2,1)} %constant.53.clone.ymat) | copy-start | bytes 393220
  41.0 5.7 %copy-start.2 = (bf16[256,256]{1,0:T(8,128)(2,1)S(1)}, bf16[256,256]{1,0:T(8,128)(2,1)}, u32[]{:S(2)}) copy-start(bf16[256,256]{1,0:T(8,128)(2,1)} %constant.52.clone.zmat) | copy-start | bytes 393220
  41.0 5.7 %copy-start.3 = (f32[1,1,2,32,32,128]{5,4,3,2,1,0:T(8,128)S(1)}, f32[1,1,2,32,32,128]{5,4,3,2,1,0:T(8,128)}, u32[]{:S(2)}) copy-start(f32[1,1,2,32,32,128]{5,4,3,2,1,0:T(8,128)} %param.24) | copy-start | bytes 3145732
  43.4 2.0 %collective-permute-start.7 = (f32[16,8,8,128]{3,2,1,0:T(8,128)S(1)}, f32[16,8,8,128]{3,2,1,0:T(8,128)S(1)}, u32[]{:S(2)}, u32[]{:S(2)}) collective-permute-start(f32[16,8,8,128]{3,2,1,0:T(8,128)S(1)} %get-tuple-element.51.refs_4_), channel_id=1, source_target_pairs={{0,1},{1,0},{2,3},{3,2},{4,5},{5,4},{6,7},{7,6},{8,9},{9,8},{10,11... | collective-permute-start | bytes 1572872 | tf_op jit(solution)/shard_map/ppermute | solution.py:64
  44.7 1.9 %collective-permute-start.8 = (f32[16,8,8,128]{3,2,1,0:T(8,128)S(1)}, f32[16,8,8,128]{3,2,1,0:T(8,128)S(1)}, u32[]{:S(2)}, u32[]{:S(2)}) collective-permute-start(f32[16,8,8,128]{3,2,1,0:T(8,128)S(1)} %collective-permute-done.5.refs_5_), channel_id=1, source_target_pairs={{0,1},{1,0},{2,3},{3,2},{4,5},{5,4},{6,7},{7,6},{8,9},{9,8},{10,11... | collective-permute-start | bytes 1572872 | tf_op jit(solution)/shard_map/ppermute | solution.py:64
  80.2 7.0 %collective-permute-start.10 = (f32[13,4,4,32,128]{4,3,2,1,0:T(8,128)S(1)}, f32[13,4,4,32,128]{4,3,2,1,0:T(8,128)S(1)}, u32[]{:S(2)}, u32[]{:S(2)}) collective-permute-start(f32[13,4,4,32,128]{4,3,2,1,0:T(8,128)S(1)} %get-tuple-element.59), channel_id=1, source_target_pairs={{0,1},{1,0},{2,3},{3,2},{4,5},{5,4},{6,7},{7,6},{8,9},{9,8},{10,11... | collective-permute-start | bytes 10223624 | tf_op jit(solution)/shard_map/ppermute | solution.py:64
  86.7 2.4 %collective-permute-start.11 = (f32[3,4,4,32,128]{4,3,2,1,0:T(8,128)S(1)}, f32[3,4,4,32,128]{4,3,2,1,0:T(8,128)S(1)}, u32[]{:S(2)}, u32[]{:S(2)}) collective-permute-start(f32[3,4,4,32,128]{4,3,2,1,0:T(8,128)S(1)} %get-tuple-element.68), channel_id=1, source_target_pairs={{0,1},{1,0},{2,3},{3,2},{4,5},{5,4},{6,7},{7,6},{8,9},{9,8},{10,11... | collective-permute-start | bytes 2359304 | tf_op jit(solution)/shard_map/ppermute | solution.py:64
  90.1 4.6 %collective-permute-start.12 = (f32[4,4,8,128]{3,2,1,0:T(8,128)S(1)}, f32[4,4,8,128]{3,2,1,0:T(8,128)S(1)}, u32[]{:S(2)}, u32[]{:S(2)}) collective-permute-start(f32[4,4,8,128]{3,2,1,0:T(8,128)S(1)} %get-tuple-element.70), channel_id=1, source_target_pairs={{0,4},{4,0},{8,12},{12,8},{1,5},{5,1},{9,13},{13,9},{2,6},{6,2},{1... | collective-permute-start | bytes 196616 | tf_op jit(solution)/shard_map/ppermute | solution.py:64
  90.1 5.8 %collective-permute-start.13 = (f32[4,4,8,128]{3,2,1,0:T(8,128)S(1)}, f32[4,4,8,128]{3,2,1,0:T(8,128)S(1)}, u32[]{:S(2)}, u32[]{:S(2)}) collective-permute-start(f32[4,4,8,128]{3,2,1,0:T(8,128)S(1)} %get-tuple-element.71), channel_id=1, source_target_pairs={{0,8},{4,12},{8,0},{12,4},{1,9},{5,13},{9,1},{13,5},{2,10},{6,14},... | collective-permute-start | bytes 196616 | tf_op jit(solution)/shard_map/ppermute | solution.py:64
  93.3 6.6 %collective-permute-start.14 = (f32[4,4,8,128]{3,2,1,0:T(8,128)S(1)}, f32[4,4,8,128]{3,2,1,0:T(8,128)S(1)}, u32[]{:S(2)}, u32[]{:S(2)}) collective-permute-start(f32[4,4,8,128]{3,2,1,0:T(8,128)S(1)} %get-tuple-element.72), channel_id=1, source_target_pairs={{0,12},{4,8},{8,4},{12,0},{1,13},{5,9},{9,5},{13,1},{2,14},{6,10},... | collective-permute-start | bytes 196616 | tf_op jit(solution)/shard_map/ppermute | solution.py:64
